TPU v7x, 256 devices: a whole 4x4x8 slice. The times are simulated.
256 devices in a mesh: sub: 64 (over y, z, core), crs: 4 (over x).
Axes of the slice: x: 4, y: 4, z: 8, core: 2. Of those that a mesh axis runs over, the one named last changes fastest.
Arguments:
- loads: float32 [4096, 128, 128], P(('sub', 'crs')), may hold values from -6 to 6
- stiffness: float32 [4096, 6, 128, 128], P(('sub', 'crs'))
- inv_diag: float32 [4096, 128, 128], P(('sub', 'crs'))
- columns: int32 [4096, 6], P(('sub', 'crs')), may hold values from 0 to 17, as said below
- send_lists: int32 [256, 2, 1], P(('sub', 'crs')), may hold values from 0 to 15
- restrict_weights: float32 [4096, 128], P(('sub', 'crs')), may hold values from -4 to 4
- coarse_map: int32 [4096], P(('sub', 'crs')), may hold values from 0 to 2047
- coarse_diag: float32 [16, 128], replicated, may hold values from 0.5 to 2
Outputs:
- solution: float32 [4096, 128, 128], P(('sub', 'crs'))
- residual: float32 [4096, 128, 128], P(('sub', 'crs'))
- precond_residual: float32 [4096, 128, 128], P(('sub', 'crs'))
Inputs may be any that keep to these rules, and one draw needn't show every extreme that they name: `columns`: entry 0 of every block row is the block's own position in its subdomain, i % 16; the other entries index the extended list.
All inputs are finite; a program needn't handle non-finite values.
Results may differ from a plain program's by a relative error of at most 0.0003.
Values sent between devices are 32-bit elements; how exact they have to be, the bound alone decides.
No kernel may reach another device: no remote copies, remote signals or barrier semaphores. Data moves between devices by JAX's collectives and lax.ppermute only.
A program may use at most 64 MiB of HBM per device.

v0:
```python
import jax
import jax.numpy as jnp
from jax import lax
from jax.sharding import PartitionSpec as P

SWEEPS = 4
ITERS = 2


OMEGA = 0.8
HIGH = lax.Precision.HIGHEST


def extended_2(value, sides, width, wrap):
    for axis, dim in sides:
        peers, length = (lax.axis_size(axis), value.shape[dim])
        up = [(i, (i + 1) % peers) for i in range(peers if wrap else peers - 1)]
        down = [(j, i) for i, j in up]
        last = lax.slice_in_dim(value, length - width, length, axis=dim)
        initial = lax.slice_in_dim(value, 0, width, axis=dim)
        before = lax.ppermute(last, axis, up)
        after = lax.ppermute(initial, axis, down)
        value = jnp.concatenate([before, value, after], axis=dim)
    return value


def operator(field, stiffness, columns, send_lists):
    ghost = send_lists.shape[2]
    chosen = send_lists.reshape(-1)
    packed = jnp.take(field, chosen, axis=0)
    padded = extended_2(packed, ((("sub", "crs"), 0),), ghost, True)
    lower = padded[:ghost]
    upper = padded[3 * ghost :]
    extended = jnp.concatenate([field, lower, upper], axis=0)
    picked = jnp.take(extended, columns, axis=0)
    return jnp.einsum(
        "bkij,bkjr->bir", stiffness, picked, precision=HIGH, preferred_element_type=jnp.float32
    )


def side_sum(field):
    cols = jnp.pad(field, ((0, 0), (1, 1), (0, 0)))
    return cols[:, 2:] + cols[:, :-2]


def slab_apply(field, diag_full):
    padded = extended_2(field, (("crs", 0),), 1, False)
    beside = padded[2:] + padded[:-2] + side_sum(field)
    return diag_full * field - beside


def precondition(field, inv_diag, restrict_weights, coarse_map, coarse_diag):
    local = jnp.einsum(
        "bij,bjr->bir", inv_diag, field, precision=HIGH, preferred_element_type=jnp.float32
    )
    reduced = jnp.einsum(
        "bi,bir->br", restrict_weights, field, precision=HIGH, preferred_element_type=jnp.float32
    )
    crows, ccols = coarse_diag.shape
    nrhs = field.shape[2]
    cells = crows * ccols
    onehot = (coarse_map[:, None] == jnp.arange(cells, dtype=jnp.int32)[None, :]).astype(
        jnp.float32
    )
    term = jnp.dot(onehot.T, reduced, precision=HIGH, preferred_element_type=jnp.float32).reshape(
        crows, ccols, nrhs
    )
    slab_rhs = lax.psum_scatter(term, "crs", scatter_dimension=0, tiled=True)
    slab_rhs = lax.psum(slab_rhs, "sub")
    rows_slab = slab_rhs.shape[0]
    start = lax.axis_index("crs") * rows_slab
    slab_diag = lax.dynamic_slice_in_dim(coarse_diag, start, rows_slab, 0)
    diag_full = (4.0 + slab_diag)[:, :, None]
    coarse = jnp.zeros_like(slab_rhs)
    for sweep in range(SWEEPS):
        coarse = coarse + OMEGA * (slab_rhs - slab_apply(coarse, diag_full)) / diag_full
    full_coarse = lax.all_gather(coarse, "crs", axis=0, tiled=True)
    picked = jnp.take(full_coarse.reshape(cells, nrhs), coarse_map, axis=0)
    return local + restrict_weights[:, :, None] * picked[:, None, :]


def precond_product(residual, precond):
    return lax.psum(jnp.sum(residual * precond, axis=(0, 1)), ("sub", "crs"))


def on_device(
    loads, stiffness, inv_diag, columns, send_lists, restrict_weights, coarse_map, coarse_diag
):
    solution = jnp.zeros_like(loads)
    residual = loads
    precond = precondition(residual, inv_diag, restrict_weights, coarse_map, coarse_diag)
    direction = precond
    gamma = precond_product(residual, precond)
    for step in range(ITERS):
        image = operator(direction, stiffness, columns, send_lists)
        curve = lax.psum(jnp.sum(direction * image, axis=(0, 1)), ("sub", "crs"))
        alpha = gamma / curve
        solution = solution + alpha * direction
        residual = residual - alpha * image
        precond = precondition(residual, inv_diag, restrict_weights, coarse_map, coarse_diag)
        gamma_next = precond_product(residual, precond)
        direction = precond + gamma_next / gamma * direction
        gamma = gamma_next
    return (solution, residual, precond)


def solution(mesh):
    placed = (
        P(("sub", "crs"), None, None),
        P(("sub", "crs"), None, None, None),
        P(("sub", "crs"), None, None),
        P(("sub", "crs"), None),
        P(("sub", "crs"), None, None),
        P(("sub", "crs"), None),
        P(("sub", "crs")),
        P(),
    )
    return jax.shard_map(
        on_device,
        mesh=mesh,
        in_specs=placed,
        out_specs=(
            P(("sub", "crs"), None, None),
            P(("sub", "crs"), None, None),
            P(("sub", "crs"), None, None),
        ),
        check_vma=False,
    )
```

profile of v0, /device:TPU:1, one launch (start us, length us, event | category | flops | bytes accessed | tf_op | source)
XLA Modules:
  0.0 1117.0 jit_solution(7240955059122570785)
XLA Ops:
  7.3 2.3 fusion.112
  9.6 2.7 fusion.93
  12.4 3.9 collective-permute-start.1
  17.7 23.3 %reduce-scatter.4.cloned.1.call-done = f32[4,128,128]{2,1,0:T(8,128)} async-done(((f32[16,128,128]{2,1,0:T(8,128)}), f32[4,128,128]{2,1,0:T(8,128)}) %reduce-scatter.4.cloned.1.call-update) | async-done | bytes 262160 | tf_op jit(solution)/shard_map/reduce_scatter | solution.py:68
  41.8 179.6 %all-reduce.17.cloned.1.call-done = f32[4,128,128]{2,1,0:T(8,128)} async-done(((f32[4,128,128]{2,1,0:T(8,128)}), f32[4,128,128]{2,1,0:T(8,128)}) %all-reduce.17.cloned.1.call-update) | async-done | bytes 262160 | tf_op jit(solution)/shard_map/psum | solution.py:69
  223.9 4.0 collective-permute-start.3
  232.2 4.6 collective-permute-start.5
  240.5 4.3 collective-permute-start.7
  249.0 26.4 %all-gather.4.cloned.1.call-done = f32[16,128,128]{2,1,0:T(8,128)} async-done(((f32[4,128,128]{2,1,0:T(8,128)}), f32[16,128,128]{2,1,0:T(8,128)}) %all-gather.4.cloned.1.call-update) | async-done | bytes 1048592 | tf_op jit(solution)/shard_map/all_gather | solution.py:77
  279.3 3.3 collective-permute-start.9
  284.3 3.6 gather_fusion.2
  288.0 13.0 %multiply_reduce_fusion.2 = (f32[128]{0:T(128)S(1)}, f32[128]{0:T(128)S(1)}, f32[16,128,128]{2,1,0:T(8,128)}) fusion(f32[16,128,128]{2,1,0:T(8,128)S(1)} %convolution_add_fusion, f32[16,128,128]{2,1,0:T(8,128)} %param.14, f32[16,6,128,128]{3,2,1,0:T(8,128)} %param.15, f32[16,6,128,128]{3,2,1,0:T(8,128)} %bitcast.57, pred[16,6]{1,0:T(8,128)(4,1)} %copy.23), kind=kOutput, calls=%fused_computation.30 | convolution fusion | flops 2418540288 | bytes 15729760 | tf_op jit(solution)/shard_map/bkij,bkjr->bir/dot_general | solution.py:36
  301.0 83.2 %all-reduce.12 = (f32[128]{0:T(128)S(1)}, f32[128]{0:T(128)S(1)}) all-reduce(f32[128]{0:T(128)S(1)} %get-tuple-element.7, f32[128]{0:T(128)S(1)} %get-tuple-element.6), channel_id=1, replica_groups=mesh['sub'=64,'crs'=4] {'sub','crs'}, use_global_device_ids=true, to_apply=%region_3.5 | all-reduce | flops 256 | bytes 2048 | tf_op jit(solution)/shard_map/psum | solution.py:83
  390.2 20.5 %reduce-scatter.6.cloned.1.call-done = f32[4,128,128]{2,1,0:T(8,128)} async-done(((f32[16,128,128]{2,1,0:T(8,128)}), f32[4,128,128]{2,1,0:T(8,128)}) %reduce-scatter.6.cloned.1.call-update) | async-done | bytes 262160 | tf_op jit(solution)/shard_map/reduce_scatter | solution.py:68
  410.8 180.2 %all-reduce.19.cloned.1.call-done = f32[4,128,128]{2,1,0:T(8,128)} async-done(((f32[4,128,128]{2,1,0:T(8,128)}), f32[4,128,128]{2,1,0:T(8,128)}) %all-reduce.19.cloned.1.call-update) | async-done | bytes 262160 | tf_op jit(solution)/shard_map/psum | solution.py:69
  593.4 4.0 collective-permute-start.11
  601.7 4.6 collective-permute-start.13
  610.0 4.3 collective-permute-start.15
  617.5 27.5 %all-gather.6.cloned.1.call-done = f32[16,128,128]{2,1,0:T(8,128)} async-done(((f32[4,128,128]{2,1,0:T(8,128)}), f32[16,128,128]{2,1,0:T(8,128)}) %all-gather.6.cloned.1.call-update) | async-done | bytes 1048592 | tf_op jit(solution)/shard_map/all_gather | solution.py:77
  647.6 2.2 multiply_reduce_fusion.1
  649.7 76.7 %psum.53 = f32[128]{0:T(128)S(1)} all-reduce(f32[128]{0:T(128)S(1)} %get-tuple-element.39), channel_id=1, replica_groups=mesh['sub'=64,'crs'=4] {'sub','crs'}, use_global_device_ids=true, to_apply=%region_9.13 | all-reduce | flops 128 | bytes 1024 | tf_op jit(solution)/shard_map/psum | solution.py:83
  730.9 12.3 %collective-permute-start.17 = (f32[1,128,128]{2,1,0:T(8,128)S(1)}, f32[1,128,128]{2,1,0:T(8,128)S(1)}, u32[]{:S(2)}, u32[]{:S(2)}) collective-permute-start(f32[1,128,128]{2,1,0:T(8,128)S(1)} %get-tuple-element.33), channel_id=1, source_target_pairs={{1,0},{2,1},{3,2},{4,3},{5,4},{6,5},{7,6},{8,7},{9,8},{10,9},{11,1... | collective-permute-start | bytes 196616 | tf_op jit(solution)/shard_map/ppermute | solution.py:22
  745.9 3.6 gather_fusion.5
  749.5 13.0 %multiply_reduce_fusion = (f32[128]{0:T(128)S(1)}, f32[16,128,128]{2,1,0:T(8,128)}) fusion(f32[16,128,128]{2,1,0:T(8,128)} %copy-done.1, f32[16,6,128,128]{3,2,1,0:T(8,128)} %param.15, f32[16,6,128,128]{3,2,1,0:T(8,128)} %bitcast.56, pred[16,6]{1,0:T(8,128)(4,1)} %copy.23), kind=kOutput, calls=%fused_computation.26 | convolution fusion | flops 2418016256 | bytes 14680672 | tf_op jit(solution)/shard_map/bkij,bkjr->bir/dot_general | solution.py:36
  762.5 82.6 %psum.54 = f32[128]{0:T(128)S(1)} all-reduce(f32[128]{0:T(128)S(1)} %get-tuple-element.41), channel_id=1, replica_groups=mesh['sub'=64,'crs'=4] {'sub','crs'}, use_global_device_ids=true, to_apply=%region_11.15 | all-reduce | flops 128 | bytes 1024 | tf_op jit(solution)/shard_map/psum | solution.py:96
  845.1 2.9 multiply_subtract_fusion
  852.1 19.5 %reduce-scatter.8.cloned.1.call-done = f32[4,128,128]{2,1,0:T(8,128)} async-done(((f32[16,128,128]{2,1,0:T(8,128)}), f32[4,128,128]{2,1,0:T(8,128)}) %reduce-scatter.8.cloned.1.call-update) | async-done | bytes 262160 | tf_op jit(solution)/shard_map/reduce_scatter | solution.py:68
  871.7 180.6 %all-reduce.21.cloned.1.call-done = f32[4,128,128]{2,1,0:T(8,128)} async-done(((f32[4,128,128]{2,1,0:T(8,128)}), f32[4,128,128]{2,1,0:T(8,128)}) %all-reduce.21.cloned.1.call-update) | async-done | bytes 262160 | tf_op jit(solution)/shard_map/psum | solution.py:69
  1054.6 4.0 collective-permute-start.19
  1062.9 4.6 collective-permute-start.21
  1071.2 4.3 collective-permute-start.23
  1078.7 27.5 %all-gather.8.cloned.1.call-done = f32[16,128,128]{2,1,0:T(8,128)} async-done(((f32[4,128,128]{2,1,0:T(8,128)}), f32[16,128,128]{2,1,0:T(8,128)}) %all-gather.8.cloned.1.call-update) | async-done | bytes 1048592 | tf_op jit(solution)/shard_map/all_gather | solution.py:77
  (166 shorter events, 73.3 us)
Async XLA Ops:
  7.2 33.7 %reduce-scatter.4.cloned.1.call-start = ((), (), s32[]{:S(2)}) async-start(), calls=%async_computation.3 | async-start | bytes 1310720 | tf_op jit(solution)/shard_map/reduce_scatter | solution.py:68
  12.3 209.0 %all-reduce.17.cloned.1.call-start = ((), (), s32[]{:S(2)}) async-start(), calls=%async_computation.4 | async-start | bytes 524288 | tf_op jit(solution)/shard_map/psum | solution.py:69
  12.4 29.4 %collective-permute-start.1 = (f32[1,128,128]{2,1,0:T(8,128)S(1)}, f32[1,128,128]{2,1,0:T(8,128)S(1)}, u32[]{:S(2)}, u32[]{:S(2)}) collective-permute-start(f32[1,128,128]{2,1,0:T(8,128)S(1)} %broadcast.83), channel_id=1, source_target_pairs={{0,1},{1,2},{2,3},{4,5},{5,6},{6,7},{8,9},{9,10},{10,11},{12,13},{... | collective-permute-start | bytes 196616 | tf_op jit(solution)/shard_map/ppermute | solution.py:21
  16.4 25.5 %collective-permute-start = (f32[1,128,128]{2,1,0:T(8,128)S(1)}, f32[1,128,128]{2,1,0:T(8,128)S(1)}, u32[]{:S(2)}, u32[]{:S(2)}) collective-permute-start(f32[1,128,128]{2,1,0:T(8,128)S(1)} %broadcast.83), channel_id=1, source_target_pairs={{1,0},{2,1},{3,2},{5,4},{6,5},{7,6},{9,8},{10,9},{11,10},{13,12},{... | collective-permute-start | bytes 196616 | tf_op jit(solution)/shard_map/ppermute | solution.py:22
  41.0 234.5 %all-gather.4.cloned.1.call-start = ((), (), s32[]{:S(2)}) async-start(), calls=%async_computation.5 | async-start | bytes 1310720 | tf_op jit(solution)/shard_map/all_gather | solution.py:77
  222.6 5.4 collective-permute-start.2
  223.9 5.9 collective-permute-start.3
  230.9 6.1 collective-permute-start.4
  232.2 5.9 collective-permute-start.5
  239.2 5.6 collective-permute-start.6
  240.5 5.6 collective-permute-start.7
  247.9 162.8 %reduce-scatter.6.cloned.1.call-start = ((), (), s32[]{:S(2)}) async-start(), calls=%async_computation.6 | async-start | bytes 1310720 | tf_op jit(solution)/shard_map/reduce_scatter | solution.py:68
  279.2 5.0 collective-permute-start.8
  390.2 200.8 %all-reduce.19.cloned.1.call-start = ((), (), s32[]{:S(2)}) async-start(), calls=%async_computation.7 | async-start | bytes 524288 | tf_op jit(solution)/shard_map/psum | solution.py:69
  410.7 234.3 %all-gather.6.cloned.1.call-start = ((), (), s32[]{:S(2)}) async-start(), calls=%async_computation.8 | async-start | bytes 1310720 | tf_op jit(solution)/shard_map/all_gather | solution.py:77
  592.1 5.4 collective-permute-start.10
  593.4 5.9 collective-permute-start.11
  600.4 6.1 collective-permute-start.12
  601.7 5.9 collective-permute-start.13
  608.7 5.6 collective-permute-start.14
  610.0 5.6 collective-permute-start.15
  617.5 254.1 %reduce-scatter.8.cloned.1.call-start = ((), (), s32[]{:S(2)}) async-start(), calls=%async_computation.9 | async-start | bytes 1310720 | tf_op jit(solution)/shard_map/reduce_scatter | solution.py:68
  730.8 12.4 %collective-permute-start.16 = (f32[1,128,128]{2,1,0:T(8,128)S(1)}, f32[1,128,128]{2,1,0:T(8,128)S(1)}, u32[]{:S(2)}, u32[]{:S(2)}) collective-permute-start(f32[1,128,128]{2,1,0:T(8,128)S(1)} %get-tuple-element.32), channel_id=1, source_target_pairs={{0,1},{1,2},{2,3},{3,4},{4,5},{5,6},{6,7},{7,8},{8,9},{9,10},{10,1... | collective-permute-start | bytes 196616 | tf_op jit(solution)/shard_map/ppermute | solution.py:21
  730.9 13.6 %collective-permute-start.17 = (f32[1,128,128]{2,1,0:T(8,128)S(1)}, f32[1,128,128]{2,1,0:T(8,128)S(1)}, u32[]{:S(2)}, u32[]{:S(2)}) collective-permute-start(f32[1,128,128]{2,1,0:T(8,128)S(1)} %get-tuple-element.33), channel_id=1, source_target_pairs={{1,0},{2,1},{3,2},{4,3},{5,4},{6,5},{7,6},{8,7},{9,8},{10,9},{11,1... | collective-permute-start | bytes 196616 | tf_op jit(solution)/shard_map/ppermute | solution.py:22
  852.0 200.2 %all-reduce.21.cloned.1.call-start = ((), (), s32[]{:S(2)}) async-start(), calls=%async_computation.10 | async-start | bytes 524288 | tf_op jit(solution)/shard_map/psum | solution.py:69
  871.6 234.6 %all-gather.8.cloned.1.call-start = ((), (), s32[]{:S(2)}) async-start(), calls=%async_computation.11 | async-start | bytes 1310720 | tf_op jit(solution)/shard_map/all_gather | solution.py:77
  1053.3 5.4 collective-permute-start.18
  1054.6 5.9 collective-permute-start.19
  1061.6 6.1 collective-permute-start.20
  1062.9 5.9 collective-permute-start.21
  1069.9 5.6 collective-permute-start.22
  1071.2 5.6 collective-permute-start.23
  (26 other events, 3243.8 us)
Sparse Core Ops, SparseCore 0:
  12.5 28.4 reduce-scatter.3
  44.8 176.5 all-reduce.16
  248.0 27.3 all-gather.3
  390.3 20.3 reduce-scatter.5
  414.4 176.5 all-reduce.18
  617.6 27.3 all-gather.5
  852.1 19.4 reduce-scatter.7
  875.5 176.7 all-reduce.20
  1078.8 27.3 all-gather.7
where the time goes:
time: 1120 us
  waiting for transfers between devices  702 us (63%)
  blocking collectives  243 us (22%)
  starting transfers between devices  71.6 us (6%)
  matrix products  42.6 us (4%)
  other arithmetic  25.6 us (2%)
  local copies, waits for them, and re-layouts  18.3 us (2%)
  between operations  14.7 us (1%)
    psum x3, waiting for transfers between devices, precondition(): slab_rhs = lax.psum(slab_rhs, 'sub')  540 us
    psum x2, blocking collectives, precond_product(): return lax.psum(jnp.sum(residual * precond, axis=(0, 1)), ('sub', 'crs'))  160 us
    psum x1, blocking collectives, on_device(): curve = lax.psum(jnp.sum(direction * image, axis=(0, 1)), ('sub', 'crs'))  82.6 us
    all_gather x3, waiting for transfers between devices, precondition(): full_coarse = lax.all_gather(coarse, 'crs', axis=0, tiled=True)  81.4 us
    reduce_scatter x3, waiting for transfers between devices, precondition(): slab_rhs = lax.psum_scatter(term, 'crs', scatter_dimension=0, tiled=True)  63.3 us
    ppermute x12, starting transfers between devices, extended_2(): before = lax.ppermute(last, axis, up)  42.7 us
    ppermute x12, starting transfers between devices, extended_2(): after = lax.ppermute(initial, axis, down)  28.5 us
    dot_general x2, matrix products, operator(): jnp.einsum('bkij,bkjr->bir', stiffness, picked, precision=HIGH, preferred...  26 us
  transfers between devices with their start and end apart: 33, of which 26 were waited for; matrix products, arithmetic and copies ran while one was open for 0% of the time, Pallas kernels for 0%

commit v1 on v0

v1 whole, which is shorter than its diff:
```python
import functools

import jax
import jax.numpy as jnp
from jax import lax
from jax.experimental import pallas as pl
from jax.experimental.pallas import tpu as pltpu
from jax.sharding import Mesh, PartitionSpec as P

OMEGA = 0.8
SWEEPS = 4
NB = 16
BLK = 128
KB = 6
EXT = 18
ROWS = 24
CROWS = 16
RING = ("y", "z", "core", "crs")
GATHER = ("y", "z")
SCATTER = ("core", "crs")
F32 = jnp.float32
BF16 = jnp.bfloat16
VMEM = 48 * 1024 * 1024


def sweep_coefficients():
    total = [0.0] * SWEEPS
    power = [1.0]
    for _ in range(SWEEPS):
        for i, c in enumerate(power):
            total[i] += c
        grown = [0.0] * (len(power) + 1)
        for i, c in enumerate(power):
            grown[i] += c * (1.0 - OMEGA)
            grown[i + 1] += c * OMEGA
        power = grown
    return total


def split(x):
    high = x.astype(BF16)
    return high, (x - high.astype(F32)).astype(BF16)


def dot(a, b):
    return jnp.dot(a, b, preferred_element_type=F32)


def dot3(a, b):
    ah, al = split(a)
    bh, bl = split(b)
    return dot(ah, bh) + (dot(ah, bl) + dot(al, bh))


def call(kernel, outs, *, scratch=(), specs=None, flops=0, moved=0):
    return pl.pallas_call(
        kernel,
        out_shape=[jax.ShapeDtypeStruct(s, d) for s, d in outs],
        in_specs=specs,
        scratch_shapes=list(scratch),
        compiler_params=pltpu.CompilerParams(vmem_limit_bytes=VMEM),
        cost_estimate=pl.CostEstimate(flops=flops, bytes_accessed=moved, transcendentals=0),
    )


def restrict_kernel(r_ref, w_ref, cells_ref, msg_ref):
    wt = w_ref[...].T
    rows = [jnp.sum(wt[:, i : i + 1] * r_ref[i], axis=0, keepdims=True) for i in range(NB)]
    rows = jnp.concatenate(rows + [cells_ref[...]], axis=0)
    for a in range(msg_ref.shape[0]):
        msg_ref[a] = rows


def local_kernel(send_ref, f_ref, d_ref, w_ref, info_ref, out_ref, prev_ref, next_ref):
    for i in range(NB):
        out_ref[i] = dot3(d_ref[i], f_ref[i])
    for slot, ref in ((0, prev_ref), (1, next_ref)):
        ref[:BLK] = out_ref[send_ref[0, slot]]
        ref[BLK:] = info_ref[slot]


def sweep_kernel(t_ref, diag_ref, out_ref):
    inv = 1.0 / (4.0 + diag_ref[...])
    coef = sweep_coefficients()
    lane = lax.broadcasted_iota(jnp.int32, (8, BLK), 1)

    def chunk(c, _):
        cell = t_ref[pl.ds(pl.multiple_of(c * 8, 8), 8), :]
        spot = [cell == (lane + BLK * r).astype(F32) for r in range(CROWS)]
        t = [jnp.where(spot[r], coef[-1], 0.0) for r in range(CROWS)]
        for power in range(SWEEPS - 2, -1, -1):
            y = [t[r] * inv[r : r + 1] for r in range(CROWS)]
            new = []
            for r in range(CROWS):
                v = jnp.where(lane == 0, 0.0, pltpu.roll(y[r], 1, 1))
                v = v + jnp.where(lane == BLK - 1, 0.0, pltpu.roll(y[r], BLK - 1, 1))
                if r > 0:
                    v = v + y[r - 1]
                if r < CROWS - 1:
                    v = v + y[r + 1]
                new.append(v + jnp.where(spot[r], coef[power], 0.0))
            t = new
        for r in range(CROWS):
            out_ref[r, pl.ds(pl.multiple_of(c * 8, 8), 8), :] = t[r] * (inv[r : r + 1] * OMEGA)
        return 0

    lax.fori_loop(0, t_ref.shape[0] // 8, chunk, 0)


def coarse_kernel(rows_ref, g_ref, part_ref, wh_ref, wl_ref, sh_ref, sl_ref, oh_ref):
    devs = g_ref.shape[0]
    sources = devs * NB
    targets = rows_ref.shape[1]
    cells = g_ref[:, NB : NB + 1, :].reshape(devs, BLK)
    cells = jnp.sum(cells.reshape(devs // 8, 8, BLK), axis=1)
    sub = lax.broadcasted_iota(jnp.int32, (BLK, BLK), 0)
    for r in range(CROWS):
        here = slice(r * BLK, (r + 1) * BLK)
        high, low = split(rows_ref[r])
        sh_ref[:, here] = high
        sl_ref[:, here] = low
        index = (sub + r * BLK).astype(F32)
        for q in range(devs // 8):
            hit = jnp.where(cells[q : q + 1] == index, 1.0, 0.0)
            oh_ref[here, q * BLK : (q + 1) * BLK] = hit.astype(BF16)
    w = dot(sh_ref[...], oh_ref[...]) + dot(sl_ref[...], oh_ref[...])
    wh, wl = split(w)
    wh_ref[...] = wh
    wl_ref[...] = wl
    gh, gl = split(g_ref[:, :NB, :].reshape(sources, BLK))
    part = dot(wh, gh) + (dot(wh, gl) + dot(wl, gh))
    part_ref[...] = part.reshape(part_ref.shape)


def apply_kernel(wh_ref, wl_ref, g_ref, part_ref):
    devs = g_ref.shape[0]
    gh, gl = split(g_ref[:, :NB, :].reshape(devs * NB, BLK))
    wh = wh_ref[...]
    part = dot(wh, gh) + (dot(wh, gl) + dot(wl_ref[...], gh))
    part = part.reshape(part_ref.shape)
    part_ref[:, :NB, :] = part[:, :NB, :]
    sums = jnp.sum(g_ref[:, NB:, :], axis=0)
    part_ref[:, NB:, :] = part[:, NB:, :] + sums[None]


def operator_kernel(first, cols_ref, s_ref, f_ref, lo_ref, up_ref, *rest):
    if first:
        w_ref, out_ref, q_ref, xh, xl = rest
    else:
        out_ref, xh, xl = rest
    step = pl.program_id(0)
    per = s_ref.shape[0]

    @pl.when(step == 0)
    def _():
        if first:
            wt = w_ref[...].T
            lane = lax.broadcasted_iota(jnp.int32, (BLK, BLK), 1)
            turned = jnp.concatenate(
                [lo_ref[BLK:, :], up_ref[BLK:, :]], axis=0
            ).T
        for e in range(EXT):
            x = f_ref[e] if e < NB else (lo_ref, up_ref)[e - NB][:BLK, :]
            high, low = split(x)
            xh[e, :, :BLK] = high
            xl[e, :, :BLK] = low
            if first:
                col = wt[:, e : e + 1] if e < NB else turned[:, 1 + 8 * (e - NB) : 2 + 8 * (e - NB)]
                high, low = split(jnp.where((lane % 32 == e) & (lane < 96), col, 0.0))
                xh[e, :, BLK:] = high
                xl[e, :, BLK:] = low

    for b in range(per):
        sh, sl, vh, vl = [], [], [], []
        for k in range(KB):
            col = cols_ref[step * per + b, k]
            high, low = split(s_ref[b, k])
            sh.append(high)
            sl.append(low)
            vh.append(xh[col])
            vl.append(xl[col])
        sh = jnp.concatenate(sh, axis=1)
        sl = jnp.concatenate(sl, axis=1)
        vh = jnp.concatenate(vh, axis=0)
        vl = jnp.concatenate(vl, axis=0)
        image = dot(sh, vh) + (dot(sh, vl) + dot(sl, vh))
        out_ref[b] = image[:, :BLK]
        if first:
            q = image[:, BLK:]
            high = q.astype(BF16)
            low = (q - high.astype(F32)).astype(BF16)
            lane = lax.broadcasted_iota(jnp.int32, (BLK, BLK), 1)
            q_ref[b] = jnp.where((lane >= 32) & (lane < 64), low.astype(F32), high.astype(F32)).astype(BF16)


def pack(u):
    keep = lax.broadcasted_iota(jnp.int32, (ROWS, BLK), 0) < EXT
    u = jnp.concatenate([jnp.where(keep, u, 0.0), jnp.zeros((32 - ROWS, BLK), F32)], axis=0)
    high, low = split(u)
    return jnp.concatenate([high, high, low, jnp.zeros((32, BLK), BF16)], axis=0)


def fold(x):
    return jnp.sum(x.reshape(BLK // 8, 8, BLK), axis=0)


def message(msg_ref, rows, dots):
    sums = [jnp.sum(d, axis=0, keepdims=True) for d in dots]
    zero = jnp.zeros((1, BLK), F32)
    tail = [zero] * (EXT - NB) + sums + [zero] * (ROWS - EXT - len(dots))
    block = jnp.concatenate(rows + tail, axis=0)
    for a in range(msg_ref.shape[0]):
        msg_ref[a] = block


def first_kernel(got_ref, r_ref, dr_ref, adr_ref, q_ref, w_ref, msg_ref, u_ref, z_ref, im_ref):
    u = jnp.sum(got_ref[...], axis=0)
    u_ref[...] = u
    packed = pack(u)
    wt = w_ref[...].T
    rows = []
    rz = jnp.zeros((8, BLK), F32)
    zw = jnp.zeros((8, BLK), F32)
    for i in range(NB):
        col = wt[:, i : i + 1]
        image = adr_ref[i] + dot(q_ref[i], packed)
        z = dr_ref[i] + col * u[i : i + 1]
        im_ref[i] = image
        z_ref[i] = z
        rows.append(jnp.sum(col * image, axis=0, keepdims=True))
        rz = rz + fold(r_ref[i] * z)
        zw = zw + fold(z * image)
    message(msg_ref, rows, [rz, zw])


def second_kernel(
    got_ref, u_ref, r_ref, z0_ref, im_ref, dr_ref, dim_ref, adr_ref, adim_ref, q_ref, w_ref,
    msg_ref, v_ref, r1_ref, dr1_ref, z1_ref, az_ref,
):
    v = jnp.sum(got_ref[...], axis=0)
    v_ref[...] = v
    alpha = v[EXT : EXT + 1] / v[EXT + 1 : EXT + 2]
    u = u_ref[...] - alpha * v
    packed = pack(u)
    wt = w_ref[...].T
    rows = []
    rz = jnp.zeros((8, BLK), F32)
    zaz = jnp.zeros((8, BLK), F32)
    cross = jnp.zeros((8, BLK), F32)
    for i in range(NB):
        col = wt[:, i : i + 1]
        image = im_ref[i]
        r1 = r_ref[i] - alpha * image
        dr1 = dr_ref[i] - alpha * dim_ref[i]
        z1 = dr1 + col * u[i : i + 1]
        az = adr_ref[i] - alpha * adim_ref[i] + dot(q_ref[i], packed)
        r1_ref[i] = r1
        dr1_ref[i] = dr1
        z1_ref[i] = z1
        az_ref[i] = az
        rows.append(jnp.sum(col * az, axis=0, keepdims=True))
        rz = rz + fold(r1 * z1)
        zaz = zaz + fold(z1 * az)
        cross = cross + fold(z1 * image + z0_ref[i] * az)
    message(msg_ref, rows, [rz, zaz, cross])


def image_kernel(f_ref, d_ref, out_ref):
    for i in range(NB):
        out_ref[i] = dot3(d_ref[i], f_ref[i])


def last_kernel(
    got_ref, u_ref, v_ref, r1_ref, dr1_ref, z0_ref, z1_ref, im_ref, dim_ref, az_ref, daz_ref, w_ref,
    sol_ref, res_ref, pre_ref,
):
    t = jnp.sum(got_ref[...], axis=0)
    v = v_ref[...]
    gamma0 = v[EXT : EXT + 1]
    curve0 = v[EXT + 1 : EXT + 2]
    gamma1 = t[EXT : EXT + 1]
    alpha0 = gamma0 / curve0
    beta = gamma1 / gamma0
    curve1 = t[EXT + 1 : EXT + 2] + beta * (t[EXT + 2 : EXT + 3] + beta * curve0)
    alpha1 = gamma1 / curve1
    u = u_ref[...] - alpha0 * v - alpha1 * (t + beta * v)
    wt = w_ref[...].T
    for i in range(NB):
        z0 = z0_ref[i]
        p1 = z1_ref[i] + beta * z0
        sol_ref[i] = alpha0 * z0 + alpha1 * p1
        res_ref[i] = r1_ref[i] - alpha1 * (az_ref[i] + beta * im_ref[i])
        local = dr1_ref[i] - alpha1 * (daz_ref[i] + beta * dim_ref[i])
        pre_ref[i] = local + wt[:, i : i + 1] * u[i : i + 1]


FIELD = (NB, BLK, BLK)


def vmem_specs(n):
    return [pl.BlockSpec(memory_space=pltpu.VMEM)] * n


def smem_spec():
    return pl.BlockSpec(memory_space=pltpu.SMEM)


def whole(shape):
    return pl.BlockSpec(shape, lambda i: (0,) * len(shape))


def apply_operator(stiffness, columns, field, lower, upper, weights=None):
    first = weights is not None
    per = 2
    wide = 2 * BLK if first else BLK
    block = pl.BlockSpec((per, BLK, BLK), lambda i: (i, 0, 0))
    outs = [jax.ShapeDtypeStruct(FIELD, F32)]
    args = [columns, stiffness, field, lower, upper]
    specs = [
        smem_spec(),
        pl.BlockSpec((per, KB, BLK, BLK), lambda i: (i, 0, 0, 0)),
        whole(FIELD),
        whole(lower.shape),
        whole(upper.shape),
    ]
    if first:
        outs.append(jax.ShapeDtypeStruct(FIELD, BF16))
        args.append(weights)
        specs.append(whole(weights.shape))
    return pl.pallas_call(
        functools.partial(operator_kernel, first),
        grid=(NB // per,),
        out_shape=outs,
        in_specs=specs,
        out_specs=[block] * len(outs),
        scratch_shapes=[pltpu.VMEM((EXT, BLK, wide), BF16)] * 2,
        compiler_params=pltpu.CompilerParams(vmem_limit_bytes=VMEM),
        cost_estimate=pl.CostEstimate(flops=6 * 10**9, bytes_accessed=8 << 20, transcendentals=0),
    )(*args)


def on_device(
    loads, stiffness, inv_diag, columns, send_lists, restrict_weights, coarse_map, coarse_diag
):
    devices = lax.axis_size(RING)
    gathered = lax.axis_size(GATHER)
    scattered = lax.axis_size(SCATTER)
    up = [(i, (i + 1) % devices) for i in range(devices)]
    down = [(j, i) for i, j in up]
    send = send_lists.reshape(1, 2)
    cells = coarse_map.astype(F32)
    msg_shape = ((gathered, ROWS, BLK), F32)
    part_shape = ((scattered, ROWS, BLK), F32)

    lane = jnp.arange(BLK, dtype=jnp.int32)
    mine = lane // NB == lax.axis_index(GATHER) % 8
    cell_rows = jnp.zeros((ROWS - NB, BLK), F32).at[0].set(jnp.where(mine, jnp.tile(cells, BLK // NB), 0.0))
    info = jnp.stack(
        [
            jnp.broadcast_to(cells[send[0], None], (2, BLK)),
            restrict_weights[send[0]],
        ],
        axis=1,
    )
    info = jnp.pad(info, ((0, 0), (0, 6), (0, 0)))

    (msg,) = call(restrict_kernel, [msg_shape], specs=vmem_specs(3), flops=10**6, moved=2 << 20)(
        loads, restrict_weights, cell_rows
    )
    packet = ((BLK + 8, BLK), F32)
    local, to_prev, to_next = call(
        local_kernel,
        [(FIELD, F32), packet, packet],
        specs=[smem_spec()] + vmem_specs(4),
        flops=2 * 10**8,
        moved=3 << 20,
    )(send, loads, inv_diag, restrict_weights, info)
    lower = lax.ppermute(to_next, RING, up)
    upper = lax.ppermute(to_prev, RING, down)

    target = jnp.concatenate(
        [
            jnp.broadcast_to(cells[:, None], (NB, BLK)),
            lower[BLK : BLK + 1],
            upper[BLK : BLK + 1],
            jnp.full((ROWS - EXT, BLK), -1.0, F32),
        ]
    )
    targets = lax.all_to_all(
        jnp.broadcast_to(target[None], part_shape[0]), SCATTER, 0, 0, tiled=True
    ).reshape(scattered * ROWS, BLK)
    (coarse_rows,) = call(
        sweep_kernel,
        [((CROWS, scattered * ROWS, BLK), F32)],
        specs=vmem_specs(2),
        flops=10**8,
        moved=2 << 20,
    )(targets, coarse_diag)
    got = lax.all_to_all(msg, GATHER, 0, 0, tiled=True)
    image_local, coupling = apply_operator(
        stiffness, columns, local, lower, upper, restrict_weights
    )
    weights_shape = ((scattered * ROWS, gathered * NB), BF16)
    cells_all = CROWS * BLK
    part, wh, wl = call(
        coarse_kernel,
        [part_shape, weights_shape, weights_shape],
        scratch=[
            pltpu.VMEM((scattered * ROWS, cells_all), BF16),
            pltpu.VMEM((scattered * ROWS, cells_all), BF16),
            pltpu.VMEM((cells_all, gathered * NB), BF16),
        ],
        specs=vmem_specs(2),
        flops=10**9,
        moved=2 << 20,
    )(coarse_rows, got)
    got = lax.all_to_all(part, SCATTER, 0, 0, tiled=True)

    msg, u0, z0, image0 = call(
        first_kernel,
        [msg_shape, (part_shape[0][1:], F32), (FIELD, F32), (FIELD, F32)],
        specs=vmem_specs(6),
        flops=10**8,
        moved=6 << 20,
    )(got, loads, local, image_local, coupling, restrict_weights)

    local_image, to_prev, to_next = call(
        local_kernel,
        [(FIELD, F32), packet, packet],
        specs=[smem_spec()] + vmem_specs(4),
        flops=2 * 10**8,
        moved=3 << 20,
    )(send, image0, inv_diag, restrict_weights, info)
    lower = lax.ppermute(to_next, RING, up)
    upper = lax.ppermute(to_prev, RING, down)
    (image_image,) = apply_operator(stiffness, columns, local_image, lower, upper)

    def exchange(msg):
        got = lax.all_to_all(msg, GATHER, 0, 0, tiled=True)
        (part,) = call(
            apply_kernel, [part_shape], specs=vmem_specs(3), flops=10**8, moved=1 << 20
        )(wh, wl, got)
        return lax.all_to_all(part, SCATTER, 0, 0, tiled=True)

    got = exchange(msg)
    msg, v0, residual1, local1, z1, image1 = call(
        second_kernel,
        [msg_shape, (part_shape[0][1:], F32)] + [(FIELD, F32)] * 4,
        specs=vmem_specs(11),
        flops=10**8,
        moved=12 << 20,
    )(
        got, u0, loads, z0, image0, local, local_image, image_local, image_image, coupling,
        restrict_weights,
    )
    (local_image1,) = call(
        image_kernel, [(FIELD, F32)], specs=vmem_specs(2), flops=2 * 10**8, moved=3 << 20
    )(image1, inv_diag)
    got = exchange(msg)
    return tuple(
        call(
            last_kernel, [(FIELD, F32)] * 3, specs=vmem_specs(12), flops=10**8, moved=12 << 20
        )(
            got, u0, v0, residual1, local1, z0, z1, image0, local_image, image1, local_image1,
            restrict_weights,
        )
    )


def solution(mesh):
    chips = mesh.devices.reshape(4, 8, 2, mesh.shape["crs"])
    fine = Mesh(chips, RING)
    placed = P(RING)
    return jax.shard_map(
        on_device,
        mesh=fine,
        in_specs=(placed,) * 7 + (P(),),
        out_specs=(placed,) * 3,
        check_vma=False,
    )
```

time: 1120 us -> 165 us (0.15)
  waiting for transfers between devices: 702 us -> 16 us
  blocking collectives: 243 us -> 16 us
  matrix products: 42.6 us -> 0 us
  Pallas kernels: 0 us -> 40.6 us
  other arithmetic: 25.6 us -> 1.43 us
  starting transfers between devices: 71.6 us -> 52.9 us
  local copies, waits for them, and re-layouts: 18.3 us -> 35.4 us
  between operations: 14.7 us -> 0.94 us
    psum x3 -> x0, waiting for transfers between devices: 540 us -> none  [precondition(): slab_rhs = lax.psum(slab_rhs, 'sub')]
    psum x3 -> x0, blocking collectives: 243 us -> none  [the longest x2 160 us: precond_product(): return lax.psum(jnp.sum(residual * precond, axis=(0, 1)), ('sub', 'crs'))]
    all_gather x3 -> x0, waiting for transfers between devices: 81.4 us -> none  [precondition(): full_coarse = lax.all_gather(coarse, 'crs', axis=0, tiled=True)]
    ppermute x24 -> x4, starting transfers between devices: 71.3 us -> 7.15 us  [the longest x2 3.67 us: on_device(): upper = lax.ppermute(to_prev, RING, down)]
    reduce_scatter x3 -> x0, waiting for transfers between devices: 63.3 us -> none  [precondition(): slab_rhs = lax.psum_scatter(term, 'crs', scatter_dimension=0, tiled=True)]
    all_to_all x0 -> x6, starting transfers between devices: none -> 45.8 us  [the longest x2 15.8 us: exchange(): return lax.all_to_all(part, SCATTER, 0, 0, tiled=True)]
    dot_general x11 -> x0, matrix products: 42.6 us -> none  [the longest x2 26 us: operator(): jnp.einsum('bkij,bkjr->bir', stiffness, picked, precision=HIGH, preferred...]
    pallas_call x0 -> x13, Pallas kernels: none -> 40.6 us  [the longest x2 15.6 us: apply_operator(): pl.pallas_call(functools.partial(operator_kernel, first), grid=(NB // per...]
  transfers between devices with their start and end apart: 33 -> 10, of which waited for: 26 -> 5; matrix products, arithmetic and copies ran while one was open for 0% -> 1% of each run, Pallas kernels for 0% -> 16%
where the time goes in v1:
time: 165 us; the launch traced here: 163 us
  starting transfers between devices  52.9 us (32%)
  Pallas kernels  40.6 us (25%)
  local copies, waits for them, and re-layouts  35.4 us (21%)
  waiting for transfers between devices  16 us (10%)
  blocking collectives  16 us (10%)
    unnamed x97, local copies, waits for them, and re-layouts  32.6 us
    all_to_all x1, blocking collectives, exchange(): got = lax.all_to_all(msg, GATHER, 0, 0, tiled=True)  16 us
    all_to_all x2, starting transfers between devices, exchange(): return lax.all_to_all(part, SCATTER, 0, 0, tiled=True)  15.8 us
    pallas_call x2, Pallas kernels, apply_operator(): pl.pallas_call(functools.partial(operator_kernel, first), grid=(NB // per...  15.6 us
    all_to_all x1, starting transfers between devices, on_device(): lax.all_to_all(jnp.broadcast_to(target[None], part_shape[0]), SCATTER, 0,...  10.9 us
    all_to_all x1, starting transfers between devices, on_device(): got = lax.all_to_all(msg, GATHER, 0, 0, tiled=True)  7.24 us
    all_to_all x1, waiting for transfers between devices, exchange(): got = lax.all_to_all(msg, GATHER, 0, 0, tiled=True)  6.84 us
    pallas_call x1, Pallas kernels, on_device(): call(sweep_kernel, [((CROWS, scattered * ROWS, BLK), F32)], specs=vmem_sp...  6.83 us
  transfers between devices with their start and end apart: 10, of which 5 were waited for; matrix products, arithmetic and copies ran while one was open for 1% of the time, Pallas kernels for 16%

profile of v1, /device:TPU:1, one launch (start us, length us, event | category | flops | bytes accessed | tf_op | source)
XLA Modules:
  0.0 163.3 jit_solution(793175021382601057)
XLA Ops:
  2.6 1.3 gather_fusion.1
  4.0 1.2 copy-done
  5.2 1.2 copy-done.3
  8.9 2.1 %collective-permute-start = (f32[136,128]{1,0:T(8,128)S(1)}, f32[136,128]{1,0:T(8,128)S(1)}, u32[]{:S(2)}, u32[]{:S(2)}) collective-permute-start(f32[136,128]{1,0:T(8,128)S(1)} %get-tuple-element.36), channel_id=1, source_target_pairs={{0,1},{1,2},{2,3},{3,4},{4,5},{5,6},{6,7},{7,8},{8,9},{9,10},{10,1... | collective-permute-start | bytes 208904 | tf_op jit(solution)/shard_map/ppermute | solution.py:378
  11.0 1.9 %collective-permute-start.1 = (f32[136,128]{1,0:T(8,128)S(1)}, f32[136,128]{1,0:T(8,128)S(1)}, u32[]{:S(2)}, u32[]{:S(2)}) collective-permute-start(f32[136,128]{1,0:T(8,128)S(1)} %get-tuple-element.37), channel_id=1, source_target_pairs={{1,0},{2,1},{3,2},{4,3},{5,4},{6,5},{7,6},{8,7},{9,8},{10,9},{11,1... | collective-permute-start | bytes 208904 | tf_op jit(solution)/shard_map/ppermute | solution.py:379
  13.1 1.7 %collective-permute-done.lo_ref = f32[136,128]{1,0:T(8,128)S(1)} collective-permute-done((f32[136,128]{1,0:T(8,128)S(1)}, f32[136,128]{1,0:T(8,128)S(1)}, u32[]{:S(2)}, u32[]{:S(2)}) %collective-permute-start) | collective-permute-done | bytes 69664 | tf_op jit(solution)/shard_map/ppermute | solution.py:378
  15.6 10.9 %all-to-all-start = ((f32[8,24,128]{2,1,0:T(8,128)}), f32[8,24,128]{2,1,0:T(8,128)S(1)}, u32[]{:S(2)}, u32[]{:S(2)}) async-start(f32[8,24,128]{2,1,0:T(8,128)} %broadcast_in_dim.12), calls=%async_computation | async-start | bytes 196608 | tf_op jit(solution)/shard_map/all_to_all | solution.py:389
  28.4 1.2 shard_map.105
  29.7 1.8 %all-to-all-done = f32[8,24,128]{2,1,0:T(8,128)S(1)} async-done(((f32[8,24,128]{2,1,0:T(8,128)}), f32[8,24,128]{2,1,0:T(8,128)S(1)}, u32[]{:S(2)}, u32[]{:S(2)}) %all-to-all-start) | async-done | bytes 98336 | tf_op jit(solution)/shard_map/all_to_all | solution.py:389
  31.5 7.2 %all-to-all-start.1 = ((f32[32,24,128]{2,1,0:T(8,128)}), f32[32,24,128]{2,1,0:T(8,128)S(1)}, u32[]{:S(2)}, u32[]{:S(2)}) async-start(f32[32,24,128]{2,1,0:T(8,128)} %shard_map.105), calls=%async_computation.1 | async-start | bytes 786432 | tf_op jit(solution)/shard_map/all_to_all | solution.py:399
  40.2 6.8 %shard_map.104.rows_ref = f32[16,192,128]{2,1,0:T(8,128)S(1)} custom-call(f32[192,128]{1,0:T(8,128)S(1)} %bitcast.7, f32[16,128]{1,0:T(8,128)S(1)} %copy-done.43), custom_call_target="tpu_custom_call" | custom-call | flops 100000000 | bytes 2097152 | tf_op jit(solution)/shard_map/pallas_call | solution.py:392
  47.0 3.4 %all-to-all-done.1.g_ref = f32[32,24,128]{2,1,0:T(8,128)S(1)} async-done(((f32[32,24,128]{2,1,0:T(8,128)}), f32[32,24,128]{2,1,0:T(8,128)S(1)}, u32[]{:S(2)}, u32[]{:S(2)}) %all-to-all-start.1) | async-done | bytes 393248 | tf_op jit(solution)/shard_map/all_to_all | solution.py:399
  50.5 2.5 %shard_map.106 = (f32[8,24,128]{2,1,0:T(8,128)}, bf16[192,512]{1,0:T(8,128)(2,1)S(1)}, bf16[192,512]{1,0:T(8,128)(2,1)S(1)}) custom-call(f32[16,192,128]{2,1,0:T(8,128)S(1)} %shard_map.104.rows_ref, f32[32,24,128]{2,1,0:T(8,128)S(1)} %all-to-all-done.1.g_ref), custom_call_target="tpu_custom_call" | custom-call | flops 1000000000 | bytes 2097152 | tf_op jit(solution)/shard_map/pallas_call | solution.py:405
  53.6 6.7 %all-to-all-start.2 = ((f32[8,24,128]{2,1,0:T(8,128)}), f32[8,24,128]{2,1,0:T(8,128)S(1)}, u32[]{:S(2)}, u32[]{:S(2)}) async-start(f32[8,24,128]{2,1,0:T(8,128)} %get-tuple-element.40), calls=%async_computation.2 | async-start | bytes 196608 | tf_op jit(solution)/shard_map/all_to_all | solution.py:417
  60.3 8.2 %shard_map.107 = (f32[16,128,128]{2,1,0:T(8,128)S(1)}, bf16[16,128,128]{2,1,0:T(8,128)(2,1)S(1)}) custom-call(s32[16,6]{1,0:T(8,128)S(1)} %copy.13.cols_ref, f32[16,6,128,128]{3,2,1,0:T(8,128)} %s_ref.3, f32[16,128,128]{2,1,0:T(8,128)S(1)} %get-tuple-element.41.f_ref.dr_ref, f32[136,128]{1,0:T(8,128)S(1)} %collective-permute-done.lo_ref, ...), custom_call_target="tpu_custom_call" | custom-call | flops 6000000000 | bytes 8388608 | tf_op jit(solution)/shard_map/pallas_call | solution.py:330
  70.4 1.2 copy-done.8
  72.6 1.9 %shard_map.108 = (f32[32,24,128]{2,1,0:T(8,128)S(1)}, f32[24,128]{1,0:T(8,128)S(1)}, f32[16,128,128]{2,1,0:T(8,128)S(1)}, f32[16,128,128]{2,1,0:T(8,128)S(1)}) custom-call(f32[8,24,128]{2,1,0:T(8,128)S(1)} %all-to-all-done.2.got_ref, f32[16,128,128]{2,1,0:T(8,128)S(1)} %copy-done.2, f32[16,128,128]{2,1,0:T(8,128)S(1)} %copy-done.8, ...), custom_call_target="tpu_custom_call" | custom-call | flops 100000000 | bytes 6291456 | tf_op jit(solution)/shard_map/pallas_call | solution.py:419
  76.9 5.2 %all-to-all-start.3 = ((f32[32,24,128]{2,1,0:T(8,128)}), f32[32,24,128]{2,1,0:T(8,128)S(1)}, u32[]{:S(2)}, u32[]{:S(2)}) async-start(f32[32,24,128]{2,1,0:T(8,128)} %copy-done.35), calls=%async_computation.3 | async-start | bytes 786432 | tf_op jit(solution)/shard_map/all_to_all | solution.py:439
  82.8 1.8 %shard_map.110 = (f32[16,128,128]{2,1,0:T(8,128)S(1)}, f32[136,128]{1,0:T(8,128)}, f32[136,128]{1,0:T(8,128)}) custom-call(s32[1,2]{1,0:T(1,128)S(1)} %bitcast.9, f32[16,128,128]{2,1,0:T(8,128)S(1)} %get-tuple-element.47.f_ref.im_ref, f32[16,128,128]{2,1,0:T(8,128)S(1)} %copy-done.4, f32[16,128]{1,0:T(8,128)S(1)} %copy-done.34, ...), custom_call_target="tpu_custom_call" | custom-call | flops 200000000 | bytes 3145728 | tf_op jit(solution)/shard_map/pallas_call | solution.py:427
  84.6 1.4 collective-permute-start.2
  85.9 1.7 %collective-permute-start.3 = (f32[136,128]{1,0:T(8,128)}, f32[136,128]{1,0:T(8,128)}, u32[]{:S(2)}, u32[]{:S(2)}) collective-permute-start(f32[136,128]{1,0:T(8,128)} %get-tuple-element.50), channel_id=1, source_target_pairs={{1,0},{2,1},{3,2},{4,3},{5,4},{6,5},{7,6},{8,7},{9,8},{10,9},{11,1... | collective-permute-start | bytes 208904 | tf_op jit(solution)/shard_map/ppermute | solution.py:435
  87.7 6.8 %all-to-all-done.3.g_ref = f32[32,24,128]{2,1,0:T(8,128)S(1)} async-done(((f32[32,24,128]{2,1,0:T(8,128)}), f32[32,24,128]{2,1,0:T(8,128)S(1)}, u32[]{:S(2)}, u32[]{:S(2)}) %all-to-all-start.3) | async-done | bytes 393248 | tf_op jit(solution)/shard_map/all_to_all | solution.py:439
  97.3 8.5 %all-to-all-start.4 = ((f32[8,24,128]{2,1,0:T(8,128)}), f32[8,24,128]{2,1,0:T(8,128)}, u32[]{:S(2)}, u32[]{:S(2)}) async-start(f32[8,24,128]{2,1,0:T(8,128)} %copy-done.36), calls=%async_computation.4 | async-start | bytes 196608 | tf_op jit(solution)/shard_map/all_to_all | solution.py:443
  106.5 7.4 %shard_map.111.adim_ref = f32[16,128,128]{2,1,0:T(8,128)S(1)} custom-call(s32[16,6]{1,0:T(8,128)S(1)} %copy-done.45, f32[16,6,128,128]{3,2,1,0:T(8,128)} %s_ref.3, f32[16,128,128]{2,1,0:T(8,128)S(1)} %get-tuple-element.48.f_ref.dim_ref, f32[136,128]{1,0:T(8,128)} %collective-permute-done.2.lo_ref, f32[136,128]{1,0:T(8,128)} %collective-permute-done.3.up_ref), custom_call_target="tpu_custom_call" | custom-call | flops 6000000000 | bytes 8388608 | tf_op jit(solution)/shard_map/pallas_call | solution.py:330
  116.6 4.3 %shard_map.112 = (f32[32,24,128]{2,1,0:T(8,128)S(1)}, f32[24,128]{1,0:T(8,128)S(1)}, f32[16,128,128]{2,1,0:T(8,128)S(1)}, f32[16,128,128]{2,1,0:T(8,128)S(1)}, f...) custom-call(f32[8,24,128]{2,1,0:T(8,128)} %all-to-all-done.4.got_ref, f32[24,128]{1,0:T(8,128)S(1)} %copy-done.39, ...), custom_call_target="tpu_custom_call" | custom-call | flops 100000000 | bytes 12582912 | tf_op jit(solution)/shard_map/pallas_call | solution.py:446
  124.8 16.0 %all_to_all.35.g_ref = f32[32,24,128]{2,1,0:T(8,128)S(1)} all-to-all(f32[32,24,128]{2,1,0:T(8,128)S(1)} %get-tuple-element.51), channel_id=1, replica_groups=mesh['y'=4,'z'=8,'core'=2,'crs'=4] {'y','z'}, dimensions={0} | all-to-all | bytes 786432 | tf_op jit(solution)/shard_map/all_to_all | solution.py:439
  141.8 7.3 %all-to-all-start.6 = ((f32[8,24,128]{2,1,0:T(8,128)}), f32[8,24,128]{2,1,0:T(8,128)S(1)}, u32[]{:S(2)}, u32[]{:S(2)}) async-start(f32[8,24,128]{2,1,0:T(8,128)} %copy-done.37), calls=%async_computation.6 | async-start | bytes 196608 | tf_op jit(solution)/shard_map/all_to_all | solution.py:443
  149.1 1.2 copy-done.14
  151.9 2.2 %all-to-all-done.6.got_ref = f32[8,24,128]{2,1,0:T(8,128)S(1)} async-done(((f32[8,24,128]{2,1,0:T(8,128)}), f32[8,24,128]{2,1,0:T(8,128)S(1)}, u32[]{:S(2)}, u32[]{:S(2)}) %all-to-all-start.6) | async-done | bytes 98336 | tf_op jit(solution)/shard_map/all_to_all | solution.py:443
  154.1 1.2 copy-done.21
  155.3 1.2 copy-done.23
  159.2 4.1 %shard_map.115 = (f32[16,128,128]{2,1,0:T(8,128)}, f32[16,128,128]{2,1,0:T(8,128)}, f32[16,128,128]{2,1,0:T(8,128)}) custom-call(f32[8,24,128]{2,1,0:T(8,128)S(1)} %all-to-all-done.6.got_ref, f32[24,128]{1,0:T(8,128)S(1)} %copy-done.40, f32[24,128]{1,0:T(8,128)S(1)} %copy-done.42, f32[16,128,128]{2,1,0:T(8,128)S(1)} %copy-done.21, ...), custom_call_target="tpu_custom_call" | custom-call | flops 100000000 | bytes 12582912 | tf_op jit(solution)/shard_map/pallas_call | solution.py:461
  (117 shorter events, 30.6 us)
Async XLA Ops:
  0.6 59.7 %copy-start.34 = (f32[16,128]{1,0:T(8,128)S(1)}, f32[16,128]{1,0:T(8,128)}, u32[]{:S(2)}) copy-start(f32[16,128]{1,0:T(8,128)} %w_ref.11) | copy-start | bytes 24580
  3.9 1.2 copy-start
  5.2 1.2 copy-start.3
  8.9 59.7 %copy-start.7 = (f32[16,128,128]{2,1,0:T(8,128)}, f32[16,128,128]{2,1,0:T(8,128)S(1)}, u32[]{:S(2)}) copy-start(f32[16,128,128]{2,1,0:T(8,128)S(1)} %get-tuple-element.41.f_ref.dr_ref) | copy-start | bytes 3145732
  8.9 5.9 %collective-permute-start = (f32[136,128]{1,0:T(8,128)S(1)}, f32[136,128]{1,0:T(8,128)S(1)}, u32[]{:S(2)}, u32[]{:S(2)}) collective-permute-start(f32[136,128]{1,0:T(8,128)S(1)} %get-tuple-element.36), channel_id=1, source_target_pairs={{0,1},{1,2},{2,3},{3,4},{4,5},{5,6},{6,7},{7,8},{8,9},{9,10},{10,1... | collective-permute-start | bytes 208904 | tf_op jit(solution)/shard_map/ppermute | solution.py:378
  11.0 3.8 %collective-permute-start.1 = (f32[136,128]{1,0:T(8,128)S(1)}, f32[136,128]{1,0:T(8,128)S(1)}, u32[]{:S(2)}, u32[]{:S(2)}) collective-permute-start(f32[136,128]{1,0:T(8,128)S(1)} %get-tuple-element.37), channel_id=1, source_target_pairs={{1,0},{2,1},{3,2},{4,3},{5,4},{6,5},{7,6},{8,7},{9,8},{10,9},{11,1... | collective-permute-start | bytes 208904 | tf_op jit(solution)/shard_map/ppermute | solution.py:379
  15.6 15.9 %all-to-all-start = ((f32[8,24,128]{2,1,0:T(8,128)}), f32[8,24,128]{2,1,0:T(8,128)S(1)}, u32[]{:S(2)}, u32[]{:S(2)}) async-start(f32[8,24,128]{2,1,0:T(8,128)} %broadcast_in_dim.12), calls=%async_computation | async-start | bytes 196608 | tf_op jit(solution)/shard_map/all_to_all | solution.py:389
  26.5 1.2 copy-start.1
  31.5 19.0 %all-to-all-start.1 = ((f32[32,24,128]{2,1,0:T(8,128)}), f32[32,24,128]{2,1,0:T(8,128)S(1)}, u32[]{:S(2)}, u32[]{:S(2)}) async-start(f32[32,24,128]{2,1,0:T(8,128)} %shard_map.105), calls=%async_computation.1 | async-start | bytes 786432 | tf_op jit(solution)/shard_map/all_to_all | solution.py:399
  39.5 29.1 %copy-start.44 = (s32[16,6]{1,0:T(8,128)}, s32[16,6]{1,0:T(8,128)S(1)}, u32[]{:S(2)}) copy-start(s32[16,6]{1,0:T(8,128)S(1)} %copy.13.cols_ref) | copy-start | bytes 1156
  53.6 6.7 %copy-start.29 = (bf16[192,512]{1,0:T(8,128)(2,1)}, bf16[192,512]{1,0:T(8,128)(2,1)S(1)}, u32[]{:S(2)}) copy-start(bf16[192,512]{1,0:T(8,128)(2,1)S(1)} %get-tuple-element.39.wl_ref) | copy-start | bytes 589828
  53.6 16.7 %all-to-all-start.2 = ((f32[8,24,128]{2,1,0:T(8,128)}), f32[8,24,128]{2,1,0:T(8,128)S(1)}, u32[]{:S(2)}, u32[]{:S(2)}) async-start(f32[8,24,128]{2,1,0:T(8,128)} %get-tuple-element.40), calls=%async_computation.2 | async-start | bytes 196608 | tf_op jit(solution)/shard_map/all_to_all | solution.py:417
  60.3 10.0 %copy-start.2 = (f32[16,128,128]{2,1,0:T(8,128)S(1)}, f32[16,128,128]{2,1,0:T(8,128)}, u32[]{:S(2)}) copy-start(f32[16,128,128]{2,1,0:T(8,128)} %r_ref.5) | copy-start | bytes 3145732
  60.3 21.8 %copy-start.4 = (f32[16,128,128]{2,1,0:T(8,128)S(1)}, f32[16,128,128]{2,1,0:T(8,128)}, u32[]{:S(2)}) copy-start(f32[16,128,128]{2,1,0:T(8,128)} %d_ref.5) | copy-start | bytes 3145732
  70.4 1.2 copy-start.8
  76.9 37.0 %copy-start.5 = (f32[16,128,128]{2,1,0:T(8,128)}, f32[16,128,128]{2,1,0:T(8,128)S(1)}, u32[]{:S(2)}) copy-start(f32[16,128,128]{2,1,0:T(8,128)S(1)} %get-tuple-element.47.f_ref.im_ref) | copy-start | bytes 3145732
  76.9 17.6 %all-to-all-start.3 = ((f32[32,24,128]{2,1,0:T(8,128)}), f32[32,24,128]{2,1,0:T(8,128)S(1)}, u32[]{:S(2)}, u32[]{:S(2)}) async-start(f32[32,24,128]{2,1,0:T(8,128)} %copy-done.35), calls=%async_computation.3 | async-start | bytes 786432 | tf_op jit(solution)/shard_map/all_to_all | solution.py:439
  84.6 29.3 %copy-start.12 = (f32[16,128,128]{2,1,0:T(8,128)}, f32[16,128,128]{2,1,0:T(8,128)S(1)}, u32[]{:S(2)}) copy-start(f32[16,128,128]{2,1,0:T(8,128)S(1)} %get-tuple-element.48.f_ref.dim_ref) | copy-start | bytes 3145732
  84.6 21.2 %collective-permute-start.2 = (f32[136,128]{1,0:T(8,128)}, f32[136,128]{1,0:T(8,128)}, u32[]{:S(2)}, u32[]{:S(2)}) collective-permute-start(f32[136,128]{1,0:T(8,128)} %get-tuple-element.49), channel_id=1, source_target_pairs={{0,1},{1,2},{2,3},{3,4},{4,5},{5,6},{6,7},{7,8},{8,9},{9,10},{10,1... | collective-permute-start | bytes 208904 | tf_op jit(solution)/shard_map/ppermute | solution.py:434
  85.9 19.8 %collective-permute-start.3 = (f32[136,128]{1,0:T(8,128)}, f32[136,128]{1,0:T(8,128)}, u32[]{:S(2)}, u32[]{:S(2)}) collective-permute-start(f32[136,128]{1,0:T(8,128)} %get-tuple-element.50), channel_id=1, source_target_pairs={{1,0},{2,1},{3,2},{4,3},{5,4},{6,5},{7,6},{8,7},{9,8},{10,9},{11,1... | collective-permute-start | bytes 208904 | tf_op jit(solution)/shard_map/ppermute | solution.py:435
  97.3 17.5 %all-to-all-start.4 = ((f32[8,24,128]{2,1,0:T(8,128)}), f32[8,24,128]{2,1,0:T(8,128)}, u32[]{:S(2)}, u32[]{:S(2)}) async-start(f32[8,24,128]{2,1,0:T(8,128)} %copy-done.36), calls=%async_computation.4 | async-start | bytes 196608 | tf_op jit(solution)/shard_map/all_to_all | solution.py:443
  106.5 34.4 %copy-start.28 = (bf16[192,512]{1,0:T(8,128)(2,1)S(1)}, bf16[192,512]{1,0:T(8,128)(2,1)}, u32[]{:S(2)}) copy-start(bf16[192,512]{1,0:T(8,128)(2,1)} %copy-done.26) | copy-start | bytes 589828
  106.5 34.4 %copy-start.31 = (bf16[192,512]{1,0:T(8,128)(2,1)S(1)}, bf16[192,512]{1,0:T(8,128)(2,1)}, u32[]{:S(2)}) copy-start(bf16[192,512]{1,0:T(8,128)(2,1)} %copy-done.29) | copy-start | bytes 589828
  114.8 1.0 copy-start.18
  116.6 37.5 %copy-start.6 = (f32[16,128,128]{2,1,0:T(8,128)S(1)}, f32[16,128,128]{2,1,0:T(8,128)}, u32[]{:S(2)}) copy-start(f32[16,128,128]{2,1,0:T(8,128)} %copy-done.5) | copy-start | bytes 3145732
  116.6 37.5 %copy-start.11 = (f32[16,128,128]{2,1,0:T(8,128)S(1)}, f32[16,128,128]{2,1,0:T(8,128)}, u32[]{:S(2)}) copy-start(f32[16,128,128]{2,1,0:T(8,128)} %copy-done.10) | copy-start | bytes 3145732
  124.8 16.0 %copy-start.41 = (f32[24,128]{1,0:T(8,128)}, f32[24,128]{1,0:T(8,128)S(1)}, u32[]{:S(2)}) copy-start(f32[24,128]{1,0:T(8,128)S(1)} %get-tuple-element.52.v_ref) | copy-start | bytes 36868
  141.8 12.3 %all-to-all-start.6 = ((f32[8,24,128]{2,1,0:T(8,128)}), f32[8,24,128]{2,1,0:T(8,128)S(1)}, u32[]{:S(2)}, u32[]{:S(2)}) async-start(f32[8,24,128]{2,1,0:T(8,128)} %copy-done.37), calls=%async_computation.6 | async-start | bytes 196608 | tf_op jit(solution)/shard_map/all_to_all | solution.py:443
  149.1 1.2 copy-start.14
  154.1 1.2 copy-start.21
  155.3 1.2 copy-start.23
  156.6 1.2 copy-start.25
  (26 other events, 21.0 us)

commit v2 on v1

v2 whole, which is shorter than its diff:
```python
import functools

import jax
import jax.numpy as jnp
from jax import lax
from jax.experimental import pallas as pl
from jax.experimental.pallas import tpu as pltpu
from jax.sharding import Mesh, PartitionSpec as P

OMEGA = 0.8
SWEEPS = 4
NB = 16
BLK = 128
KB = 6
EXT = 18
ROWS = 24
CROWS = 16
RING = ("y", "z", "core", "crs")
GATHER = ("y", "z")
SCATTER = ("core", "crs")
F32 = jnp.float32
BF16 = jnp.bfloat16
BIG = 60 * 1024 * 1024
SMALL = 12 * 1024 * 1024
TROWS = 32
CHUNK = 4


def sweep_coefficients():
    total = [0.0] * SWEEPS
    power = [1.0]
    for _ in range(SWEEPS):
        for i, c in enumerate(power):
            total[i] += c
        grown = [0.0] * (len(power) + 1)
        for i, c in enumerate(power):
            grown[i] += c * (1.0 - OMEGA)
            grown[i + 1] += c * OMEGA
        power = grown
    return total


def split(x):
    high = x.astype(BF16)
    return high, (x - high.astype(F32)).astype(BF16)


def dot(a, b):
    return jnp.dot(a, b, preferred_element_type=F32)


def dot3(a, b):
    ah, al = split(a)
    bh, bl = split(b)
    return dot(ah, bh) + (dot(ah, bl) + dot(al, bh))


def staged(body, ins, outs, scratch=(), flops=0, moved=0, limit=BIG):
    kinds_in = [k for _, k in ins]
    kinds_out = [k for _, _, k in outs]
    n_in, n_out = len(ins), len(outs)
    parts = NB // CHUNK

    def buffer(shape, dtype, kind):
        return pltpu.SMEM(shape, dtype) if kind == "scalar" else pltpu.VMEM(shape, dtype)

    buffers = [buffer(a.shape, a.dtype, k) for a, k in ins if k not in ("vmem", "hbm")]
    buffers += [buffer(sh, dt, k) for sh, dt, k in outs if k != "vmem"]

    def kernel(*refs):
        sources, targets = refs[:n_in], refs[n_in : n_in + n_out]
        rest = list(refs[n_in + n_out :])
        sem_in, sem_out = rest.pop(), rest.pop()
        bufs_in = [r if k in ("vmem", "hbm") else rest.pop(0) for r, k in zip(sources, kinds_in)]
        bufs_out = [r if k == "vmem" else rest.pop(0) for r, k in zip(targets, kinds_out)]

        def chunk(ref, c):
            return ref.at[pl.ds(c * CHUNK, CHUNK)]

        first = [
            pltpu.make_async_copy(s, b, sem_in.at[j, 0])
            for j, (s, b, k) in enumerate(zip(sources, bufs_in, kinds_in))
            if k in ("whole", "scalar")
        ]
        fields = [
            [
                pltpu.make_async_copy(chunk(s, c), chunk(b, c), sem_in.at[j, c])
                for j, (s, b, k) in enumerate(zip(sources, bufs_in, kinds_in))
                if k == "field"
            ]
            for c in range(parts)
        ]
        for copy in first + sum(fields, []):
            copy.start()
        sent = []

        def ready(c):
            for copy in fields[c]:
                copy.wait()

        def emit(n, c=0):
            if kinds_out[n] == "field":
                copy = pltpu.make_async_copy(chunk(bufs_out[n], c), chunk(targets[n], c), sem_out.at[n, c])
            else:
                copy = pltpu.make_async_copy(bufs_out[n], targets[n], sem_out.at[n, 0])
            copy.start()
            sent.append(copy)

        for copy in first:
            copy.wait()
        body(ready, emit, *bufs_in, *bufs_out, *rest)
        for copy in sent:
            copy.wait()

    def spec(kind):
        return pl.BlockSpec(memory_space=pltpu.VMEM if kind == "vmem" else pltpu.HBM)

    return pl.pallas_call(
        kernel,
        out_shape=[jax.ShapeDtypeStruct(sh, dt) for sh, dt, _ in outs],
        in_specs=[spec(k) for k in kinds_in],
        out_specs=[spec(k) for k in kinds_out],
        scratch_shapes=buffers
        + list(scratch)
        + [pltpu.SemaphoreType.DMA((n_out, parts)), pltpu.SemaphoreType.DMA((n_in, parts))],
        compiler_params=pltpu.CompilerParams(vmem_limit_bytes=limit),
        cost_estimate=pl.CostEstimate(flops=flops, bytes_accessed=moved, transcendentals=0),
    )(*[a for a, _ in ins])


def column_cells(map_ref):
    rows = [jnp.full((1, BLK), map_ref[i], jnp.int32) for i in range(NB)]
    return jnp.concatenate(rows, axis=0).astype(F32)


def broadcast(msg_ref, rows):
    for a in range(msg_ref.shape[0]):
        msg_ref[a] = rows


def chunks():
    return [(c, range(c * CHUNK, (c + 1) * CHUNK)) for c in range(NB // CHUNK)]


def start_body(ready, emit, map_ref, w_ref, r_ref, rows_ref):
    wt = w_ref[...].T
    lane = lax.broadcasted_iota(jnp.int32, (1, BLK), 1)
    cells = jnp.zeros((1, BLK), jnp.int32)
    for i in range(NB):
        cells = jnp.where(lane % NB == i, map_ref[i], cells)
    mine = lane // NB == lax.axis_index(GATHER) % 8
    cells = jnp.where(mine, cells, 0).astype(F32)
    rows = []
    for c, blocks in chunks():
        ready(c)
        rows += [jnp.sum(wt[:, i : i + 1] * r_ref[i], axis=0, keepdims=True) for i in blocks]
    rows_ref[...] = jnp.concatenate(rows + [cells, jnp.zeros((ROWS - NB - 1, BLK), F32)], axis=0)


def group_ghosts(t_ref):
    return jnp.sum(t_ref[:, NB:, :], axis=0)


def open_body(ready, emit, rows_ref, t_ref, msg_ref):
    ghosts = group_ghosts(t_ref)
    rows = jnp.concatenate(
        [rows_ref[: NB + 1], ghosts[:1], ghosts[NB - 1 :], rows_ref[NB + 3 :]], axis=0
    )
    broadcast(msg_ref, rows)
    emit(0)


def local_body(ready, emit, send_ref, w_ref, r_ref, d_ref, out_ref, prev_ref, next_ref):
    for c, blocks in chunks():
        ready(c)
        for i in blocks:
            out_ref[i] = dot3(d_ref[i], r_ref[i])
        emit(0, c)
    for slot, ref in ((0, prev_ref), (1, next_ref)):
        block = send_ref[0, slot]
        ref[:BLK] = out_ref[block]
        ref[BLK:] = jnp.concatenate(
            [w_ref[pl.ds(block, 1), :], jnp.zeros((7, BLK), F32)], axis=0
        )


def target_body(ready, emit, send_ref, map_ref, out_ref):
    slots = 2 * out_ref.shape[0]
    place = lax.axis_index(SCATTER)
    row = lax.broadcasted_iota(jnp.int32, (slots, BLK), 0)
    to_next = jnp.full((slots, BLK), map_ref[send_ref[0, 1]], jnp.int32)
    to_prev = jnp.full((slots, BLK), map_ref[send_ref[0, 0]], jnp.int32)
    ghosts = jnp.where(row == (2 * place + 2) % slots, to_next, 0)
    ghosts = jnp.where(row == (2 * place + slots - 1) % slots, to_prev, ghosts).astype(F32)
    own = column_cells(map_ref)
    for a in range(out_ref.shape[0]):
        out_ref[a, :NB] = own
        out_ref[a, NB:] = ghosts
    emit(0)


def image_body(ready, emit, send_ref, f_ref, d_ref, out_ref, prev_ref, next_ref):
    for c, blocks in chunks():
        ready(c)
        for i in blocks:
            out_ref[i] = dot3(d_ref[i], f_ref[i])
        emit(0, c)
    for slot, ref in ((0, prev_ref), (1, next_ref)):
        ref[...] = out_ref[send_ref[0, slot]]


def product_body(ready, emit, f_ref, d_ref, out_ref):
    for c, blocks in chunks():
        ready(c)
        for i in blocks:
            out_ref[i] = dot3(d_ref[i], f_ref[i])
        emit(0, c)


def solve_rows(cell, inv, use):
    coef = sweep_coefficients()
    lane = lax.broadcasted_iota(jnp.int32, (8, BLK), 1)
    spot = [jnp.where(cell == (lane + BLK * r).astype(F32), 1.0, 0.0) for r in range(CROWS)]
    t = [coef[-1] * spot[r] for r in range(CROWS)]
    for power in range(SWEEPS - 2, -1, -1):
        y = [t[r] * inv[r : r + 1] for r in range(CROWS)]
        new = []
        for r in range(CROWS):
            v = jnp.where(lane == 0, 0.0, pltpu.roll(y[r], 1, 1))
            v = v + jnp.where(lane == BLK - 1, 0.0, pltpu.roll(y[r], BLK - 1, 1))
            if r > 0:
                v = v + y[r - 1]
            if r < CROWS - 1:
                v = v + y[r + 1]
            new.append(v + coef[power] * spot[r])
        t = new
    for r in range(CROWS):
        use(r, t[r] * (inv[r : r + 1] * OMEGA))


def sweep_body(ready, emit, t_ref, diag_ref, out_ref, cell_ref):
    inv = 1.0 / (4.0 + diag_ref[...])
    devs = t_ref.shape[0]
    for g in range(devs):
        cell_ref[g * NB : (g + 1) * NB] = t_ref[g, :NB]
    slots = 2 * devs
    row = lax.broadcasted_iota(jnp.int32, (slots, BLK), 0)
    inner = (row > 0) & (row < slots - 1)
    cell_ref[devs * NB :] = jnp.where(inner, group_ghosts(t_ref), -1.0)

    def chunk(c, _):
        here = pl.ds(pl.multiple_of(c * 8, 8), 8)

        def use(r, value):
            out_ref[r, here, :] = value

        solve_rows(cell_ref[here, :], inv, use)
        return 0

    lax.fori_loop(0, cell_ref.shape[0] // 8, chunk, 0)
    emit(0)


def spread(part, sums, part_ref):
    devs = part_ref.shape[0]
    part_ref[:, :NB, :] = part[: devs * NB].reshape(devs, NB, BLK)
    for g in range(devs):
        ghosts = part[devs * NB + 2 * g : devs * NB + 2 * g + 2]
        part_ref[g, NB:, :] = jnp.concatenate([ghosts, sums[EXT - NB :]], axis=0)


def coarse_body(
    ready, emit, rows_hbm, diag_ref, g_ref, part_ref, wh_ref, wl_ref, rows_ref, sh_ref, sl_ref, oh_ref, sem
):
    copy = pltpu.make_async_copy(rows_hbm, rows_ref, sem)
    copy.start()
    devs = g_ref.shape[0]
    sources = devs * NB
    cells = g_ref[:, NB : NB + 1, :].reshape(devs, BLK)
    cells = jnp.sum(cells.reshape(devs // 8, 8, BLK), axis=1)
    sub = lax.broadcasted_iota(jnp.int32, (BLK, BLK), 0)
    for r in range(CROWS):
        index = (sub + r * BLK).astype(F32)
        for q in range(devs // 8):
            hit = jnp.where(cells[q : q + 1] == index, 1.0, 0.0)
            oh_ref[r * BLK : (r + 1) * BLK, q * BLK : (q + 1) * BLK] = hit.astype(BF16)
    place = lax.axis_index(GATHER)
    before = g_ref[(place + devs - 1) % devs][NB + 1 : NB + 2]
    after = g_ref[(place + 1) % devs][NB + 2 : NB + 3]
    row = lax.broadcasted_iota(jnp.int32, (8, BLK), 0)
    outer = jnp.where(row == 0, before, jnp.where(row == 7, after, -1.0))
    copy.wait()
    size = rows_ref.shape[1]
    base = size - NB

    def use(r, value):
        rows_ref[r, base : base + 8, :] += jnp.where(row == 0, value, 0.0)
        rows_ref[r, size - 8 :, :] += jnp.where(row == 7, value, 0.0)

    solve_rows(outer, 1.0 / (4.0 + diag_ref[...]), use)
    for r in range(CROWS):
        here = slice(r * BLK, (r + 1) * BLK)
        high, low = split(rows_ref[r])
        sh_ref[:, here] = high
        sl_ref[:, here] = low
    w = dot(sh_ref[...], oh_ref[...]) + dot(sl_ref[...], oh_ref[...])
    wh, wl = split(w)
    wh_ref[...] = wh
    wl_ref[...] = wl
    emit(1)
    emit(2)
    gh, gl = split(g_ref[:, :NB, :].reshape(sources, BLK))
    part = dot(wh, gh) + (dot(wh, gl) + dot(wl, gh))
    spread(part, jnp.zeros((ROWS - NB, BLK), F32), part_ref)
    emit(0)


def apply_body(ready, emit, wh_ref, wl_ref, g_ref, part_ref):
    devs = g_ref.shape[0]
    gh, gl = split(g_ref[:, :NB, :].reshape(devs * NB, BLK))
    wh = wh_ref[...]
    part = dot(wh, gh) + (dot(wh, gl) + dot(wl_ref[...], gh))
    spread(part, jnp.sum(g_ref[:, NB:, :], axis=0), part_ref)
    emit(0)


def operator_kernel(first, cols_ref, s_ref, f_ref, lo_ref, up_ref, *rest):
    if first:
        w_ref, out_ref, q_ref, xh, xl = rest
    else:
        out_ref, xh, xl = rest
    step = pl.program_id(0)
    per = s_ref.shape[0]

    @pl.when(step == 0)
    def _():
        if first:
            wt = w_ref[...].T
            lane = lax.broadcasted_iota(jnp.int32, (BLK, BLK), 1)
            turned = jnp.concatenate(
                [lo_ref[BLK:, :], up_ref[BLK:, :]], axis=0
            ).T
        for e in range(EXT):
            x = f_ref[e] if e < NB else (lo_ref, up_ref)[e - NB][:BLK, :]
            high, low = split(x)
            xh[e, :, :BLK] = high
            xl[e, :, :BLK] = low
            if first:
                col = wt[:, e : e + 1] if e < NB else turned[:, 8 * (e - NB) : 1 + 8 * (e - NB)]
                high, low = split(jnp.where((lane % 32 == e) & (lane < 96), col, 0.0))
                xh[e, :, BLK:] = high
                xl[e, :, BLK:] = low

    for b in range(per):
        sh, sl, vh, vl = [], [], [], []
        for k in range(KB):
            col = cols_ref[k, step * per + b]
            high, low = split(s_ref[b, k])
            sh.append(high)
            sl.append(low)
            vh.append(xh[col])
            vl.append(xl[col])
        sh = jnp.concatenate(sh, axis=1)
        sl = jnp.concatenate(sl, axis=1)
        vh = jnp.concatenate(vh, axis=0)
        vl = jnp.concatenate(vl, axis=0)
        image = dot(sh, vh) + (dot(sh, vl) + dot(sl, vh))
        out_ref[b] = image[:, :BLK]
        if first:
            q = image[:, BLK:]
            high = q.astype(BF16)
            low = (q - high.astype(F32)).astype(BF16)
            lane = lax.broadcasted_iota(jnp.int32, (BLK, BLK), 1)
            q_ref[b] = jnp.where((lane >= 32) & (lane < 64), low.astype(F32), high.astype(F32)).astype(BF16)


def pack(u):
    keep = lax.broadcasted_iota(jnp.int32, (ROWS, BLK), 0) < EXT
    u = jnp.concatenate([jnp.where(keep, u, 0.0), jnp.zeros((32 - ROWS, BLK), F32)], axis=0)
    high, low = split(u)
    return jnp.concatenate([high, high, low, jnp.zeros((32, BLK), BF16)], axis=0)


def fold(x):
    return jnp.sum(x.reshape(BLK // 8, 8, BLK), axis=0)


def message(rows, dots):
    sums = [jnp.sum(d, axis=0, keepdims=True) for d in dots]
    zero = jnp.zeros((1, BLK), F32)
    end = [zero] * (EXT - NB) + sums + [zero] * (ROWS - EXT - len(dots))
    return jnp.concatenate(rows + end, axis=0)


def first_body(ready, emit, got_ref, w_ref, r_ref, dr_ref, adr_ref, q_ref, msg_ref, u_ref, im_ref):
    u = jnp.sum(got_ref[...], axis=0)
    u_ref[...] = u
    emit(1)
    packed = pack(u)
    wt = w_ref[...].T
    rows = []
    rz = jnp.zeros((8, BLK), F32)
    zw = jnp.zeros((8, BLK), F32)
    for c, blocks in chunks():
        ready(c)
        for i in blocks:
            col = wt[:, i : i + 1]
            image = adr_ref[i] + dot(q_ref[i], packed)
            z = dr_ref[i] + col * u[i : i + 1]
            im_ref[i] = image
            rows.append(jnp.sum(col * image, axis=0, keepdims=True))
            rz = rz + fold(r_ref[i] * z)
            zw = zw + fold(z * image)
        emit(2, c)
    broadcast(msg_ref, message(rows, [rz, zw]))
    emit(0)


def second_body(
    ready, emit, got_ref, u_ref, w_ref, r_ref, im_ref, dr_ref, dim_ref, adr_ref, adim_ref, q_ref,
    msg_ref, v_ref, az_ref,
):
    v = jnp.sum(got_ref[...], axis=0)
    v_ref[...] = v
    emit(1)
    alpha = v[EXT : EXT + 1] / v[EXT + 1 : EXT + 2]
    u0 = u_ref[...]
    u = u0 - alpha * v
    packed = pack(u)
    wt = w_ref[...].T
    rows = []
    rz = jnp.zeros((8, BLK), F32)
    zaz = jnp.zeros((8, BLK), F32)
    cross = jnp.zeros((8, BLK), F32)
    for c, blocks in chunks():
        ready(c)
        for i in blocks:
            col = wt[:, i : i + 1]
            image = im_ref[i]
            dr = dr_ref[i]
            z0 = dr + col * u0[i : i + 1]
            z1 = dr - alpha * dim_ref[i] + col * u[i : i + 1]
            az = adr_ref[i] - alpha * adim_ref[i] + dot(q_ref[i], packed)
            az_ref[i] = az
            rows.append(jnp.sum(col * az, axis=0, keepdims=True))
            rz = rz + fold((r_ref[i] - alpha * image) * z1)
            zaz = zaz + fold(z1 * az)
            cross = cross + fold(z1 * image + z0 * az)
        emit(2, c)
    broadcast(msg_ref, message(rows, [rz, zaz, cross]))
    emit(0)


def last_body(
    ready, emit, got_ref, u_ref, v_ref, w_ref, r_ref, im_ref, dr_ref, dim_ref, az_ref, daz_ref,
    sol_ref, res_ref, pre_ref,
):
    t = jnp.sum(got_ref[...], axis=0)
    v = v_ref[...]
    gamma0 = v[EXT : EXT + 1]
    curve0 = v[EXT + 1 : EXT + 2]
    gamma1 = t[EXT : EXT + 1]
    alpha0 = gamma0 / curve0
    beta = gamma1 / gamma0
    curve1 = t[EXT + 1 : EXT + 2] + beta * (t[EXT + 2 : EXT + 3] + beta * curve0)
    alpha1 = gamma1 / curve1
    u0 = u_ref[...]
    u1 = u0 - alpha0 * v
    u2 = u1 - alpha1 * (t + beta * v)
    wt = w_ref[...].T
    for c, blocks in chunks():
        ready(c)
        for i in blocks:
            col = wt[:, i : i + 1]
            image = im_ref[i]
            dr = dr_ref[i]
            dim = dim_ref[i]
            z0 = dr + col * u0[i : i + 1]
            dr1 = dr - alpha0 * dim
            z1 = dr1 + col * u1[i : i + 1]
            sol_ref[i] = alpha0 * z0 + alpha1 * (z1 + beta * z0)
            res_ref[i] = r_ref[i] - alpha0 * image - alpha1 * (az_ref[i] + beta * image)
            local = dr1 - alpha1 * (daz_ref[i] + beta * dim)
            pre_ref[i] = local + col * u2[i : i + 1]
        for n in range(3):
            emit(n, c)


FIELD = (NB, BLK, BLK)


def block_of(shape):
    return pl.BlockSpec(shape, lambda i: (0,) * len(shape))


def apply_operator(stiffness, columns, field, lower, upper, weights=None):
    first = weights is not None
    per = 4
    wide = 2 * BLK if first else BLK
    block = pl.BlockSpec((per, BLK, BLK), lambda i: (i, 0, 0))
    outs = [jax.ShapeDtypeStruct(FIELD, F32)]
    args = [columns, stiffness, field, lower, upper]
    specs = [
        pl.BlockSpec(memory_space=pltpu.SMEM),
        pl.BlockSpec((per, KB, BLK, BLK), lambda i: (i, 0, 0, 0)),
        block_of(FIELD),
        block_of(lower.shape),
        block_of(upper.shape),
    ]
    if first:
        outs.append(jax.ShapeDtypeStruct(FIELD, BF16))
        args.append(weights)
        specs.append(block_of(weights.shape))
    return pl.pallas_call(
        functools.partial(operator_kernel, first),
        grid=(NB // per,),
        out_shape=outs,
        in_specs=specs,
        out_specs=[block] * len(outs),
        scratch_shapes=[pltpu.VMEM((EXT, BLK, wide), BF16)] * 2,
        compiler_params=pltpu.CompilerParams(vmem_limit_bytes=BIG),
        cost_estimate=pl.CostEstimate(flops=6 * 10**9, bytes_accessed=8 << 20, transcendentals=0),
    )(*args)


def on_device(
    loads, stiffness, inv_diag, columns, send_lists, restrict_weights, coarse_map, coarse_diag
):
    devices = lax.axis_size(RING)
    gathered = lax.axis_size(GATHER)
    scattered = lax.axis_size(SCATTER)
    up = [(i, (i + 1) % devices) for i in range(devices)]
    down = [(j, i) for i, j in up]
    send = (send_lists.reshape(1, 2), "scalar")
    cells = (coarse_map, "scalar")
    columns = columns.T
    weights = (restrict_weights, "whole")
    msg_out = ((gathered, ROWS, BLK), F32, "whole")
    part_shape = (scattered, ROWS, BLK)
    part_out = (part_shape, F32, "whole")
    short_out = (part_shape[1:], F32, "whole")
    field_out = (FIELD, F32, "field")
    big = 2 << 20

    (target,) = staged(
        target_body,
        [send, cells],
        [((scattered, TROWS, BLK), F32, "whole")],
        moved=1 << 18,
        limit=SMALL,
    )
    targets = lax.all_to_all(target, SCATTER, 0, 0, tiled=True)
    (start_rows,) = staged(
        start_body,
        [cells, weights, (loads, "field")],
        [((ROWS, BLK), F32, "vmem")],
        flops=10**6,
        moved=big,
    )
    (msg,) = staged(
        open_body, [(start_rows, "vmem"), (targets, "vmem")], [msg_out], moved=1 << 18, limit=SMALL
    )
    got = lax.all_to_all(msg, GATHER, 0, 0, tiled=True)
    packet = ((BLK + 8, BLK), F32, "vmem")
    local, to_prev, to_next = staged(
        local_body,
        [send, weights, (loads, "field"), (inv_diag, "field")],
        [field_out, packet, packet],
        flops=2 * 10**8,
        moved=big,
    )
    lower = lax.ppermute(to_next, RING, up)
    upper = lax.ppermute(to_prev, RING, down)
    rows = scattered * EXT
    (coarse_rows,) = staged(
        sweep_body,
        [(targets, "vmem"), (coarse_diag, "whole")],
        [((CROWS, rows, BLK), F32, "whole")],
        scratch=[pltpu.VMEM((rows, BLK), F32)],
        flops=10**8,
        moved=big,
        limit=SMALL,
    )
    image_local, coupling = apply_operator(
        stiffness, columns, local, lower, upper, restrict_weights
    )
    weights_out = ((rows, gathered * NB), BF16, "whole")
    cells_all = CROWS * BLK
    part, wh, wl = staged(
        coarse_body,
        [(coarse_rows, "hbm"), (coarse_diag, "whole"), (got, "vmem")],
        [part_out, weights_out, weights_out],
        scratch=[
            pltpu.VMEM((CROWS, rows, BLK), F32),
            pltpu.VMEM((rows, cells_all), BF16),
            pltpu.VMEM((rows, cells_all), BF16),
            pltpu.VMEM((cells_all, gathered * NB), BF16),
            pltpu.SemaphoreType.DMA(()),
        ],
        flops=10**9,
        moved=big,
        limit=SMALL,
    )
    got = lax.all_to_all(part, SCATTER, 0, 0, tiled=True)

    msg, u0, image0 = staged(
        first_body,
        [(got, "vmem"), weights, (loads, "field"), (local, "field"), (image_local, "field"),
         (coupling, "field")],
        [msg_out, short_out, field_out],
        flops=10**8,
        moved=big,
    )
    packet = ((BLK, BLK), F32, "vmem")
    local_image, to_prev, to_next = staged(
        image_body,
        [send, (image0, "field"), (inv_diag, "field")],
        [field_out, packet, packet],
        flops=2 * 10**8,
        moved=big,
    )
    lower = lax.ppermute(to_next, RING, up)
    upper = lax.ppermute(to_prev, RING, down)
    (image_image,) = apply_operator(stiffness, columns, local_image, lower, upper)

    def exchange(msg):
        got = lax.all_to_all(msg, GATHER, 0, 0, tiled=True)
        (part,) = staged(
            apply_body,
            [(wh, "whole"), (wl, "whole"), (got, "vmem")],
            [part_out],
            flops=10**8,
            moved=big,
            limit=SMALL,
        )
        return lax.all_to_all(part, SCATTER, 0, 0, tiled=True)

    got = exchange(msg)
    msg, v0, image1 = staged(
        second_body,
        [(got, "vmem"), (u0, "whole"), weights, (loads, "field"), (image0, "field"),
         (local, "field"), (local_image, "field"), (image_local, "field"),
         (image_image, "field"), (coupling, "field")],
        [msg_out, short_out, field_out],
        flops=10**8,
        moved=big,
    )
    (local_image1,) = staged(
        product_body,
        [(image1, "field"), (inv_diag, "field")],
        [field_out],
        flops=2 * 10**8,
        moved=big,
    )
    got = exchange(msg)
    return tuple(
        staged(
            last_body,
            [(got, "vmem"), (u0, "whole"), (v0, "whole"), weights, (loads, "field"),
             (image0, "field"), (local, "field"), (local_image, "field"), (image1, "field"),
             (local_image1, "field")],
            [field_out] * 3,
            flops=10**8,
            moved=big,
        )
    )


def solution(mesh):
    chips = mesh.devices.reshape(4, 8, 2, mesh.shape["crs"])
    fine = Mesh(chips, RING)
    placed = P(RING)
    return jax.shard_map(
        on_device,
        mesh=fine,
        in_specs=(placed,) * 7 + (P(),),
        out_specs=(placed,) * 3,
        check_vma=False,
    )
```

time: 165 us -> 146 us (0.88)
  local copies, waits for them, and re-layouts: 35.4 us -> 6.56 us
  Pallas kernels: 40.6 us -> 55.8 us
  waiting for transfers between devices: 16 us -> 10.3 us
  starting transfers between devices: 52.9 us -> 54.8 us
    unnamed x97 -> x24, local copies, waits for them, and re-layouts: 32.6 us -> 6.56 us
    pallas_call x11 -> x13, Pallas kernels: 25 us -> 42 us  [staged(): pl.pallas_call(kernel, out_shape=[jax.ShapeDtypeStruct(sh, dt) for sh, dt...]
    all_to_all x1, starting transfers between devices: 10.9 us -> 6.55 us  [on_device(): targets = lax.all_to_all(target, SCATTER, 0, 0, tiled=True)]
    all_to_all x1, waiting for transfers between devices: 3.44 us -> 0.01 us  [on_device(): got = lax.all_to_all(msg, GATHER, 0, 0, tiled=True)]
    all_to_all x1, starting transfers between devices: 7.24 us -> 10.5 us  [on_device(): got = lax.all_to_all(msg, GATHER, 0, 0, tiled=True)]
    all_to_all x1, starting transfers between devices: 5.22 us -> 7.41 us  [exchange(): got = lax.all_to_all(msg, GATHER, 0, 0, tiled=True)]
    gather x2 -> x0, local copies, waits for them, and re-layouts: 1.89 us -> none  [the longest x1 1.25 us: on_device(): restrict_weights[send[0]]]
    pallas_call x2, Pallas kernels: 15.6 us -> 13.8 us  [apply_operator(): pl.pallas_call(functools.partial(operator_kernel, first), grid=(NB // per...]
  transfers between devices with their start and end apart: 10 -> 10, of which waited for: 5 -> 3; matrix products, arithmetic and copies ran while one was open for 1% -> 0% of each run, Pallas kernels for 16% -> 25%
where the time goes in v2:
time: 146 us; the launch traced here: 145 us
  Pallas kernels  55.8 us (38%)
  starting transfers between devices  54.8 us (38%)
  blocking collectives  16.3 us (11%)
  waiting for transfers between devices  10.3 us (7%)
  local copies, waits for them, and re-layouts  6.56 us (4%)
    pallas_call x13, Pallas kernels, staged(): pl.pallas_call(kernel, out_shape=[jax.ShapeDtypeStruct(sh, dt) for sh, dt...  42 us
    all_to_all x1, blocking collectives, exchange(): got = lax.all_to_all(msg, GATHER, 0, 0, tiled=True)  16.3 us
    all_to_all x2, starting transfers between devices, exchange(): return lax.all_to_all(part, SCATTER, 0, 0, tiled=True)  15.8 us
    pallas_call x2, Pallas kernels, apply_operator(): pl.pallas_call(functools.partial(operator_kernel, first), grid=(NB // per...  13.8 us
    all_to_all x1, starting transfers between devices, on_device(): got = lax.all_to_all(msg, GATHER, 0, 0, tiled=True)  10.5 us
    all_to_all x1, starting transfers between devices, on_device(): got = lax.all_to_all(part, SCATTER, 0, 0, tiled=True)  8.19 us
    all_to_all x1, starting transfers between devices, exchange(): got = lax.all_to_all(msg, GATHER, 0, 0, tiled=True)  7.41 us
    unnamed x24, local copies, waits for them, and re-layouts  6.56 us
  transfers between devices with their start and end apart: 10, of which 3 were waited for; matrix products, arithmetic and copies ran while one was open for 0% of the time, Pallas kernels for 25%

profile of v2, /device:TPU:1, one launch (start us, length us, event | category | flops | bytes accessed | tf_op | source)
XLA Modules:
  0.0 144.8 jit_solution(15175500552401344841)
XLA Ops:
  1.9 1.3 shard_map.103
  3.3 6.5 %all-to-all-start = ((f32[8,32,128]{2,1,0:T(8,128)}), f32[8,32,128]{2,1,0:T(8,128)S(1)}, u32[]{:S(2)}, u32[]{:S(2)}) async-start(f32[8,32,128]{2,1,0:T(8,128)} %shard_map.103), calls=%async_computation | async-start | bytes 262144 | tf_op jit(solution)/shard_map/all_to_all | solution.py:552
  9.8 2.3 %shard_map.105.refs_0_ = f32[24,128]{1,0:T(8,128)} custom-call(s32[16]{0:T(128)} %refs_0_.1, f32[16,128]{1,0:T(8,128)} %refs_3_.5, f32[16,128,128]{2,1,0:T(8,128)} %refs_4_.1), custom_call_target="tpu_custom_call" | custom-call | flops 1000000 | bytes 2097152 | tf_op jit(solution)/shard_map/pallas_call | solution.py:118
  12.1 2.9 %all-to-all-done.refs_0_.refs_1_ = f32[8,32,128]{2,1,0:T(8,128)S(1)} async-done(((f32[8,32,128]{2,1,0:T(8,128)}), f32[8,32,128]{2,1,0:T(8,128)S(1)}, u32[]{:S(2)}, u32[]{:S(2)}) %all-to-all-start) | async-done | bytes 131104 | tf_op jit(solution)/shard_map/all_to_all | solution.py:552
  15.0 0.7 copy-done
  15.7 0.9 shard_map.106
  16.6 10.5 %all-to-all-start.1 = ((f32[32,24,128]{2,1,0:T(8,128)}), f32[32,24,128]{2,1,0:T(8,128)S(1)}, u32[]{:S(2)}, u32[]{:S(2)}) async-start(f32[32,24,128]{2,1,0:T(8,128)} %shard_map.106), calls=%async_computation.1 | async-start | bytes 786432 | tf_op jit(solution)/shard_map/all_to_all | solution.py:563
  27.1 3.7 %shard_map.108 = (f32[16,128,128]{2,1,0:T(8,128)}, f32[136,128]{1,0:T(8,128)}, f32[136,128]{1,0:T(8,128)}) custom-call(s32[1,2]{1,0:T(1,128)} %bitcast.2, f32[16,128]{1,0:T(8,128)} %refs_3_.5, f32[16,128,128]{2,1,0:T(8,128)} %refs_4_.1, f32[16,128,128]{2,1,0:T(8,128)} %refs_1_.13), custom_call_target="tpu_custom_call" | custom-call | flops 200000000 | bytes 2097152 | tf_op jit(solution)/shard_map/pallas_call | solution.py:118
  30.8 0.8 collective-permute-start
  31.6 2.3 %collective-permute-start.1 = (f32[136,128]{1,0:T(8,128)}, f32[136,128]{1,0:T(8,128)S(1)}, u32[]{:S(2)}, u32[]{:S(2)}) collective-permute-start(f32[136,128]{1,0:T(8,128)} %get-tuple-element.25), channel_id=1, source_target_pairs={{1,0},{2,1},{3,2},{4,3},{5,4},{6,5},{7,6},{8,7},{9,8},{10,9},{11,1... | collective-permute-start | bytes 208904 | tf_op jit(solution)/shard_map/ppermute | solution.py:573
  33.8 0.7 copy-done.1
  34.5 5.5 %shard_map.104.refs_0_ = f32[16,144,128]{2,1,0:T(8,128)S(1)} custom-call(f32[8,32,128]{2,1,0:T(8,128)S(1)} %all-to-all-done.refs_0_.refs_1_, f32[16,128]{1,0:T(8,128)S(1)} %copy-done.1), custom_call_target="tpu_custom_call" | custom-call | flops 100000000 | bytes 2097152 | tf_op jit(solution)/shard_map/pallas_call | solution.py:118
  40.1 0.7 copy-done.2
  40.8 3.4 %shard_map.107 = (f32[8,24,128]{2,1,0:T(8,128)}, bf16[144,512]{1,0:T(8,128)(2,1)S(1)}, bf16[144,512]{1,0:T(8,128)(2,1)S(1)}) custom-call(f32[16,144,128]{2,1,0:T(8,128)S(1)} %shard_map.104.refs_0_, f32[16,128]{1,0:T(8,128)S(1)} %copy-done.2, f32[32,24,128]{2,1,0:T(8,128)S(1)} %all-to-all-done.1.refs_2_), custom_call_target="tpu_custom_call" | custom-call | flops 1000000000 | bytes 2097152 | tf_op jit(solution)/shard_map/pallas_call | solution.py:118
  44.2 8.2 %all-to-all-start.2 = ((f32[8,24,128]{2,1,0:T(8,128)}), f32[8,24,128]{2,1,0:T(8,128)S(1)}, u32[]{:S(2)}, u32[]{:S(2)}) async-start(f32[8,24,128]{2,1,0:T(8,128)} %get-tuple-element.22), calls=%async_computation.2 | async-start | bytes 196608 | tf_op jit(solution)/shard_map/all_to_all | solution.py:604
  53.1 7.3 %shard_map.109 = (f32[16,128,128]{2,1,0:T(8,128)}, bf16[16,128,128]{2,1,0:T(8,128)(2,1)}) custom-call(s32[6,16]{1,0:T(8,128)} %bitcast.5, f32[16,6,128,128]{3,2,1,0:T(8,128)} %s_ref.3, f32[16,128,128]{2,1,0:T(8,128)} %get-tuple-element.23.f_ref.refs_3_.refs_5_.refs_6_, f32[136,128]{1,0:T(8,128)} %copy-done.8, f32[136,128]{1,0:T(8,128)} %copy-done.9, ...), custom_call_target="tpu_custom_call" | custom-call | flops 6000000000 | bytes 8388608 | tf_op jit(solution)/shard_map/pallas_call | solution.py:514
  61.0 4.2 %shard_map.110 = (f32[32,24,128]{2,1,0:T(8,128)}, f32[24,128]{1,0:T(8,128)}, f32[16,128,128]{2,1,0:T(8,128)}) custom-call(f32[8,24,128]{2,1,0:T(8,128)} %copy-done.5, f32[16,128]{1,0:T(8,128)} %refs_3_.5, f32[16,128,128]{2,1,0:T(8,128)} %refs_4_.1, f32[16,128,128]{2,1,0:T(8,128)} %get-tuple-element.23.f_ref.refs_3_.refs_5_.refs_6_, ...), custom_call_target="tpu_custom_call" | custom-call | flops 100000000 | bytes 2097152 | tf_op jit(solution)/shard_map/pallas_call | solution.py:118
  65.2 7.4 %all-to-all-start.3 = ((f32[32,24,128]{2,1,0:T(8,128)}), f32[32,24,128]{2,1,0:T(8,128)S(1)}, u32[]{:S(2)}, u32[]{:S(2)}) async-start(f32[32,24,128]{2,1,0:T(8,128)} %get-tuple-element.28), calls=%async_computation.3 | async-start | bytes 786432 | tf_op jit(solution)/shard_map/all_to_all | solution.py:627
  72.6 3.6 %shard_map.112 = (f32[16,128,128]{2,1,0:T(8,128)}, f32[128,128]{1,0:T(8,128)}, f32[128,128]{1,0:T(8,128)}) custom-call(s32[1,2]{1,0:T(1,128)} %bitcast.3, f32[16,128,128]{2,1,0:T(8,128)} %get-tuple-element.30.refs_1_.refs_4_.refs_5_, f32[16,128,128]{2,1,0:T(8,128)} %refs_1_.13), custom_call_target="tpu_custom_call" | custom-call | flops 200000000 | bytes 2097152 | tf_op jit(solution)/shard_map/pallas_call | solution.py:118
  76.3 1.5 %collective-permute-start.2 = (f32[128,128]{1,0:T(8,128)}, f32[128,128]{1,0:T(8,128)S(1)}, u32[]{:S(2)}, u32[]{:S(2)}) collective-permute-start(f32[128,128]{1,0:T(8,128)} %get-tuple-element.32), channel_id=1, source_target_pairs={{0,1},{1,2},{2,3},{3,4},{4,5},{5,6},{6,7},{7,8},{8,9},{9,10},{10,1... | collective-permute-start | bytes 196616 | tf_op jit(solution)/shard_map/ppermute | solution.py:622
  77.7 1.8 %collective-permute-start.3 = (f32[128,128]{1,0:T(8,128)}, f32[128,128]{1,0:T(8,128)S(1)}, u32[]{:S(2)}, u32[]{:S(2)}) collective-permute-start(f32[128,128]{1,0:T(8,128)} %get-tuple-element.33), channel_id=1, source_target_pairs={{1,0},{2,1},{3,2},{4,3},{5,4},{6,5},{7,6},{8,7},{9,8},{10,9},{11,1... | collective-permute-start | bytes 196616 | tf_op jit(solution)/shard_map/ppermute | solution.py:623
  79.5 5.3 %all-to-all-done.3.refs_2_ = f32[32,24,128]{2,1,0:T(8,128)S(1)} async-done(((f32[32,24,128]{2,1,0:T(8,128)}), f32[32,24,128]{2,1,0:T(8,128)S(1)}, u32[]{:S(2)}, u32[]{:S(2)}) %all-to-all-start.3) | async-done | bytes 393248 | tf_op jit(solution)/shard_map/all_to_all | solution.py:627
  84.9 1.4 shard_map.111
  86.3 8.5 %all-to-all-start.4 = ((f32[8,24,128]{2,1,0:T(8,128)}), f32[8,24,128]{2,1,0:T(8,128)S(1)}, u32[]{:S(2)}, u32[]{:S(2)}) async-start(f32[8,24,128]{2,1,0:T(8,128)} %shard_map.111), calls=%async_computation.4 | async-start | bytes 196608 | tf_op jit(solution)/shard_map/all_to_all | solution.py:636
  95.5 6.6 %shard_map.113.refs_8_ = f32[16,128,128]{2,1,0:T(8,128)} custom-call(s32[6,16]{1,0:T(8,128)} %bitcast.6, f32[16,6,128,128]{3,2,1,0:T(8,128)} %s_ref.3, f32[16,128,128]{2,1,0:T(8,128)} %get-tuple-element.31.f_ref.refs_6_.refs_7_, f32[128,128]{1,0:T(8,128)} %copy-done.10, f32[128,128]{1,0:T(8,128)} %copy-done.11), custom_call_target="tpu_custom_call" | custom-call | flops 6000000000 | bytes 8388608 | tf_op jit(solution)/shard_map/pallas_call | solution.py:514
  102.7 5.5 %shard_map.114 = (f32[32,24,128]{2,1,0:T(8,128)}, f32[24,128]{1,0:T(8,128)}, f32[16,128,128]{2,1,0:T(8,128)}) custom-call(f32[8,24,128]{2,1,0:T(8,128)} %copy-done.6, f32[24,128]{1,0:T(8,128)} %get-tuple-element.29.refs_1_, f32[16,128]{1,0:T(8,128)} %refs_3_.5, f32[16,128,128]{2,1,0:T(8,128)} %refs_4_.1, ...), custom_call_target="tpu_custom_call" | custom-call | flops 100000000 | bytes 2097152 | tf_op jit(solution)/shard_map/pallas_call | solution.py:118
  108.2 16.3 %all_to_all.35.refs_2_ = f32[32,24,128]{2,1,0:T(8,128)S(1)} all-to-all(f32[32,24,128]{2,1,0:T(8,128)} %get-tuple-element.34), channel_id=1, replica_groups=mesh['y'=4,'z'=8,'core'=2,'crs'=4] {'y','z'}, dimensions={0} | all-to-all | bytes 786432 | tf_op jit(solution)/shard_map/all_to_all | solution.py:627
  124.5 1.4 shard_map.115
  125.9 7.3 %all-to-all-start.6 = ((f32[8,24,128]{2,1,0:T(8,128)}), f32[8,24,128]{2,1,0:T(8,128)S(1)}, u32[]{:S(2)}, u32[]{:S(2)}) async-start(f32[8,24,128]{2,1,0:T(8,128)} %shard_map.115), calls=%async_computation.6 | async-start | bytes 196608 | tf_op jit(solution)/shard_map/all_to_all | solution.py:636
  133.2 2.9 %shard_map.116.refs_9_ = f32[16,128,128]{2,1,0:T(8,128)} custom-call(f32[16,128,128]{2,1,0:T(8,128)} %get-tuple-element.36.refs_0_.refs_8_, f32[16,128,128]{2,1,0:T(8,128)} %refs_1_.13), custom_call_target="tpu_custom_call" | custom-call | flops 200000000 | bytes 2097152 | tf_op jit(solution)/shard_map/pallas_call | solution.py:118
  136.1 2.1 %all-to-all-done.6.refs_0_ = f32[8,24,128]{2,1,0:T(8,128)S(1)} async-done(((f32[8,24,128]{2,1,0:T(8,128)}), f32[8,24,128]{2,1,0:T(8,128)S(1)}, u32[]{:S(2)}, u32[]{:S(2)}) %all-to-all-start.6) | async-done | bytes 98336 | tf_op jit(solution)/shard_map/all_to_all | solution.py:636
  138.9 5.8 %shard_map.117 = (f32[16,128,128]{2,1,0:T(8,128)}, f32[16,128,128]{2,1,0:T(8,128)}, f32[16,128,128]{2,1,0:T(8,128)}) custom-call(f32[8,24,128]{2,1,0:T(8,128)} %copy-done.7, f32[24,128]{1,0:T(8,128)} %get-tuple-element.29.refs_1_, f32[24,128]{1,0:T(8,128)} %get-tuple-element.35.refs_2_, f32[16,128]{1,0:T(8,128)} %refs_3_.5, f32[16,128,128]{2,1,0:T(8,128)} %refs_4_.1, ...), custom_call_target="tpu_custom_call" | custom-call | flops 100000000 | bytes 2097152 | tf_op jit(solution)/shard_map/pallas_call | solution.py:118
  (28 shorter events, 4.5 us)
Async XLA Ops:
  0.6 0.7 copy-start.3
  1.3 0.7 copy-start.4
  3.3 11.7 %all-to-all-start = ((f32[8,32,128]{2,1,0:T(8,128)}), f32[8,32,128]{2,1,0:T(8,128)S(1)}, u32[]{:S(2)}, u32[]{:S(2)}) async-start(f32[8,32,128]{2,1,0:T(8,128)} %shard_map.103), calls=%async_computation | async-start | bytes 262144 | tf_op jit(solution)/shard_map/all_to_all | solution.py:552
  15.0 0.7 copy-start
  16.6 23.5 %all-to-all-start.1 = ((f32[32,24,128]{2,1,0:T(8,128)}), f32[32,24,128]{2,1,0:T(8,128)S(1)}, u32[]{:S(2)}, u32[]{:S(2)}) async-start(f32[32,24,128]{2,1,0:T(8,128)} %shard_map.106), calls=%async_computation.1 | async-start | bytes 786432 | tf_op jit(solution)/shard_map/all_to_all | solution.py:563
  30.8 21.6 %collective-permute-start = (f32[136,128]{1,0:T(8,128)}, f32[136,128]{1,0:T(8,128)S(1)}, u32[]{:S(2)}, u32[]{:S(2)}) collective-permute-start(f32[136,128]{1,0:T(8,128)} %get-tuple-element.24), channel_id=1, source_target_pairs={{0,1},{1,2},{2,3},{3,4},{4,5},{5,6},{6,7},{7,8},{8,9},{9,10},{10,1... | collective-permute-start | bytes 208904 | tf_op jit(solution)/shard_map/ppermute | solution.py:572
  31.6 20.9 %collective-permute-start.1 = (f32[136,128]{1,0:T(8,128)}, f32[136,128]{1,0:T(8,128)S(1)}, u32[]{:S(2)}, u32[]{:S(2)}) collective-permute-start(f32[136,128]{1,0:T(8,128)} %get-tuple-element.25), channel_id=1, source_target_pairs={{1,0},{2,1},{3,2},{4,3},{5,4},{6,5},{7,6},{8,7},{9,8},{10,9},{11,1... | collective-permute-start | bytes 208904 | tf_op jit(solution)/shard_map/ppermute | solution.py:573
  33.8 0.7 copy-start.1
  40.1 0.7 copy-start.2
  44.2 16.1 %all-to-all-start.2 = ((f32[8,24,128]{2,1,0:T(8,128)}), f32[8,24,128]{2,1,0:T(8,128)S(1)}, u32[]{:S(2)}, u32[]{:S(2)}) async-start(f32[8,24,128]{2,1,0:T(8,128)} %get-tuple-element.22), calls=%async_computation.2 | async-start | bytes 196608 | tf_op jit(solution)/shard_map/all_to_all | solution.py:604
  52.4 0.6 copy-start.8
  52.4 0.6 copy-start.9
  60.3 0.6 copy-start.5
  65.2 19.7 %all-to-all-start.3 = ((f32[32,24,128]{2,1,0:T(8,128)}), f32[32,24,128]{2,1,0:T(8,128)S(1)}, u32[]{:S(2)}, u32[]{:S(2)}) async-start(f32[32,24,128]{2,1,0:T(8,128)} %get-tuple-element.28), calls=%async_computation.3 | async-start | bytes 786432 | tf_op jit(solution)/shard_map/all_to_all | solution.py:627
  76.3 18.6 %collective-permute-start.2 = (f32[128,128]{1,0:T(8,128)}, f32[128,128]{1,0:T(8,128)S(1)}, u32[]{:S(2)}, u32[]{:S(2)}) collective-permute-start(f32[128,128]{1,0:T(8,128)} %get-tuple-element.32), channel_id=1, source_target_pairs={{0,1},{1,2},{2,3},{3,4},{4,5},{5,6},{6,7},{7,8},{8,9},{9,10},{10,1... | collective-permute-start | bytes 196616 | tf_op jit(solution)/shard_map/ppermute | solution.py:622
  77.7 17.1 %collective-permute-start.3 = (f32[128,128]{1,0:T(8,128)}, f32[128,128]{1,0:T(8,128)S(1)}, u32[]{:S(2)}, u32[]{:S(2)}) collective-permute-start(f32[128,128]{1,0:T(8,128)} %get-tuple-element.33), channel_id=1, source_target_pairs={{1,0},{2,1},{3,2},{4,3},{5,4},{6,5},{7,6},{8,7},{9,8},{10,9},{11,1... | collective-permute-start | bytes 196616 | tf_op jit(solution)/shard_map/ppermute | solution.py:623
  86.3 15.7 %all-to-all-start.4 = ((f32[8,24,128]{2,1,0:T(8,128)}), f32[8,24,128]{2,1,0:T(8,128)S(1)}, u32[]{:S(2)}, u32[]{:S(2)}) async-start(f32[8,24,128]{2,1,0:T(8,128)} %shard_map.111), calls=%async_computation.4 | async-start | bytes 196608 | tf_op jit(solution)/shard_map/all_to_all | solution.py:636
  94.8 0.6 copy-start.10
  94.8 0.6 copy-start.11
  102.0 0.6 copy-start.6
  125.9 12.3 %all-to-all-start.6 = ((f32[8,24,128]{2,1,0:T(8,128)}), f32[8,24,128]{2,1,0:T(8,128)S(1)}, u32[]{:S(2)}, u32[]{:S(2)}) async-start(f32[8,24,128]{2,1,0:T(8,128)} %shard_map.115), calls=%async_computation.6 | async-start | bytes 196608 | tf_op jit(solution)/shard_map/all_to_all | solution.py:636
  138.2 0.6 copy-start.7

commit v3 on v2

--- a/solution.py
+++ b/solution.py
@@ -13,6 +13,7 @@
 BLK = 128
 KB = 6
 EXT = 18
+MROWS = 19
 ROWS = 24
 CROWS = 16
 RING = ("y", "z", "core", "crs")
@@ -23,7 +24,8 @@
 BIG = 60 * 1024 * 1024
 SMALL = 12 * 1024 * 1024
 TROWS = 32
-CHUNK = 4
+GROUP = 4
+CHUNK = 8
 
 
 def sweep_coefficients():
@@ -163,21 +165,23 @@
 
 def open_body(ready, emit, rows_ref, t_ref, msg_ref):
     ghosts = group_ghosts(t_ref)
-    rows = jnp.concatenate(
-        [rows_ref[: NB + 1], ghosts[:1], ghosts[NB - 1 :], rows_ref[NB + 3 :]], axis=0
-    )
+    rows = jnp.concatenate([rows_ref[: NB + 1], ghosts[:1], ghosts[NB - 1 :]], axis=0)
     broadcast(msg_ref, rows)
     emit(0)
 
 
-def local_body(ready, emit, send_ref, w_ref, r_ref, d_ref, out_ref, prev_ref, next_ref):
+def slot_of(swap):
+    return (lax.axis_index("crs") + 1 + swap) % 2
+
+
+def local_body(ready, emit, send_ref, w_ref, r_ref, d_ref, out_ref, inner_ref, outer_ref):
     for c, blocks in chunks():
         ready(c)
         for i in blocks:
             out_ref[i] = dot3(d_ref[i], r_ref[i])
         emit(0, c)
-    for slot, ref in ((0, prev_ref), (1, next_ref)):
-        block = send_ref[0, slot]
+    for n, ref in ((0, inner_ref), (1, outer_ref)):
+        block = send_ref[0, slot_of(n)]
         ref[:BLK] = out_ref[block]
         ref[BLK:] = jnp.concatenate(
             [w_ref[pl.ds(block, 1), :], jnp.zeros((7, BLK), F32)], axis=0
@@ -199,14 +203,14 @@
     emit(0)
 
 
-def image_body(ready, emit, send_ref, f_ref, d_ref, out_ref, prev_ref, next_ref):
+def image_body(ready, emit, send_ref, f_ref, d_ref, out_ref, inner_ref, outer_ref):
     for c, blocks in chunks():
         ready(c)
         for i in blocks:
             out_ref[i] = dot3(d_ref[i], f_ref[i])
         emit(0, c)
-    for slot, ref in ((0, prev_ref), (1, next_ref)):
-        ref[...] = out_ref[send_ref[0, slot]]
+    for n, ref in ((0, inner_ref), (1, outer_ref)):
+        ref[...] = out_ref[send_ref[0, slot_of(n)]]
 
 
 def product_body(ready, emit, f_ref, d_ref, out_ref):
@@ -257,7 +261,7 @@
         solve_rows(cell_ref[here, :], inv, use)
         return 0
 
-    lax.fori_loop(0, cell_ref.shape[0] // 8, chunk, 0)
+    lax.fori_loop(0, cell_ref.shape[0] // 8, chunk, 0, unroll=2)
     emit(0)
 
 
@@ -266,7 +270,7 @@
     part_ref[:, :NB, :] = part[: devs * NB].reshape(devs, NB, BLK)
     for g in range(devs):
         ghosts = part[devs * NB + 2 * g : devs * NB + 2 * g + 2]
-        part_ref[g, NB:, :] = jnp.concatenate([ghosts, sums[EXT - NB :]], axis=0)
+        part_ref[g, NB:, :] = jnp.concatenate([ghosts, sums], axis=0)
 
 
 def coarse_body(
@@ -311,7 +315,7 @@
     emit(2)
     gh, gl = split(g_ref[:, :NB, :].reshape(sources, BLK))
     part = dot(wh, gh) + (dot(wh, gl) + dot(wl, gh))
-    spread(part, jnp.zeros((ROWS - NB, BLK), F32), part_ref)
+    spread(part, jnp.zeros((ROWS - EXT, BLK), F32), part_ref)
     emit(0)
 
 
@@ -320,58 +324,100 @@
     gh, gl = split(g_ref[:, :NB, :].reshape(devs * NB, BLK))
     wh = wh_ref[...]
     part = dot(wh, gh) + (dot(wh, gl) + dot(wl_ref[...], gh))
-    spread(part, jnp.sum(g_ref[:, NB:, :], axis=0), part_ref)
+    sums = jnp.sum(g_ref[:, NB:, :], axis=0)
+    pad = jnp.zeros((ROWS - EXT - (MROWS - NB), BLK), F32)
+    spread(part, jnp.concatenate([sums, pad], axis=0), part_ref)
     emit(0)
 
 
-def operator_kernel(first, cols_ref, s_ref, f_ref, lo_ref, up_ref, *rest):
+def operator_kernel(first, cols_hbm, s_hbm, f_hbm, inner_hbm, outer_hbm, *rest):
     if first:
-        w_ref, out_ref, q_ref, xh, xl = rest
+        (w_hbm, out_hbm, q_hbm, cols_ref, s_ref, f_ref, inner_ref, outer_ref, out_ref, xh, sem, out_sem,
+         w_ref, q_ref, xl) = rest
     else:
-        out_ref, xh, xl = rest
-    step = pl.program_id(0)
-    per = s_ref.shape[0]
-
-    @pl.when(step == 0)
-    def _():
+        out_hbm, cols_ref, s_ref, f_ref, inner_ref, outer_ref, out_ref, xh, sem, out_sem = rest
+    steps = NB // GROUP
+
+    def part(ref, g):
+        return ref.at[pl.ds(g * GROUP, GROUP)]
+
+    def block(g):
+        return pltpu.make_async_copy(part(s_hbm, g), part(s_ref, g), sem.at[g])
+
+    def result(n, g):
+        source, target = ((out_ref, out_hbm), (q_ref, q_hbm))[n] if first else (out_ref, out_hbm)
+        return pltpu.make_async_copy(part(source, g), part(target, g), out_sem.at[n, g])
+
+    pairs = [(cols_hbm, cols_ref), (f_hbm, f_ref), (inner_hbm, inner_ref), (outer_hbm, outer_ref)]
+    if first:
+        pairs.append((w_hbm, w_ref))
+    head = [pltpu.make_async_copy(a, b, sem.at[steps + n]) for n, (a, b) in enumerate(pairs)]
+    for copy in head:
+        copy.start()
+    for g in range(steps):
+        block(g).start()
+    for copy in head:
+        copy.wait()
+    lane = lax.broadcasted_iota(jnp.int32, (BLK, BLK), 1)
+    odd = lax.axis_index("crs") % 2 == 1
+
+    def lower(rows):
+        return jnp.where(odd, inner_ref[rows, :], outer_ref[rows, :])
+
+    def upper(rows):
+        return jnp.where(odd, outer_ref[rows, :], inner_ref[rows, :])
+
+    if first:
+        wt = w_ref[...].T
+        turned = jnp.concatenate([lower(slice(BLK, None)), upper(slice(BLK, None))], axis=0).T
+    for e in range(EXT):
+        x = f_ref[e] if e < NB else (lower, upper)[e - NB](slice(0, BLK))
+        high, low = split(x)
+        xh[e, :, :BLK] = high
         if first:
-            wt = w_ref[...].T
-            lane = lax.broadcasted_iota(jnp.int32, (BLK, BLK), 1)
-            turned = jnp.concatenate(
-                [lo_ref[BLK:, :], up_ref[BLK:, :]], axis=0
-            ).T
-        for e in range(EXT):
-            x = f_ref[e] if e < NB else (lo_ref, up_ref)[e - NB][:BLK, :]
-            high, low = split(x)
-            xh[e, :, :BLK] = high
             xl[e, :, :BLK] = low
+            at = 8 * (e - NB)
+            col = wt[:, e : e + 1] if e < NB else turned[:, at : at + 1]
+            high, low = split(jnp.where((lane % 32 == e) & (lane < 96), col, 0.0))
+            xh[e, :, BLK:] = high
+            xl[e, :, BLK:] = low
+        else:
+            xh[e, :, BLK:] = low
+
+    def step(g, _):
+        block(g).wait()
+        for b in range(GROUP):
+            i = g * GROUP + b
+            sh, sl, vh, vl = [], [], [], []
+            for k in range(KB):
+                col = cols_ref[k, i]
+                high, low = split(s_ref[i, k])
+                sh.append(high)
+                sl.append(low)
+                vh.append(xh[col])
+                if first:
+                    vl.append(xl[col])
+            sh = jnp.concatenate(sh, axis=1)
+            both = jnp.concatenate([sh, jnp.concatenate(sl, axis=1)], axis=0)
+            image = dot(both, jnp.concatenate(vh, axis=0))
             if first:
-                col = wt[:, e : e + 1] if e < NB else turned[:, 8 * (e - NB) : 1 + 8 * (e - NB)]
-                high, low = split(jnp.where((lane % 32 == e) & (lane < 96), col, 0.0))
-                xh[e, :, BLK:] = high
-                xl[e, :, BLK:] = low
-
-    for b in range(per):
-        sh, sl, vh, vl = [], [], [], []
-        for k in range(KB):
-            col = cols_ref[k, step * per + b]
-            high, low = split(s_ref[b, k])
-            sh.append(high)
-            sl.append(low)
-            vh.append(xh[col])
-            vl.append(xl[col])
-        sh = jnp.concatenate(sh, axis=1)
-        sl = jnp.concatenate(sl, axis=1)
-        vh = jnp.concatenate(vh, axis=0)
-        vl = jnp.concatenate(vl, axis=0)
-        image = dot(sh, vh) + (dot(sh, vl) + dot(sl, vh))
-        out_ref[b] = image[:, :BLK]
+                image = image[:BLK] + (image[BLK:] + dot(sh, jnp.concatenate(vl, axis=0)))
+                high, low = split(image[:, BLK:])
+                q_ref[i] = jnp.where((lane >= 32) & (lane < 64), low.astype(F32), high.astype(F32)).astype(BF16)
+                image = image[:, :BLK]
+            else:
+                image = image[:BLK, :BLK] + (image[:BLK, BLK:] + image[BLK:, :BLK])
+            out_ref[i] = image
+        result(0, g).start()
         if first:
-            q = image[:, BLK:]
-            high = q.astype(BF16)
-            low = (q - high.astype(F32)).astype(BF16)
-            lane = lax.broadcasted_iota(jnp.int32, (BLK, BLK), 1)
-            q_ref[b] = jnp.where((lane >= 32) & (lane < 64), low.astype(F32), high.astype(F32)).astype(BF16)
+            result(1, g).start()
+        return 0
+
+    lax.fori_loop(0, steps, step, 0)
+    for g in range(steps):
+        result(0, g).wait()
+        if first:
+            result(1, g).wait()
 
 
 def pack(u):
@@ -387,9 +433,8 @@
 
 def message(rows, dots):
     sums = [jnp.sum(d, axis=0, keepdims=True) for d in dots]
-    zero = jnp.zeros((1, BLK), F32)
-    end = [zero] * (EXT - NB) + sums + [zero] * (ROWS - EXT - len(dots))
-    return jnp.concatenate(rows + end, axis=0)
+    pad = [jnp.zeros((1, BLK), F32)] * (MROWS - NB - len(dots))
+    return jnp.concatenate(rows + sums + pad, axis=0)
 
 
 def first_body(ready, emit, got_ref, w_ref, r_ref, dr_ref, adr_ref, q_ref, msg_ref, u_ref, im_ref):
@@ -489,35 +534,36 @@
 FIELD = (NB, BLK, BLK)
 
 
-def block_of(shape):
-    return pl.BlockSpec(shape, lambda i: (0,) * len(shape))
-
-
-def apply_operator(stiffness, columns, field, lower, upper, weights=None):
+def apply_operator(stiffness, columns, field, inner, outer, weights=None):
     first = weights is not None
-    per = 4
-    wide = 2 * BLK if first else BLK
-    block = pl.BlockSpec((per, BLK, BLK), lambda i: (i, 0, 0))
+    hbm = pl.BlockSpec(memory_space=pltpu.HBM)
     outs = [jax.ShapeDtypeStruct(FIELD, F32)]
-    args = [columns, stiffness, field, lower, upper]
-    specs = [
-        pl.BlockSpec(memory_space=pltpu.SMEM),
-        pl.BlockSpec((per, KB, BLK, BLK), lambda i: (i, 0, 0, 0)),
-        block_of(FIELD),
-        block_of(lower.shape),
-        block_of(upper.shape),
+    args = [columns, stiffness, field, inner, outer]
+    scratch = [
+        pltpu.SMEM(columns.shape, jnp.int32),
+        pltpu.VMEM(stiffness.shape, F32),
+        pltpu.VMEM(FIELD, F32),
+        pltpu.VMEM(inner.shape, F32),
+        pltpu.VMEM(outer.shape, F32),
+        pltpu.VMEM(FIELD, F32),
+        pltpu.VMEM((EXT, BLK, 2 * BLK), BF16),
+        pltpu.SemaphoreType.DMA((NB // GROUP + 5,)),
+        pltpu.SemaphoreType.DMA((2, NB // GROUP)),
     ]
     if first:
         outs.append(jax.ShapeDtypeStruct(FIELD, BF16))
         args.append(weights)
-        specs.append(block_of(weights.shape))
+        scratch += [
+            pltpu.VMEM(weights.shape, F32),
+            pltpu.VMEM(FIELD, BF16),
+            pltpu.VMEM((EXT, BLK, 2 * BLK), BF16),
+        ]
     return pl.pallas_call(
         functools.partial(operator_kernel, first),
-        grid=(NB // per,),
         out_shape=outs,
-        in_specs=specs,
-        out_specs=[block] * len(outs),
-        scratch_shapes=[pltpu.VMEM((EXT, BLK, wide), BF16)] * 2,
+        in_specs=[hbm] * len(args),
+        out_specs=[hbm] * len(outs),
+        scratch_shapes=scratch,
         compiler_params=pltpu.CompilerParams(vmem_limit_bytes=BIG),
         cost_estimate=pl.CostEstimate(flops=6 * 10**9, bytes_accessed=8 << 20, transcendentals=0),
     )(*args)
@@ -529,13 +575,15 @@
     devices = lax.axis_size(RING)
     gathered = lax.axis_size(GATHER)
     scattered = lax.axis_size(SCATTER)
-    up = [(i, (i + 1) % devices) for i in range(devices)]
-    down = [(j, i) for i, j in up]
+    swaps = []
+    for first in (0, 1):
+        pairs = [((first + 2 * i) % devices, (first + 2 * i + 1) % devices) for i in range(devices // 2)]
+        swaps.append(pairs + [(j, i) for i, j in pairs])
     send = (send_lists.reshape(1, 2), "scalar")
     cells = (coarse_map, "scalar")
     columns = columns.T
     weights = (restrict_weights, "whole")
-    msg_out = ((gathered, ROWS, BLK), F32, "whole")
+    msg_out = ((gathered, MROWS, BLK), F32, "whole")
     part_shape = (scattered, ROWS, BLK)
     part_out = (part_shape, F32, "whole")
     short_out = (part_shape[1:], F32, "whole")
@@ -547,7 +595,6 @@
         [send, cells],
         [((scattered, TROWS, BLK), F32, "whole")],
         moved=1 << 18,
-        limit=SMALL,
     )
     targets = lax.all_to_all(target, SCATTER, 0, 0, tiled=True)
     (start_rows,) = staged(
@@ -562,33 +609,34 @@
     )
     got = lax.all_to_all(msg, GATHER, 0, 0, tiled=True)
     packet = ((BLK + 8, BLK), F32, "vmem")
-    local, to_prev, to_next = staged(
+    local, inner, outer = staged(
         local_body,
         [send, weights, (loads, "field"), (inv_diag, "field")],
         [field_out, packet, packet],
         flops=2 * 10**8,
         moved=big,
     )
-    lower = lax.ppermute(to_next, RING, up)
-    upper = lax.ppermute(to_prev, RING, down)
+    inner = lax.ppermute(inner, RING, swaps[0])
+    outer = lax.ppermute(outer, RING, swaps[1])
     rows = scattered * EXT
     (coarse_rows,) = staged(
         sweep_body,
-        [(targets, "vmem"), (coarse_diag, "whole")],
+        [(targets, "vmem"), (coarse_diag, "vmem")],
         [((CROWS, rows, BLK), F32, "whole")],
         scratch=[pltpu.VMEM((rows, BLK), F32)],
         flops=10**8,
         moved=big,
         limit=SMALL,
     )
+    got, inner, outer = lax.optimization_barrier((got, inner, outer))
     image_local, coupling = apply_operator(
-        stiffness, columns, local, lower, upper, restrict_weights
+        stiffness, columns, local, inner, outer, restrict_weights
     )
     weights_out = ((rows, gathered * NB), BF16, "whole")
     cells_all = CROWS * BLK
     part, wh, wl = staged(
         coarse_body,
-        [(coarse_rows, "hbm"), (coarse_diag, "whole"), (got, "vmem")],
+        [(coarse_rows, "hbm"), (coarse_diag, "vmem"), (got, "vmem")],
         [part_out, weights_out, weights_out],
         scratch=[
             pltpu.VMEM((CROWS, rows, BLK), F32),
@@ -605,26 +653,27 @@
 
     msg, u0, image0 = staged(
         first_body,
-        [(got, "vmem"), weights, (loads, "field"), (local, "field"), (image_local, "field"),
+        [(got, "whole"), weights, (loads, "field"), (local, "field"), (image_local, "field"),
          (coupling, "field")],
         [msg_out, short_out, field_out],
         flops=10**8,
         moved=big,
     )
     packet = ((BLK, BLK), F32, "vmem")
-    local_image, to_prev, to_next = staged(
+    local_image, inner, outer = staged(
         image_body,
         [send, (image0, "field"), (inv_diag, "field")],
         [field_out, packet, packet],
         flops=2 * 10**8,
         moved=big,
     )
-    lower = lax.ppermute(to_next, RING, up)
-    upper = lax.ppermute(to_prev, RING, down)
-    (image_image,) = apply_operator(stiffness, columns, local_image, lower, upper)
-
-    def exchange(msg):
+    inner = lax.ppermute(inner, RING, swaps[0])
+    outer = lax.ppermute(outer, RING, swaps[1])
+    (image_image,) = apply_operator(stiffness, columns, local_image, inner, outer)
+
+    def exchange(msg, ahead):
         got = lax.all_to_all(msg, GATHER, 0, 0, tiled=True)
+        got, ahead = lax.optimization_barrier((got, ahead))
         (part,) = staged(
             apply_body,
             [(wh, "whole"), (wl, "whole"), (got, "vmem")],
@@ -633,12 +682,12 @@
             moved=big,
             limit=SMALL,
         )
-        return lax.all_to_all(part, SCATTER, 0, 0, tiled=True)
-
-    got = exchange(msg)
+        return lax.all_to_all(part, SCATTER, 0, 0, tiled=True), ahead
+
+    got, local_image = exchange(msg, local_image)
     msg, v0, image1 = staged(
         second_body,
-        [(got, "vmem"), (u0, "whole"), weights, (loads, "field"), (image0, "field"),
+        [(got, "whole"), (u0, "whole"), weights, (loads, "field"), (image0, "field"),
          (local, "field"), (local_image, "field"), (image_local, "field"),
          (image_image, "field"), (coupling, "field")],
         [msg_out, short_out, field_out],
@@ -652,11 +701,11 @@
         flops=2 * 10**8,
         moved=big,
     )
-    got = exchange(msg)
+    got, local_image1 = exchange(msg, local_image1)
     return tuple(
         staged(
             last_body,
-            [(got, "vmem"), (u0, "whole"), (v0, "whole"), weights, (loads, "field"),
+            [(got, "whole"), (u0, "whole"), (v0, "whole"), weights, (loads, "field"),
              (image0, "field"), (local, "field"), (local_image, "field"), (image1, "field"),
              (local_image1, "field")],
             [field_out] * 3,

time: 146 us -> 134 us (0.918)
  Pallas kernels: 55.8 us -> 47.2 us
  waiting for transfers between devices: 10.3 us -> 18.5 us
  starting transfers between devices: 54.8 us -> 49.6 us
  blocking collectives: 16.3 us -> 12.2 us
  local copies, waits for them, and re-layouts: 6.56 us -> 4.6 us
    all_to_all x1 -> x2, waiting for transfers between devices: 5.35 us -> 14.1 us  [exchange(): got = lax.all_to_all(msg, GATHER, 0, 0, tiled=True)]
    all_to_all x2 -> x1, starting transfers between devices: 15.8 us -> 7.42 us  [exchange(): return (lax.all_to_all(part, SCATTER, 0, 0, tiled=True), ahead)]
    pallas_call x13, Pallas kernels: 42 us -> 36.1 us  [staged(): pl.pallas_call(kernel, out_shape=[jax.ShapeDtypeStruct(sh, dt) for sh, dt...]
    all_to_all x1 -> x2, starting transfers between devices: 7.41 us -> 11.6 us  [exchange(): got = lax.all_to_all(msg, GATHER, 0, 0, tiled=True)]
    all_to_all x1, blocking collectives: 16.3 us -> 12.2 us  [exchange(): return (lax.all_to_all(part, SCATTER, 0, 0, tiled=True), ahead)]
    pallas_call x2, Pallas kernels: 13.8 us -> 11.1 us  [apply_operator(): pl.pallas_call(functools.partial(operator_kernel, first), out_shape=outs,...]
    all_to_all x2 -> x1, waiting for transfers between devices: 2.1 us -> 0.01 us  [exchange(): return (lax.all_to_all(part, SCATTER, 0, 0, tiled=True), ahead)]
    unnamed x24 -> x18, local copies, waits for them, and re-layouts: 6.56 us -> 4.6 us
  transfers between devices with their start and end apart: 10 -> 10, of which waited for: 3 -> 4; matrix products, arithmetic and copies ran while one was open for 0% -> 0% of each run, Pallas kernels for 25% -> 21%
where the time goes in v3:
time: 134 us; the launch traced here: 133 us
  starting transfers between devices  49.6 us (37%)
  Pallas kernels  47.2 us (35%)
  waiting for transfers between devices  18.5 us (14%)
  blocking collectives  12.2 us (9%)
  local copies, waits for them, and re-layouts  4.6 us (3%)
    pallas_call x13, Pallas kernels, staged(): pl.pallas_call(kernel, out_shape=[jax.ShapeDtypeStruct(sh, dt) for sh, dt...  36.1 us
    all_to_all x2, waiting for transfers between devices, exchange(): got = lax.all_to_all(msg, GATHER, 0, 0, tiled=True)  14.1 us
    all_to_all x1, blocking collectives, exchange(): return (lax.all_to_all(part, SCATTER, 0, 0, tiled=True), ahead)  12.2 us
    all_to_all x2, starting transfers between devices, exchange(): got = lax.all_to_all(msg, GATHER, 0, 0, tiled=True)  11.6 us
    pallas_call x2, Pallas kernels, apply_operator(): pl.pallas_call(functools.partial(operator_kernel, first), out_shape=outs,...  11.1 us
    all_to_all x1, starting transfers between devices, on_device(): got = lax.all_to_all(msg, GATHER, 0, 0, tiled=True)  10.5 us
    all_to_all x1, starting transfers between devices, exchange(): return (lax.all_to_all(part, SCATTER, 0, 0, tiled=True), ahead)  7.42 us
    all_to_all x1, starting transfers between devices, on_device(): got = lax.all_to_all(part, SCATTER, 0, 0, tiled=True)  7.22 us
  transfers between devices with their start and end apart: 10, of which 4 were waited for; matrix products, arithmetic and copies ran while one was open for 0% of the time, Pallas kernels for 21%

profile of v3, /device:TPU:1, one launch (start us, length us, event | category | flops | bytes accessed | tf_op | source)
XLA Modules:
  0.0 132.9 jit_solution(14356902362601431570)
XLA Ops:
  0.6 1.4 %shard_map.103 = f32[8,32,128]{2,1,0:T(8,128)} custom-call(s32[1,2]{1,0:T(1,128)} %bitcast.2, s32[16]{0:T(128)} %refs_0_.1), custom_call_target="tpu_custom_call" | custom-call | bytes 262144 | tf_op jit(solution)/shard_map/pallas_call | solution.py:120
  2.0 6.5 %all-to-all-start = ((f32[8,32,128]{2,1,0:T(8,128)}), f32[8,32,128]{2,1,0:T(8,128)S(1)}, u32[]{:S(2)}, u32[]{:S(2)}) async-start(f32[8,32,128]{2,1,0:T(8,128)} %shard_map.103), calls=%async_computation | async-start | bytes 262144 | tf_op jit(solution)/shard_map/all_to_all | solution.py:599
  8.6 2.2 %shard_map.105.refs_0_ = f32[24,128]{1,0:T(8,128)} custom-call(s32[16]{0:T(128)} %refs_0_.1, f32[16,128]{1,0:T(8,128)} %refs_3_.5, f32[16,128,128]{2,1,0:T(8,128)} %refs_4_.1), custom_call_target="tpu_custom_call" | custom-call | flops 1000000 | bytes 2097152 | tf_op jit(solution)/shard_map/pallas_call | solution.py:120
  10.8 3.0 %all-to-all-done.refs_0_.refs_1_ = f32[8,32,128]{2,1,0:T(8,128)S(1)} async-done(((f32[8,32,128]{2,1,0:T(8,128)}), f32[8,32,128]{2,1,0:T(8,128)S(1)}, u32[]{:S(2)}, u32[]{:S(2)}) %all-to-all-start) | async-done | bytes 131104 | tf_op jit(solution)/shard_map/all_to_all | solution.py:599
  13.8 0.7 copy-done
  14.5 0.8 shard_map.106
  15.3 10.5 %all-to-all-start.1 = ((f32[32,19,128]{2,1,0:T(8,128)}), f32[32,19,128]{2,1,0:T(8,128)S(1)}, u32[]{:S(2)}, u32[]{:S(2)}) async-start(f32[32,19,128]{2,1,0:T(8,128)} %shard_map.106), calls=%async_computation.1 | async-start | bytes 786432 | tf_op jit(solution)/shard_map/all_to_all | solution.py:610
  25.8 3.5 %shard_map.107 = (f32[16,128,128]{2,1,0:T(8,128)}, f32[136,128]{1,0:T(8,128)}, f32[136,128]{1,0:T(8,128)}) custom-call(s32[1,2]{1,0:T(1,128)} %bitcast.3, f32[16,128]{1,0:T(8,128)} %refs_3_.5, f32[16,128,128]{2,1,0:T(8,128)} %refs_4_.1, f32[16,128,128]{2,1,0:T(8,128)} %refs_1_.13), custom_call_target="tpu_custom_call" | custom-call | flops 200000000 | bytes 2097152 | tf_op jit(solution)/shard_map/pallas_call | solution.py:120
  29.3 0.8 collective-permute-start
  30.1 1.4 %collective-permute-start.1 = (f32[136,128]{1,0:T(8,128)}, f32[136,128]{1,0:T(8,128)S(1)}, u32[]{:S(2)}, u32[]{:S(2)}) collective-permute-start(f32[136,128]{1,0:T(8,128)} %get-tuple-element.28), channel_id=1, source_target_pairs={{1,2},{3,4},{5,6},{7,8},{9,10},{11,12},{13,14},{15,16},{17,18},{19... | collective-permute-start | bytes 208904 | tf_op jit(solution)/shard_map/ppermute | solution.py:620
  32.2 3.9 %shard_map.104.refs_0_ = f32[16,144,128]{2,1,0:T(8,128)S(1)} custom-call(f32[8,32,128]{2,1,0:T(8,128)S(1)} %all-to-all-done.refs_0_.refs_1_, f32[16,128]{1,0:T(8,128)S(1)} %copy-done.1), custom_call_target="tpu_custom_call" | custom-call | flops 100000000 | bytes 2097152 | tf_op jit(solution)/shard_map/pallas_call | solution.py:120
  36.2 1.3 %all-to-all-done.1.refs_2_ = f32[32,19,128]{2,1,0:T(8,128)S(1)} async-done(((f32[32,19,128]{2,1,0:T(8,128)}), f32[32,19,128]{2,1,0:T(8,128)S(1)}, u32[]{:S(2)}, u32[]{:S(2)}) %all-to-all-start.1) | async-done | bytes 311328 | tf_op jit(solution)/shard_map/all_to_all | solution.py:610
  37.5 0.7 copy-done.2
  38.2 3.3 %shard_map.108 = (f32[8,24,128]{2,1,0:T(8,128)}, bf16[144,512]{1,0:T(8,128)(2,1)S(1)}, bf16[144,512]{1,0:T(8,128)(2,1)S(1)}) custom-call(f32[16,144,128]{2,1,0:T(8,128)S(1)} %shard_map.104.refs_0_, f32[16,128]{1,0:T(8,128)S(1)} %copy-done.2, f32[32,19,128]{2,1,0:T(8,128)S(1)} %all-to-all-done.1.refs_2_), custom_call_target="tpu_custom_call" | custom-call | flops 1000000000 | bytes 2097152 | tf_op jit(solution)/shard_map/pallas_call | solution.py:120
  41.5 7.2 %all-to-all-start.2 = ((f32[8,24,128]{2,1,0:T(8,128)}), f32[8,24,128]{2,1,0:T(8,128)S(1)}, u32[]{:S(2)}, u32[]{:S(2)}) async-start(f32[8,24,128]{2,1,0:T(8,128)} %get-tuple-element.32), calls=%async_computation.2 | async-start | bytes 196608 | tf_op jit(solution)/shard_map/all_to_all | solution.py:652
  48.8 6.1 %shard_map.109 = (f32[16,128,128]{2,1,0:T(8,128)}, bf16[16,128,128]{2,1,0:T(8,128)(2,1)}) custom-call(s32[6,16]{1,0:T(8,128)} %bitcast.5, f32[16,6,128,128]{3,2,1,0:T(8,128)} %s_hbm.3, f32[16,128,128]{2,1,0:T(8,128)} %get-tuple-element.33.f_hbm.refs_3_.refs_5_.refs_6_, f32[136,128]{1,0:T(8,128)} %copy-done.5, f32[136,128]{1,0:T(8,128)} %copy-done.6, ...), custom_call_target="tpu_custom_call" | custom-call | flops 6000000000 | bytes 8388608 | tf_op jit(solution)/shard_map/pallas_call | solution.py:561
  55.6 3.4 %shard_map.110 = (f32[32,19,128]{2,1,0:T(8,128)}, f32[24,128]{1,0:T(8,128)}, f32[16,128,128]{2,1,0:T(8,128)}) custom-call(f32[8,24,128]{2,1,0:T(8,128)} %copy-done.4, f32[16,128]{1,0:T(8,128)} %refs_3_.5, f32[16,128,128]{2,1,0:T(8,128)} %refs_4_.1, f32[16,128,128]{2,1,0:T(8,128)} %get-tuple-element.33.f_hbm.refs_3_.refs_5_.refs_6_, ...), custom_call_target="tpu_custom_call" | custom-call | flops 100000000 | bytes 2097152 | tf_op jit(solution)/shard_map/pallas_call | solution.py:120
  58.9 6.4 %all-to-all-start.3 = ((f32[32,19,128]{2,1,0:T(8,128)}), f32[32,19,128]{2,1,0:T(8,128)S(1)}, u32[]{:S(2)}, u32[]{:S(2)}) async-start(f32[32,19,128]{2,1,0:T(8,128)} %get-tuple-element.38), calls=%async_computation.3 | async-start | bytes 786432 | tf_op jit(solution)/shard_map/all_to_all | solution.py:675
  65.4 3.5 %shard_map.111 = (f32[16,128,128]{2,1,0:T(8,128)}, f32[128,128]{1,0:T(8,128)}, f32[128,128]{1,0:T(8,128)}) custom-call(s32[1,2]{1,0:T(1,128)} %bitcast.4, f32[16,128,128]{2,1,0:T(8,128)} %get-tuple-element.39.refs_1_.refs_4_.refs_5_, f32[16,128,128]{2,1,0:T(8,128)} %refs_1_.13), custom_call_target="tpu_custom_call" | custom-call | flops 200000000 | bytes 2097152 | tf_op jit(solution)/shard_map/pallas_call | solution.py:120
  68.9 1.4 %collective-permute-start.2 = (f32[128,128]{1,0:T(8,128)}, f32[128,128]{1,0:T(8,128)S(1)}, u32[]{:S(2)}, u32[]{:S(2)}) collective-permute-start(f32[128,128]{1,0:T(8,128)} %get-tuple-element.44), channel_id=1, source_target_pairs={{0,1},{2,3},{4,5},{6,7},{8,9},{10,11},{12,13},{14,15},{16,17},{18,... | collective-permute-start | bytes 196616 | tf_op jit(solution)/shard_map/ppermute | solution.py:670
  70.3 2.6 %collective-permute-start.3 = (f32[128,128]{1,0:T(8,128)}, f32[128,128]{1,0:T(8,128)S(1)}, u32[]{:S(2)}, u32[]{:S(2)}) collective-permute-start(f32[128,128]{1,0:T(8,128)} %get-tuple-element.45), channel_id=1, source_target_pairs={{1,2},{3,4},{5,6},{7,8},{9,10},{11,12},{13,14},{15,16},{17,18},{19... | collective-permute-start | bytes 196616 | tf_op jit(solution)/shard_map/ppermute | solution.py:671
  72.9 4.7 %all-to-all-done.3.refs_2_ = f32[32,19,128]{2,1,0:T(8,128)S(1)} async-done(((f32[32,19,128]{2,1,0:T(8,128)}), f32[32,19,128]{2,1,0:T(8,128)S(1)}, u32[]{:S(2)}, u32[]{:S(2)}) %all-to-all-start.3) | async-done | bytes 311328 | tf_op jit(solution)/shard_map/all_to_all | solution.py:675
  77.6 1.3 %shard_map.112 = f32[8,24,128]{2,1,0:T(8,128)} custom-call(bf16[144,512]{1,0:T(8,128)(2,1)S(1)} %get-tuple-element.30.refs_0_, bf16[144,512]{1,0:T(8,128)(2,1)S(1)} %get-tuple-element.31.refs_1_, f32[32,19,128]{2,1,0:T(8,128)S(1)} %all-to-all-done.3.refs_2_), custom_call_target="tpu_custom_call" | custom-call | flops 100000000 | bytes 2097152 | tf_op jit(solution)/shard_map/pallas_call | solution.py:120
  79.0 7.4 %all-to-all-start.4 = ((f32[8,24,128]{2,1,0:T(8,128)}), f32[8,24,128]{2,1,0:T(8,128)S(1)}, u32[]{:S(2)}, u32[]{:S(2)}) async-start(f32[8,24,128]{2,1,0:T(8,128)} %shard_map.112), calls=%async_computation.4 | async-start | bytes 196608 | tf_op jit(solution)/shard_map/all_to_all | solution.py:685
  87.6 4.9 %shard_map.113.refs_8_ = f32[16,128,128]{2,1,0:T(8,128)} custom-call(s32[6,16]{1,0:T(8,128)} %bitcast.6, f32[16,6,128,128]{3,2,1,0:T(8,128)} %s_hbm.3, f32[16,128,128]{2,1,0:T(8,128)} %get-tuple-element.43.f_hbm.refs_6_.refs_7_, f32[128,128]{1,0:T(8,128)} %copy-done.7, f32[128,128]{1,0:T(8,128)} %copy-done.8), custom_call_target="tpu_custom_call" | custom-call | flops 6000000000 | bytes 8388608 | tf_op jit(solution)/shard_map/pallas_call | solution.py:561
  93.2 4.6 %shard_map.114 = (f32[32,19,128]{2,1,0:T(8,128)}, f32[24,128]{1,0:T(8,128)}, f32[16,128,128]{2,1,0:T(8,128)}) custom-call(f32[8,24,128]{2,1,0:T(8,128)} %copy-done.3, f32[24,128]{1,0:T(8,128)} %get-tuple-element.42.refs_1_, f32[16,128]{1,0:T(8,128)} %refs_3_.5, f32[16,128,128]{2,1,0:T(8,128)} %refs_4_.1, ...), custom_call_target="tpu_custom_call" | custom-call | flops 100000000 | bytes 2097152 | tf_op jit(solution)/shard_map/pallas_call | solution.py:120
  97.8 5.2 %all-to-all-start.5 = ((f32[32,19,128]{2,1,0:T(8,128)}), f32[32,19,128]{2,1,0:T(8,128)S(1)}, u32[]{:S(2)}, u32[]{:S(2)}) async-start(f32[32,19,128]{2,1,0:T(8,128)} %get-tuple-element.46), calls=%async_computation.5 | async-start | bytes 786432 | tf_op jit(solution)/shard_map/all_to_all | solution.py:675
  103.1 2.8 %shard_map.115.refs_9_ = f32[16,128,128]{2,1,0:T(8,128)} custom-call(f32[16,128,128]{2,1,0:T(8,128)} %get-tuple-element.47.refs_0_.refs_8_, f32[16,128,128]{2,1,0:T(8,128)} %refs_1_.13), custom_call_target="tpu_custom_call" | custom-call | flops 200000000 | bytes 2097152 | tf_op jit(solution)/shard_map/pallas_call | solution.py:120
  105.9 9.4 %all-to-all-done.5.refs_2_ = f32[32,19,128]{2,1,0:T(8,128)S(1)} async-done(((f32[32,19,128]{2,1,0:T(8,128)}), f32[32,19,128]{2,1,0:T(8,128)S(1)}, u32[]{:S(2)}, u32[]{:S(2)}) %all-to-all-start.5) | async-done | bytes 311328 | tf_op jit(solution)/shard_map/all_to_all | solution.py:675
  115.3 0.8 shard_map.116
  116.1 12.2 %all_to_all.35.refs_0_ = f32[8,24,128]{2,1,0:T(8,128)} all-to-all(f32[8,24,128]{2,1,0:T(8,128)S(1)} %shard_map.116), channel_id=1, replica_groups=mesh['y'=4,'z'=8,'core'=2,'crs'=4] {'core','crs'}, dimensions={0} | all-to-all | bytes 196608 | tf_op jit(solution)/shard_map/all_to_all | solution.py:685
  128.3 4.6 %shard_map.117 = (f32[16,128,128]{2,1,0:T(8,128)}, f32[16,128,128]{2,1,0:T(8,128)}, f32[16,128,128]{2,1,0:T(8,128)}) custom-call(f32[8,24,128]{2,1,0:T(8,128)} %all_to_all.35.refs_0_, f32[24,128]{1,0:T(8,128)} %get-tuple-element.42.refs_1_, f32[24,128]{1,0:T(8,128)} %get-tuple-element.49.refs_2_, f32[16,128]{1,0:T(8,128)} %refs_3_.5, ...), custom_call_target="tpu_custom_call" | custom-call | flops 100000000 | bytes 2097152 | tf_op jit(solution)/shard_map/pallas_call | solution.py:120
  (22 shorter events, 3.2 us)
Async XLA Ops:
  2.0 11.7 %all-to-all-start = ((f32[8,32,128]{2,1,0:T(8,128)}), f32[8,32,128]{2,1,0:T(8,128)S(1)}, u32[]{:S(2)}, u32[]{:S(2)}) async-start(f32[8,32,128]{2,1,0:T(8,128)} %shard_map.103), calls=%async_computation | async-start | bytes 262144 | tf_op jit(solution)/shard_map/all_to_all | solution.py:599
  13.8 0.7 copy-start
  15.3 22.3 %all-to-all-start.1 = ((f32[32,19,128]{2,1,0:T(8,128)}), f32[32,19,128]{2,1,0:T(8,128)S(1)}, u32[]{:S(2)}, u32[]{:S(2)}) async-start(f32[32,19,128]{2,1,0:T(8,128)} %shard_map.106), calls=%async_computation.1 | async-start | bytes 786432 | tf_op jit(solution)/shard_map/all_to_all | solution.py:610
  29.3 6.8 %collective-permute-start = (f32[136,128]{1,0:T(8,128)}, f32[136,128]{1,0:T(8,128)S(1)}, u32[]{:S(2)}, u32[]{:S(2)}) collective-permute-start(f32[136,128]{1,0:T(8,128)} %get-tuple-element.27), channel_id=1, source_target_pairs={{0,1},{2,3},{4,5},{6,7},{8,9},{10,11},{12,13},{14,15},{16,17},{18,... | collective-permute-start | bytes 208904 | tf_op jit(solution)/shard_map/ppermute | solution.py:619
  30.1 6.1 %collective-permute-start.1 = (f32[136,128]{1,0:T(8,128)}, f32[136,128]{1,0:T(8,128)S(1)}, u32[]{:S(2)}, u32[]{:S(2)}) collective-permute-start(f32[136,128]{1,0:T(8,128)} %get-tuple-element.28), channel_id=1, source_target_pairs={{1,2},{3,4},{5,6},{7,8},{9,10},{11,12},{13,14},{15,16},{17,18},{19... | collective-permute-start | bytes 208904 | tf_op jit(solution)/shard_map/ppermute | solution.py:620
  31.5 0.7 copy-start.1
  36.1 12.6 %copy-start.5 = (f32[136,128]{1,0:T(8,128)}, f32[136,128]{1,0:T(8,128)S(1)}, u32[]{:S(2)}) copy-start(f32[136,128]{1,0:T(8,128)S(1)} %collective-permute-done.inner_hbm) | copy-start | bytes 208900
  36.2 12.6 %copy-start.6 = (f32[136,128]{1,0:T(8,128)}, f32[136,128]{1,0:T(8,128)S(1)}, u32[]{:S(2)}) copy-start(f32[136,128]{1,0:T(8,128)S(1)} %collective-permute-done.1.outer_hbm) | copy-start | bytes 208900
  37.5 0.7 copy-start.2
  41.5 13.4 %all-to-all-start.2 = ((f32[8,24,128]{2,1,0:T(8,128)}), f32[8,24,128]{2,1,0:T(8,128)S(1)}, u32[]{:S(2)}, u32[]{:S(2)}) async-start(f32[8,24,128]{2,1,0:T(8,128)} %get-tuple-element.32), calls=%async_computation.2 | async-start | bytes 196608 | tf_op jit(solution)/shard_map/all_to_all | solution.py:652
  54.9 0.6 copy-start.4
  58.9 18.7 %all-to-all-start.3 = ((f32[32,19,128]{2,1,0:T(8,128)}), f32[32,19,128]{2,1,0:T(8,128)S(1)}, u32[]{:S(2)}, u32[]{:S(2)}) async-start(f32[32,19,128]{2,1,0:T(8,128)} %get-tuple-element.38), calls=%async_computation.3 | async-start | bytes 786432 | tf_op jit(solution)/shard_map/all_to_all | solution.py:675
  68.9 17.5 %collective-permute-start.2 = (f32[128,128]{1,0:T(8,128)}, f32[128,128]{1,0:T(8,128)S(1)}, u32[]{:S(2)}, u32[]{:S(2)}) collective-permute-start(f32[128,128]{1,0:T(8,128)} %get-tuple-element.44), channel_id=1, source_target_pairs={{0,1},{2,3},{4,5},{6,7},{8,9},{10,11},{12,13},{14,15},{16,17},{18,... | collective-permute-start | bytes 196616 | tf_op jit(solution)/shard_map/ppermute | solution.py:670
  70.3 16.1 %collective-permute-start.3 = (f32[128,128]{1,0:T(8,128)}, f32[128,128]{1,0:T(8,128)S(1)}, u32[]{:S(2)}, u32[]{:S(2)}) collective-permute-start(f32[128,128]{1,0:T(8,128)} %get-tuple-element.45), channel_id=1, source_target_pairs={{1,2},{3,4},{5,6},{7,8},{9,10},{11,12},{13,14},{15,16},{17,18},{19... | collective-permute-start | bytes 196616 | tf_op jit(solution)/shard_map/ppermute | solution.py:671
  79.0 13.6 %all-to-all-start.4 = ((f32[8,24,128]{2,1,0:T(8,128)}), f32[8,24,128]{2,1,0:T(8,128)S(1)}, u32[]{:S(2)}, u32[]{:S(2)}) async-start(f32[8,24,128]{2,1,0:T(8,128)} %shard_map.112), calls=%async_computation.4 | async-start | bytes 196608 | tf_op jit(solution)/shard_map/all_to_all | solution.py:685
  86.4 0.6 copy-start.7
  87.0 0.6 copy-start.8
  92.6 0.6 copy-start.3
  97.8 17.5 %all-to-all-start.5 = ((f32[32,19,128]{2,1,0:T(8,128)}), f32[32,19,128]{2,1,0:T(8,128)S(1)}, u32[]{:S(2)}, u32[]{:S(2)}) async-start(f32[32,19,128]{2,1,0:T(8,128)} %get-tuple-element.46), calls=%async_computation.5 | async-start | bytes 786432 | tf_op jit(solution)/shard_map/all_to_all | solution.py:675

commit v4 on v3

--- a/solution.py
+++ b/solution.py
@@ -13,7 +13,7 @@
 BLK = 128
 KB = 6
 EXT = 18
-MROWS = 19
+DOTS = EXT
 ROWS = 24
 CROWS = 16
 RING = ("y", "z", "core", "crs")
@@ -23,7 +23,7 @@
 BF16 = jnp.bfloat16
 BIG = 60 * 1024 * 1024
 SMALL = 12 * 1024 * 1024
-TROWS = 32
+TROWS = 48
 GROUP = 4
 CHUNK = 8
 
@@ -82,7 +82,7 @@
         first = [
             pltpu.make_async_copy(s, b, sem_in.at[j, 0])
             for j, (s, b, k) in enumerate(zip(sources, bufs_in, kinds_in))
-            if k in ("whole", "scalar")
+            if k in ("whole", "scalar", "any")
         ]
         fields = [
             [
@@ -115,7 +115,7 @@
             copy.wait()
 
     def spec(kind):
-        return pl.BlockSpec(memory_space=pltpu.VMEM if kind == "vmem" else pltpu.HBM)
+        return pl.BlockSpec(memory_space={"vmem": pltpu.VMEM, "any": pl.ANY}.get(kind, pltpu.HBM))
 
     return pl.pallas_call(
         kernel,
@@ -160,12 +160,14 @@
 
 
 def group_ghosts(t_ref):
-    return jnp.sum(t_ref[:, NB:, :], axis=0)
+    return jnp.sum(t_ref[:, NB : 2 * NB, :], axis=0)
 
 
 def open_body(ready, emit, rows_ref, t_ref, msg_ref):
     ghosts = group_ghosts(t_ref)
-    rows = jnp.concatenate([rows_ref[: NB + 1], ghosts[:1], ghosts[NB - 1 :]], axis=0)
+    lane = lax.broadcasted_iota(jnp.int32, (1, BLK), 1)
+    ends = jnp.where(lane < BLK // 2, ghosts[:1], ghosts[NB - 1 :])
+    rows = jnp.concatenate([rows_ref[: NB + 1], ends], axis=0)
     broadcast(msg_ref, rows)
     emit(0)
 
@@ -174,12 +176,17 @@
     return (lax.axis_index("crs") + 1 + swap) % 2
 
 
-def local_body(ready, emit, send_ref, w_ref, r_ref, d_ref, out_ref, inner_ref, outer_ref):
+def local_body(ready, emit, send_ref, w_ref, r_ref, d_ref, out_ref, inner_ref, outer_ref, dot_ref):
+    total = jnp.zeros((8, BLK), F32)
     for c, blocks in chunks():
         ready(c)
         for i in blocks:
-            out_ref[i] = dot3(d_ref[i], r_ref[i])
+            product = dot3(d_ref[i], r_ref[i])
+            out_ref[i] = product
+            total = total + fold(r_ref[i] * product)
         emit(0, c)
+    dot_ref[...] = total
+    emit(3)
     for n, ref in ((0, inner_ref), (1, outer_ref)):
         block = send_ref[0, slot_of(n)]
         ref[:BLK] = out_ref[block]
@@ -188,7 +195,7 @@
         )
 
 
-def target_body(ready, emit, send_ref, map_ref, out_ref):
+def target_body(ready, emit, send_ref, map_ref, diag_ref, out_ref):
     slots = 2 * out_ref.shape[0]
     place = lax.axis_index(SCATTER)
     row = lax.broadcasted_iota(jnp.int32, (slots, BLK), 0)
@@ -199,26 +206,39 @@
     own = column_cells(map_ref)
     for a in range(out_ref.shape[0]):
         out_ref[a, :NB] = own
-        out_ref[a, NB:] = ghosts
+        out_ref[a, NB : 2 * NB] = ghosts
+        out_ref[a, 2 * NB :] = diag_ref[...]
     emit(0)
 
 
-def image_body(ready, emit, send_ref, f_ref, d_ref, out_ref, inner_ref, outer_ref):
+def image_body(
+    ready, emit, send_ref, u_ref, adr_ref, q_ref, d_ref, im_ref, out_ref, inner_ref, outer_ref
+):
+    packed = pack(u_ref[...])
     for c, blocks in chunks():
         ready(c)
         for i in blocks:
-            out_ref[i] = dot3(d_ref[i], f_ref[i])
+            image = adr_ref[i] + dot(q_ref[i], packed)
+            im_ref[i] = image
+            out_ref[i] = dot3(d_ref[i], image)
         emit(0, c)
+        emit(1, c)
     for n, ref in ((0, inner_ref), (1, outer_ref)):
         ref[...] = out_ref[send_ref[0, slot_of(n)]]
 
 
-def product_body(ready, emit, f_ref, d_ref, out_ref):
+def product_body(ready, emit, v_ref, im_ref, adim_ref, q_ref, d_ref, az_ref, daz_ref):
+    v = v_ref[...]
+    alpha = v[EXT : EXT + 1] / v[EXT + 1 : EXT + 2]
+    packed = pack(v)
     for c, blocks in chunks():
         ready(c)
         for i in blocks:
-            out_ref[i] = dot3(d_ref[i], f_ref[i])
+            az = im_ref[i] - alpha * (adim_ref[i] + dot(q_ref[i], packed))
+            az_ref[i] = az
+            daz_ref[i] = dot3(d_ref[i], az)
         emit(0, c)
+        emit(1, c)
 
 
 def solve_rows(cell, inv, use):
@@ -242,8 +262,9 @@
         use(r, t[r] * (inv[r : r + 1] * OMEGA))
 
 
-def sweep_body(ready, emit, t_ref, diag_ref, out_ref, cell_ref):
-    inv = 1.0 / (4.0 + diag_ref[...])
+def sweep_body(ready, emit, t_ref, out_ref, cell_ref):
+    inv = 1.0 / (4.0 + t_ref[0, 2 * NB :, :])
+    out_ref[CROWS, :CROWS, :] = inv
     devs = t_ref.shape[0]
     for g in range(devs):
         cell_ref[g * NB : (g + 1) * NB] = t_ref[g, :NB]
@@ -261,7 +282,7 @@
         solve_rows(cell_ref[here, :], inv, use)
         return 0
 
-    lax.fori_loop(0, cell_ref.shape[0] // 8, chunk, 0, unroll=2)
+    lax.fori_loop(0, cell_ref.shape[0] // 8, chunk, 0, unroll=3)
     emit(0)
 
 
@@ -274,7 +295,7 @@
 
 
 def coarse_body(
-    ready, emit, rows_hbm, diag_ref, g_ref, part_ref, wh_ref, wl_ref, rows_ref, sh_ref, sl_ref, oh_ref, sem
+    ready, emit, rows_hbm, g_ref, part_ref, wh_ref, wl_ref, rows_ref, sh_ref, sl_ref, oh_ref, sem
 ):
     copy = pltpu.make_async_copy(rows_hbm, rows_ref, sem)
     copy.start()
@@ -289,8 +310,8 @@
             hit = jnp.where(cells[q : q + 1] == index, 1.0, 0.0)
             oh_ref[r * BLK : (r + 1) * BLK, q * BLK : (q + 1) * BLK] = hit.astype(BF16)
     place = lax.axis_index(GATHER)
-    before = g_ref[(place + devs - 1) % devs][NB + 1 : NB + 2]
-    after = g_ref[(place + 1) % devs][NB + 2 : NB + 3]
+    before = g_ref[(place + devs - 1) % devs][NB + 1 : NB + 2, :1]
+    after = g_ref[(place + 1) % devs][NB + 1 : NB + 2, BLK - 1 :]
     row = lax.broadcasted_iota(jnp.int32, (8, BLK), 0)
     outer = jnp.where(row == 0, before, jnp.where(row == 7, after, -1.0))
     copy.wait()
@@ -301,7 +322,7 @@
         rows_ref[r, base : base + 8, :] += jnp.where(row == 0, value, 0.0)
         rows_ref[r, size - 8 :, :] += jnp.where(row == 7, value, 0.0)
 
-    solve_rows(outer, 1.0 / (4.0 + diag_ref[...]), use)
+    solve_rows(outer, rows_ref[CROWS, :CROWS, :], use)
     for r in range(CROWS):
         here = slice(r * BLK, (r + 1) * BLK)
         high, low = split(rows_ref[r])
@@ -325,7 +346,7 @@
     wh = wh_ref[...]
     part = dot(wh, gh) + (dot(wh, gl) + dot(wl_ref[...], gh))
     sums = jnp.sum(g_ref[:, NB:, :], axis=0)
-    pad = jnp.zeros((ROWS - EXT - (MROWS - NB), BLK), F32)
+    pad = jnp.zeros((ROWS - DOTS - sums.shape[0], BLK), F32)
     spread(part, jnp.concatenate([sums, pad], axis=0), part_ref)
     emit(0)
 
@@ -427,51 +448,52 @@
     return jnp.concatenate([high, high, low, jnp.zeros((32, BLK), BF16)], axis=0)
 
 
+def fold_rows(x):
+    return jnp.sum(x.reshape(NB // 8, 8, BLK), axis=0)
+
+
 def fold(x):
     return jnp.sum(x.reshape(BLK // 8, 8, BLK), axis=0)
 
 
 def message(rows, dots):
     sums = [jnp.sum(d, axis=0, keepdims=True) for d in dots]
-    pad = [jnp.zeros((1, BLK), F32)] * (MROWS - NB - len(dots))
-    return jnp.concatenate(rows + sums + pad, axis=0)
-
-
-def first_body(ready, emit, got_ref, w_ref, r_ref, dr_ref, adr_ref, q_ref, msg_ref, u_ref, im_ref):
+    return jnp.concatenate(rows + sums, axis=0)
+
+
+def first_body(
+    ready, emit, got_ref, w_ref, rows_ref, dot_ref, dr_ref, adr_ref, q_ref, msg_ref, u_ref
+):
     u = jnp.sum(got_ref[...], axis=0)
     u_ref[...] = u
     emit(1)
     packed = pack(u)
     wt = w_ref[...].T
     rows = []
-    rz = jnp.zeros((8, BLK), F32)
+    rz = dot_ref[...] + fold_rows(rows_ref[:NB] * u[:NB])
     zw = jnp.zeros((8, BLK), F32)
     for c, blocks in chunks():
         ready(c)
         for i in blocks:
             col = wt[:, i : i + 1]
             image = adr_ref[i] + dot(q_ref[i], packed)
-            z = dr_ref[i] + col * u[i : i + 1]
-            im_ref[i] = image
             rows.append(jnp.sum(col * image, axis=0, keepdims=True))
-            rz = rz + fold(r_ref[i] * z)
-            zw = zw + fold(z * image)
-        emit(2, c)
+            zw = zw + fold((dr_ref[i] + col * u[i : i + 1]) * image)
     broadcast(msg_ref, message(rows, [rz, zw]))
     emit(0)
 
 
 def second_body(
-    ready, emit, got_ref, u_ref, w_ref, r_ref, im_ref, dr_ref, dim_ref, adr_ref, adim_ref, q_ref,
-    msg_ref, v_ref, az_ref,
+    ready, emit, got_ref, u_ref, w_ref, r_ref, im_ref, dr_ref, dim_ref, adim_ref, q_ref,
+    msg_ref, v_ref,
 ):
     v = jnp.sum(got_ref[...], axis=0)
     v_ref[...] = v
     emit(1)
     alpha = v[EXT : EXT + 1] / v[EXT + 1 : EXT + 2]
     u0 = u_ref[...]
-    u = u0 - alpha * v
-    packed = pack(u)
+    u1 = u0 - alpha * v
+    packed = pack(v)
     wt = w_ref[...].T
     rows = []
     rz = jnp.zeros((8, BLK), F32)
@@ -484,14 +506,12 @@
             image = im_ref[i]
             dr = dr_ref[i]
             z0 = dr + col * u0[i : i + 1]
-            z1 = dr - alpha * dim_ref[i] + col * u[i : i + 1]
-            az = adr_ref[i] - alpha * adim_ref[i] + dot(q_ref[i], packed)
-            az_ref[i] = az
+            z1 = dr - alpha * dim_ref[i] + col * u1[i : i + 1]
+            az = image - alpha * (adim_ref[i] + dot(q_ref[i], packed))
             rows.append(jnp.sum(col * az, axis=0, keepdims=True))
             rz = rz + fold((r_ref[i] - alpha * image) * z1)
             zaz = zaz + fold(z1 * az)
             cross = cross + fold(z1 * image + z0 * az)
-        emit(2, c)
     broadcast(msg_ref, message(rows, [rz, zaz, cross]))
     emit(0)
 
@@ -561,7 +581,7 @@
     return pl.pallas_call(
         functools.partial(operator_kernel, first),
         out_shape=outs,
-        in_specs=[hbm] * len(args),
+        in_specs=[hbm] * 3 + [pl.BlockSpec(memory_space=pl.ANY)] * 2 + [hbm] * (len(args) - 5),
         out_specs=[hbm] * len(outs),
         scratch_shapes=scratch,
         compiler_params=pltpu.CompilerParams(vmem_limit_bytes=BIG),
@@ -583,7 +603,10 @@
     cells = (coarse_map, "scalar")
     columns = columns.T
     weights = (restrict_weights, "whole")
-    msg_out = ((gathered, MROWS, BLK), F32, "whole")
+
+    def msg_out(extra):
+        return ((gathered, NB + extra, BLK), F32, "whole")
+
     part_shape = (scattered, ROWS, BLK)
     part_out = (part_shape, F32, "whole")
     short_out = (part_shape[1:], F32, "whole")
@@ -592,7 +615,7 @@
 
     (target,) = staged(
         target_body,
-        [send, cells],
+        [send, cells, (coarse_diag, "whole")],
         [((scattered, TROWS, BLK), F32, "whole")],
         moved=1 << 18,
     )
@@ -605,14 +628,14 @@
         moved=big,
     )
     (msg,) = staged(
-        open_body, [(start_rows, "vmem"), (targets, "vmem")], [msg_out], moved=1 << 18, limit=SMALL
+        open_body, [(start_rows, "vmem"), (targets, "vmem")], [msg_out(2)], moved=1 << 18, limit=SMALL
     )
     got = lax.all_to_all(msg, GATHER, 0, 0, tiled=True)
     packet = ((BLK + 8, BLK), F32, "vmem")
-    local, inner, outer = staged(
+    local, inner, outer, local_dot = staged(
         local_body,
         [send, weights, (loads, "field"), (inv_diag, "field")],
-        [field_out, packet, packet],
+        [field_out, packet, packet, ((8, BLK), F32, "whole")],
         flops=2 * 10**8,
         moved=big,
     )
@@ -621,14 +644,14 @@
     rows = scattered * EXT
     (coarse_rows,) = staged(
         sweep_body,
-        [(targets, "vmem"), (coarse_diag, "vmem")],
-        [((CROWS, rows, BLK), F32, "whole")],
+        [(targets, "vmem")],
+        [((CROWS + 1, rows, BLK), F32, "whole")],
         scratch=[pltpu.VMEM((rows, BLK), F32)],
         flops=10**8,
         moved=big,
         limit=SMALL,
     )
-    got, inner, outer = lax.optimization_barrier((got, inner, outer))
+    got, inner = lax.optimization_barrier((got, inner))
     image_local, coupling = apply_operator(
         stiffness, columns, local, inner, outer, restrict_weights
     )
@@ -636,10 +659,10 @@
     cells_all = CROWS * BLK
     part, wh, wl = staged(
         coarse_body,
-        [(coarse_rows, "hbm"), (coarse_diag, "vmem"), (got, "vmem")],
+        [(coarse_rows, "hbm"), (got, "vmem")],
         [part_out, weights_out, weights_out],
         scratch=[
-            pltpu.VMEM((CROWS, rows, BLK), F32),
+            pltpu.VMEM((CROWS + 1, rows, BLK), F32),
             pltpu.VMEM((rows, cells_all), BF16),
             pltpu.VMEM((rows, cells_all), BF16),
             pltpu.VMEM((cells_all, gathered * NB), BF16),
@@ -651,19 +674,19 @@
     )
     got = lax.all_to_all(part, SCATTER, 0, 0, tiled=True)
 
-    msg, u0, image0 = staged(
+    msg, u0 = staged(
         first_body,
-        [(got, "whole"), weights, (loads, "field"), (local, "field"), (image_local, "field"),
-         (coupling, "field")],
-        [msg_out, short_out, field_out],
+        [(got, "any"), weights, (start_rows, "whole"), (local_dot, "whole"), (local, "field"),
+         (image_local, "field"), (coupling, "field")],
+        [msg_out(2), short_out],
         flops=10**8,
         moved=big,
     )
     packet = ((BLK, BLK), F32, "vmem")
-    local_image, inner, outer = staged(
+    image0, local_image, inner, outer = staged(
         image_body,
-        [send, (image0, "field"), (inv_diag, "field")],
-        [field_out, packet, packet],
+        [send, (u0, "whole"), (image_local, "field"), (coupling, "field"), (inv_diag, "field")],
+        [field_out, field_out, packet, packet],
         flops=2 * 10**8,
         moved=big,
     )
@@ -671,9 +694,7 @@
     outer = lax.ppermute(outer, RING, swaps[1])
     (image_image,) = apply_operator(stiffness, columns, local_image, inner, outer)
 
-    def exchange(msg, ahead):
-        got = lax.all_to_all(msg, GATHER, 0, 0, tiled=True)
-        got, ahead = lax.optimization_barrier((got, ahead))
+    def exchange(got):
         (part,) = staged(
             apply_body,
             [(wh, "whole"), (wl, "whole"), (got, "vmem")],
@@ -682,30 +703,33 @@
             moved=big,
             limit=SMALL,
         )
-        return lax.all_to_all(part, SCATTER, 0, 0, tiled=True), ahead
-
-    got, local_image = exchange(msg, local_image)
-    msg, v0, image1 = staged(
+        return lax.all_to_all(part, SCATTER, 0, 0, tiled=True)
+
+    got = exchange(lax.all_to_all(msg, GATHER, 0, 0, tiled=True))
+    msg, v0 = staged(
         second_body,
-        [(got, "whole"), (u0, "whole"), weights, (loads, "field"), (image0, "field"),
-         (local, "field"), (local_image, "field"), (image_local, "field"),
-         (image_image, "field"), (coupling, "field")],
-        [msg_out, short_out, field_out],
+        [(got, "any"), (u0, "whole"), weights, (loads, "field"), (image0, "field"),
+         (local, "field"), (local_image, "field"), (image_image, "field"),
+         (coupling, "field")],
+        [msg_out(3), short_out],
         flops=10**8,
         moved=big,
     )
-    (local_image1,) = staged(
+    image1, local_image1 = staged(
         product_body,
-        [(image1, "field"), (inv_diag, "field")],
-        [field_out],
+        [(v0, "whole"), (image0, "field"), (image_image, "field"), (coupling, "field"),
+         (inv_diag, "field")],
+        [field_out] * 2,
         flops=2 * 10**8,
         moved=big,
     )
-    got, local_image1 = exchange(msg, local_image1)
+    got = lax.all_to_all(msg, GATHER, 0, 0, tiled=True)
+    got, local_image1 = lax.optimization_barrier((got, local_image1))
+    got = exchange(got)
     return tuple(
         staged(
             last_body,
-            [(got, "whole"), (u0, "whole"), (v0, "whole"), weights, (loads, "field"),
+            [(got, "any"), (u0, "whole"), (v0, "whole"), weights, (loads, "field"),
              (image0, "field"), (local, "field"), (local_image, "field"), (image1, "field"),
              (local_image1, "field")],
             [field_out] * 3,

time: 134 us -> 131 us (0.978)
  Pallas kernels: 47.2 us -> 49.1 us
  starting transfers between devices: 49.6 us -> 47.7 us
  local copies, waits for them, and re-layouts: 4.6 us -> 3.19 us
    all_to_all x3 -> x2, waiting for transfers between devices: 14.1 us -> 3.4 us  [the longest x1 3.39 us: on_device(): got = exchange(lax.all_to_all(msg, GATHER, 0, 0, tiled=True))]
    all_to_all x1 -> x2, waiting for transfers between devices: 1.34 us -> 10.2 us  [on_device(): got = lax.all_to_all(msg, GATHER, 0, 0, tiled=True)]
    all_to_all x3 -> x2, starting transfers between devices: 19.1 us -> 12.5 us  [the longest x1 7.22 us: exchange(): return lax.all_to_all(part, SCATTER, 0, 0, tiled=True)]
    all_to_all x1 -> x2, starting transfers between devices: 10.5 us -> 15.7 us  [on_device(): got = lax.all_to_all(msg, GATHER, 0, 0, tiled=True)]
    pallas_call x13, Pallas kernels: 36.1 us -> 38 us  [staged(): pl.pallas_call(kernel, out_shape=[jax.ShapeDtypeStruct(sh, dt) for sh, dt...]
    unnamed x18 -> x14, local copies, waits for them, and re-layouts: 4.6 us -> 3.19 us
  transfers between devices with their start and end apart: 10 -> 10, of which waited for: 4 -> 4; matrix products, arithmetic and copies ran while one was open for 0% -> 0% of each run, Pallas kernels for 21% -> 26%
where the time goes in v4:
time: 131 us; the launch traced here: 130 us
  Pallas kernels  49.1 us (37%)
  starting transfers between devices  47.7 us (36%)
  waiting for transfers between devices  17.3 us (13%)
  blocking collectives  12.2 us (9%)
  local copies, waits for them, and re-layouts  3.19 us (2%)
    pallas_call x13, Pallas kernels, staged(): pl.pallas_call(kernel, out_shape=[jax.ShapeDtypeStruct(sh, dt) for sh, dt...  38 us
    all_to_all x2, starting transfers between devices, on_device(): got = lax.all_to_all(msg, GATHER, 0, 0, tiled=True)  15.7 us
    all_to_all x1, blocking collectives, exchange(): return lax.all_to_all(part, SCATTER, 0, 0, tiled=True)  12.2 us
    pallas_call x2, Pallas kernels, apply_operator(): pl.pallas_call(functools.partial(operator_kernel, first), out_shape=outs,...  11.1 us
    all_to_all x2, waiting for transfers between devices, on_device(): got = lax.all_to_all(msg, GATHER, 0, 0, tiled=True)  10.2 us
    all_to_all x1, starting transfers between devices, exchange(): return lax.all_to_all(part, SCATTER, 0, 0, tiled=True)  7.22 us
    all_to_all x1, starting transfers between devices, on_device(): got = lax.all_to_all(part, SCATTER, 0, 0, tiled=True)  6.67 us
    all_to_all x1, starting transfers between devices, on_device(): targets = lax.all_to_all(target, SCATTER, 0, 0, tiled=True)  6.57 us
  transfers between devices with their start and end apart: 10, of which 4 were waited for; matrix products, arithmetic and copies ran while one was open for 0% of the time, Pallas kernels for 26%

profile of v4, /device:TPU:1, one launch (start us, length us, event | category | flops | bytes accessed | tf_op | source)
XLA Modules:
  0.0 130.5 jit_solution(17257039510099116302)
XLA Ops:
  0.6 1.5 %shard_map.103 = f32[8,48,128]{2,1,0:T(8,128)} custom-call(s32[1,2]{1,0:T(1,128)} %bitcast.2, s32[16]{0:T(128)} %refs_0_.1, f32[16,128]{1,0:T(8,128)} %refs_2_.4), custom_call_target="tpu_custom_call" | custom-call | bytes 262144 | tf_op jit(solution)/shard_map/pallas_call | solution.py:120
  2.1 6.6 %all-to-all-start = ((f32[8,48,128]{2,1,0:T(8,128)}), f32[8,48,128]{2,1,0:T(8,128)S(1)}, u32[]{:S(2)}, u32[]{:S(2)}) async-start(f32[8,48,128]{2,1,0:T(8,128)} %shard_map.103), calls=%async_computation | async-start | bytes 393216 | tf_op jit(solution)/shard_map/all_to_all | solution.py:622
  8.7 2.2 %shard_map.105.refs_0_.refs_2_ = f32[24,128]{1,0:T(8,128)} custom-call(s32[16]{0:T(128)} %refs_0_.1, f32[16,128]{1,0:T(8,128)} %refs_3_.5, f32[16,128,128]{2,1,0:T(8,128)} %refs_4_.5), custom_call_target="tpu_custom_call" | custom-call | flops 1000000 | bytes 2097152 | tf_op jit(solution)/shard_map/pallas_call | solution.py:120
  10.8 3.7 %all-to-all-done.refs_0_.refs_1_ = f32[8,48,128]{2,1,0:T(8,128)S(1)} async-done(((f32[8,48,128]{2,1,0:T(8,128)}), f32[8,48,128]{2,1,0:T(8,128)S(1)}, u32[]{:S(2)}, u32[]{:S(2)}) %all-to-all-start) | async-done | bytes 196640 | tf_op jit(solution)/shard_map/all_to_all | solution.py:622
  14.6 0.7 copy-done
  15.3 0.8 shard_map.106
  16.1 10.5 %all-to-all-start.1 = ((f32[32,18,128]{2,1,0:T(8,128)}), f32[32,18,128]{2,1,0:T(8,128)S(1)}, u32[]{:S(2)}, u32[]{:S(2)}) async-start(f32[32,18,128]{2,1,0:T(8,128)} %shard_map.106), calls=%async_computation.1 | async-start | bytes 786432 | tf_op jit(solution)/shard_map/all_to_all | solution.py:633
  26.5 3.6 %shard_map.107 = (f32[16,128,128]{2,1,0:T(8,128)}, f32[136,128]{1,0:T(8,128)}, f32[136,128]{1,0:T(8,128)}, f32[8,128]{1,0:T(8,128)}) custom-call(s32[1,2]{1,0:T(1,128)} %bitcast.3, f32[16,128]{1,0:T(8,128)} %refs_3_.5, f32[16,128,128]{2,1,0:T(8,128)} %refs_4_.5, f32[16,128,128]{2,1,0:T(8,128)} %refs_4_.4), custom_call_target="tpu_custom_call" | custom-call | flops 200000000 | bytes 2097152 | tf_op jit(solution)/shard_map/pallas_call | solution.py:120
  30.1 0.7 collective-permute-start
  30.8 1.5 %collective-permute-start.1 = (f32[136,128]{1,0:T(8,128)}, f32[136,128]{1,0:T(8,128)S(1)}, u32[]{:S(2)}, u32[]{:S(2)}) collective-permute-start(f32[136,128]{1,0:T(8,128)} %get-tuple-element.34), channel_id=1, source_target_pairs={{1,2},{3,4},{5,6},{7,8},{9,10},{11,12},{13,14},{15,16},{17,18},{19... | collective-permute-start | bytes 208904 | tf_op jit(solution)/shard_map/ppermute | solution.py:643
  32.3 3.7 %shard_map.104.refs_0_ = f32[17,144,128]{2,1,0:T(8,128)S(1)} custom-call(f32[8,48,128]{2,1,0:T(8,128)S(1)} %all-to-all-done.refs_0_.refs_1_), custom_call_target="tpu_custom_call" | custom-call | flops 100000000 | bytes 2097152 | tf_op jit(solution)/shard_map/pallas_call | solution.py:120
  36.0 2.3 %all-to-all-done.1.refs_1_ = f32[32,18,128]{2,1,0:T(8,128)S(1)} async-done(((f32[32,18,128]{2,1,0:T(8,128)}), f32[32,18,128]{2,1,0:T(8,128)S(1)}, u32[]{:S(2)}, u32[]{:S(2)}) %all-to-all-start.1) | async-done | bytes 294944 | tf_op jit(solution)/shard_map/all_to_all | solution.py:633
  38.3 3.5 %shard_map.108 = (f32[8,24,128]{2,1,0:T(8,128)}, bf16[144,512]{1,0:T(8,128)(2,1)S(1)}, bf16[144,512]{1,0:T(8,128)(2,1)S(1)}) custom-call(f32[17,144,128]{2,1,0:T(8,128)S(1)} %shard_map.104.refs_0_, f32[32,18,128]{2,1,0:T(8,128)S(1)} %all-to-all-done.1.refs_1_), custom_call_target="tpu_custom_call" | custom-call | flops 1000000000 | bytes 2097152 | tf_op jit(solution)/shard_map/pallas_call | solution.py:120
  41.8 6.7 %all-to-all-start.2 = ((f32[8,24,128]{2,1,0:T(8,128)}), f32[8,24,128]{2,1,0:T(8,128)S(1)}, u32[]{:S(2)}, u32[]{:S(2)}) async-start(f32[8,24,128]{2,1,0:T(8,128)} %get-tuple-element.30), calls=%async_computation.2 | async-start | bytes 196608 | tf_op jit(solution)/shard_map/all_to_all | solution.py:675
  49.1 6.1 %shard_map.109 = (f32[16,128,128]{2,1,0:T(8,128)}, bf16[16,128,128]{2,1,0:T(8,128)(2,1)}) custom-call(s32[6,16]{1,0:T(8,128)} %bitcast.5, f32[16,6,128,128]{3,2,1,0:T(8,128)} %s_hbm.3, f32[16,128,128]{2,1,0:T(8,128)} %get-tuple-element.32.f_hbm.refs_4_.refs_5_.refs_6_, f32[136,128]{1,0:T(8,128)} %copy-done.3, f32[136,128]{1,0:T(8,128)} %copy-done.4, ...), custom_call_target="tpu_custom_call" | custom-call | flops 6000000000 | bytes 8388608 | tf_op jit(solution)/shard_map/pallas_call | solution.py:581
  55.3 0.6 copy-done.1
  55.9 2.9 %shard_map.110 = (f32[32,18,128]{2,1,0:T(8,128)}, f32[24,128]{1,0:T(8,128)}) custom-call(f32[8,24,128]{2,1,0:T(8,128)} %copy-done.1, f32[16,128]{1,0:T(8,128)} %refs_3_.5, f32[24,128]{1,0:T(8,128)} %shard_map.105.refs_0_.refs_2_, f32[8,128]{1,0:T(8,128)} %get-tuple-element.31.refs_3_, f32[16,128,128]{2,1,0:T(8,128)} %get-tuple-element.32.f_hbm.refs_4_.refs_5_.refs_6_, ...), custom_call_target="tpu_custom_call" | custom-call | flops 100000000 | bytes 2097152 | tf_op jit(solution)/shard_map/pallas_call | solution.py:120
  58.8 5.2 %all-to-all-start.3 = ((f32[32,18,128]{2,1,0:T(8,128)}), f32[32,18,128]{2,1,0:T(8,128)S(1)}, u32[]{:S(2)}, u32[]{:S(2)}) async-start(f32[32,18,128]{2,1,0:T(8,128)} %get-tuple-element.37), calls=%async_computation.3 | async-start | bytes 786432 | tf_op jit(solution)/shard_map/all_to_all | solution.py:708
  64.0 4.8 %shard_map.112 = (f32[16,128,128]{2,1,0:T(8,128)}, f32[16,128,128]{2,1,0:T(8,128)}, f32[128,128]{1,0:T(8,128)}, f32[128,128]{1,0:T(8,128)}) custom-call(s32[1,2]{1,0:T(1,128)} %bitcast.4, f32[24,128]{1,0:T(8,128)} %get-tuple-element.38.refs_1_, f32[16,128,128]{2,1,0:T(8,128)} %get-tuple-element.35.refs_5_.refs_2_, ...), custom_call_target="tpu_custom_call" | custom-call | flops 200000000 | bytes 2097152 | tf_op jit(solution)/shard_map/pallas_call | solution.py:120
  68.9 1.4 %collective-permute-start.2 = (f32[128,128]{1,0:T(8,128)}, f32[128,128]{1,0:T(8,128)S(1)}, u32[]{:S(2)}, u32[]{:S(2)}) collective-permute-start(f32[128,128]{1,0:T(8,128)} %get-tuple-element.41), channel_id=1, source_target_pairs={{0,1},{2,3},{4,5},{6,7},{8,9},{10,11},{12,13},{14,15},{16,17},{18,... | collective-permute-start | bytes 196616 | tf_op jit(solution)/shard_map/ppermute | solution.py:693
  70.3 2.6 %collective-permute-start.3 = (f32[128,128]{1,0:T(8,128)}, f32[128,128]{1,0:T(8,128)S(1)}, u32[]{:S(2)}, u32[]{:S(2)}) collective-permute-start(f32[128,128]{1,0:T(8,128)} %get-tuple-element.42), channel_id=1, source_target_pairs={{1,2},{3,4},{5,6},{7,8},{9,10},{11,12},{13,14},{15,16},{17,18},{19... | collective-permute-start | bytes 196616 | tf_op jit(solution)/shard_map/ppermute | solution.py:694
  72.9 3.4 %all-to-all-done.3.refs_2_ = f32[32,18,128]{2,1,0:T(8,128)S(1)} async-done(((f32[32,18,128]{2,1,0:T(8,128)}), f32[32,18,128]{2,1,0:T(8,128)S(1)}, u32[]{:S(2)}, u32[]{:S(2)}) %all-to-all-start.3) | async-done | bytes 294944 | tf_op jit(solution)/shard_map/all_to_all | solution.py:708
  76.3 1.3 %shard_map.111 = f32[8,24,128]{2,1,0:T(8,128)} custom-call(bf16[144,512]{1,0:T(8,128)(2,1)S(1)} %get-tuple-element.28.refs_0_, bf16[144,512]{1,0:T(8,128)(2,1)S(1)} %get-tuple-element.29.refs_1_, f32[32,18,128]{2,1,0:T(8,128)S(1)} %all-to-all-done.3.refs_2_), custom_call_target="tpu_custom_call" | custom-call | flops 100000000 | bytes 2097152 | tf_op jit(solution)/shard_map/pallas_call | solution.py:120
  77.7 7.2 %all-to-all-start.4 = ((f32[8,24,128]{2,1,0:T(8,128)}), f32[8,24,128]{2,1,0:T(8,128)S(1)}, u32[]{:S(2)}, u32[]{:S(2)}) async-start(f32[8,24,128]{2,1,0:T(8,128)} %shard_map.111), calls=%async_computation.4 | async-start | bytes 196608 | tf_op jit(solution)/shard_map/all_to_all | solution.py:706
  85.5 4.9 %shard_map.113.refs_7_.refs_2_ = f32[16,128,128]{2,1,0:T(8,128)} custom-call(s32[6,16]{1,0:T(8,128)} %bitcast.6, f32[16,6,128,128]{3,2,1,0:T(8,128)} %s_hbm.3, f32[16,128,128]{2,1,0:T(8,128)} %get-tuple-element.40.f_hbm.refs_6_.refs_7_, f32[128,128]{1,0:T(8,128)} %copy-done.5, f32[128,128]{1,0:T(8,128)} %copy-done.6), custom_call_target="tpu_custom_call" | custom-call | flops 6000000000 | bytes 8388608 | tf_op jit(solution)/shard_map/pallas_call | solution.py:581
  91.1 4.1 %shard_map.114 = (f32[32,19,128]{2,1,0:T(8,128)}, f32[24,128]{1,0:T(8,128)}) custom-call(f32[8,24,128]{2,1,0:T(8,128)} %copy-done.2, f32[24,128]{1,0:T(8,128)} %get-tuple-element.38.refs_1_, f32[16,128]{1,0:T(8,128)} %refs_3_.5, f32[16,128,128]{2,1,0:T(8,128)} %refs_4_.5, f32[16,128,128]{2,1,0:T(8,128)} %get-tuple-element.39.refs_4_.refs_1_.refs_5_, ...), custom_call_target="tpu_custom_call" | custom-call | flops 100000000 | bytes 2097152 | tf_op jit(solution)/shard_map/pallas_call | solution.py:120
  95.2 5.3 %all-to-all-start.5 = ((f32[32,19,128]{2,1,0:T(8,128)}), f32[32,19,128]{2,1,0:T(8,128)S(1)}, u32[]{:S(2)}, u32[]{:S(2)}) async-start(f32[32,19,128]{2,1,0:T(8,128)} %get-tuple-element.43), calls=%async_computation.5 | async-start | bytes 786432 | tf_op jit(solution)/shard_map/all_to_all | solution.py:726
  100.5 4.3 %shard_map.115 = (f32[16,128,128]{2,1,0:T(8,128)}, f32[16,128,128]{2,1,0:T(8,128)}) custom-call(f32[24,128]{1,0:T(8,128)} %get-tuple-element.44.refs_0_.refs_2_, f32[16,128,128]{2,1,0:T(8,128)} %get-tuple-element.39.refs_4_.refs_1_.refs_5_, f32[16,128,128]{2,1,0:T(8,128)} %shard_map.113.refs_7_.refs_2_, ...), custom_call_target="tpu_custom_call" | custom-call | flops 200000000 | bytes 2097152 | tf_op jit(solution)/shard_map/pallas_call | solution.py:120
  104.8 7.9 %all-to-all-done.5.refs_2_ = f32[32,19,128]{2,1,0:T(8,128)S(1)} async-done(((f32[32,19,128]{2,1,0:T(8,128)}), f32[32,19,128]{2,1,0:T(8,128)S(1)}, u32[]{:S(2)}, u32[]{:S(2)}) %all-to-all-start.5) | async-done | bytes 311328 | tf_op jit(solution)/shard_map/all_to_all | solution.py:726
  112.7 0.8 shard_map.116
  113.5 12.2 %all_to_all.35.refs_0_ = f32[8,24,128]{2,1,0:T(8,128)} all-to-all(f32[8,24,128]{2,1,0:T(8,128)S(1)} %shard_map.116), channel_id=1, replica_groups=mesh['y'=4,'z'=8,'core'=2,'crs'=4] {'core','crs'}, dimensions={0} | all-to-all | bytes 196608 | tf_op jit(solution)/shard_map/all_to_all | solution.py:706
  125.7 4.6 %shard_map.117 = (f32[16,128,128]{2,1,0:T(8,128)}, f32[16,128,128]{2,1,0:T(8,128)}, f32[16,128,128]{2,1,0:T(8,128)}) custom-call(f32[8,24,128]{2,1,0:T(8,128)} %all_to_all.35.refs_0_, f32[24,128]{1,0:T(8,128)} %get-tuple-element.38.refs_1_, f32[24,128]{1,0:T(8,128)} %get-tuple-element.44.refs_0_.refs_2_, f32[16,128]{1,0:T(8,128)} %refs_3_.5, ...), custom_call_target="tpu_custom_call" | custom-call | flops 100000000 | bytes 2097152 | tf_op jit(solution)/shard_map/pallas_call | solution.py:120
  (18 shorter events, 1.9 us)
Async XLA Ops:
  2.1 12.5 %all-to-all-start = ((f32[8,48,128]{2,1,0:T(8,128)}), f32[8,48,128]{2,1,0:T(8,128)S(1)}, u32[]{:S(2)}, u32[]{:S(2)}) async-start(f32[8,48,128]{2,1,0:T(8,128)} %shard_map.103), calls=%async_computation | async-start | bytes 393216 | tf_op jit(solution)/shard_map/all_to_all | solution.py:622
  14.6 0.7 copy-start
  16.1 22.2 %all-to-all-start.1 = ((f32[32,18,128]{2,1,0:T(8,128)}), f32[32,18,128]{2,1,0:T(8,128)S(1)}, u32[]{:S(2)}, u32[]{:S(2)}) async-start(f32[32,18,128]{2,1,0:T(8,128)} %shard_map.106), calls=%async_computation.1 | async-start | bytes 786432 | tf_op jit(solution)/shard_map/all_to_all | solution.py:633
  30.1 5.9 %collective-permute-start = (f32[136,128]{1,0:T(8,128)}, f32[136,128]{1,0:T(8,128)S(1)}, u32[]{:S(2)}, u32[]{:S(2)}) collective-permute-start(f32[136,128]{1,0:T(8,128)} %get-tuple-element.26), channel_id=1, source_target_pairs={{0,1},{2,3},{4,5},{6,7},{8,9},{10,11},{12,13},{14,15},{16,17},{18,... | collective-permute-start | bytes 208904 | tf_op jit(solution)/shard_map/ppermute | solution.py:642
  30.8 17.7 %collective-permute-start.1 = (f32[136,128]{1,0:T(8,128)}, f32[136,128]{1,0:T(8,128)S(1)}, u32[]{:S(2)}, u32[]{:S(2)}) collective-permute-start(f32[136,128]{1,0:T(8,128)} %get-tuple-element.34), channel_id=1, source_target_pairs={{1,2},{3,4},{5,6},{7,8},{9,10},{11,12},{13,14},{15,16},{17,18},{19... | collective-permute-start | bytes 208904 | tf_op jit(solution)/shard_map/ppermute | solution.py:643
  36.0 12.5 %copy-start.3 = (f32[136,128]{1,0:T(8,128)}, f32[136,128]{1,0:T(8,128)S(1)}, u32[]{:S(2)}) copy-start(f32[136,128]{1,0:T(8,128)S(1)} %collective-permute-done.inner_hbm) | copy-start | bytes 208900
  41.8 13.4 %all-to-all-start.2 = ((f32[8,24,128]{2,1,0:T(8,128)}), f32[8,24,128]{2,1,0:T(8,128)S(1)}, u32[]{:S(2)}, u32[]{:S(2)}) async-start(f32[8,24,128]{2,1,0:T(8,128)} %get-tuple-element.30), calls=%async_computation.2 | async-start | bytes 196608 | tf_op jit(solution)/shard_map/all_to_all | solution.py:675
  48.5 0.6 copy-start.4
  55.2 0.6 copy-start.1
  58.8 17.5 %all-to-all-start.3 = ((f32[32,18,128]{2,1,0:T(8,128)}), f32[32,18,128]{2,1,0:T(8,128)S(1)}, u32[]{:S(2)}, u32[]{:S(2)}) async-start(f32[32,18,128]{2,1,0:T(8,128)} %get-tuple-element.37), calls=%async_computation.3 | async-start | bytes 786432 | tf_op jit(solution)/shard_map/all_to_all | solution.py:708
  68.9 16.0 %collective-permute-start.2 = (f32[128,128]{1,0:T(8,128)}, f32[128,128]{1,0:T(8,128)S(1)}, u32[]{:S(2)}, u32[]{:S(2)}) collective-permute-start(f32[128,128]{1,0:T(8,128)} %get-tuple-element.41), channel_id=1, source_target_pairs={{0,1},{2,3},{4,5},{6,7},{8,9},{10,11},{12,13},{14,15},{16,17},{18,... | collective-permute-start | bytes 196616 | tf_op jit(solution)/shard_map/ppermute | solution.py:693
  70.3 14.6 %collective-permute-start.3 = (f32[128,128]{1,0:T(8,128)}, f32[128,128]{1,0:T(8,128)S(1)}, u32[]{:S(2)}, u32[]{:S(2)}) collective-permute-start(f32[128,128]{1,0:T(8,128)} %get-tuple-element.42), channel_id=1, source_target_pairs={{1,2},{3,4},{5,6},{7,8},{9,10},{11,12},{13,14},{15,16},{17,18},{19... | collective-permute-start | bytes 196616 | tf_op jit(solution)/shard_map/ppermute | solution.py:694
  77.7 12.8 %all-to-all-start.4 = ((f32[8,24,128]{2,1,0:T(8,128)}), f32[8,24,128]{2,1,0:T(8,128)S(1)}, u32[]{:S(2)}, u32[]{:S(2)}) async-start(f32[8,24,128]{2,1,0:T(8,128)} %shard_map.111), calls=%async_computation.4 | async-start | bytes 196608 | tf_op jit(solution)/shard_map/all_to_all | solution.py:706
  84.9 0.6 copy-start.5
  84.9 0.6 copy-start.6
  90.5 0.6 copy-start.2
  95.2 17.5 %all-to-all-start.5 = ((f32[32,19,128]{2,1,0:T(8,128)}), f32[32,19,128]{2,1,0:T(8,128)S(1)}, u32[]{:S(2)}, u32[]{:S(2)}) async-start(f32[32,19,128]{2,1,0:T(8,128)} %get-tuple-element.43), calls=%async_computation.5 | async-start | bytes 786432 | tf_op jit(solution)/shard_map/all_to_all | solution.py:726

commit v5 on v4

--- a/solution.py
+++ b/solution.py
@@ -23,7 +23,7 @@
 BF16 = jnp.bfloat16
 BIG = 60 * 1024 * 1024
 SMALL = 12 * 1024 * 1024
-TROWS = 48
+TROWS = 24
 GROUP = 4
 CHUNK = 8
 
@@ -130,9 +130,11 @@
     )(*[a for a, _ in ins])
 
 
-def column_cells(map_ref):
-    rows = [jnp.full((1, BLK), map_ref[i], jnp.int32) for i in range(NB)]
-    return jnp.concatenate(rows, axis=0).astype(F32)
+def cell_row(map_ref, lane):
+    cells = jnp.zeros(lane.shape, jnp.int32)
+    for i in range(NB):
+        cells = jnp.where(lane % NB == i, map_ref[i], cells)
+    return cells
 
 
 def broadcast(msg_ref, rows):
@@ -147,9 +149,7 @@
 def start_body(ready, emit, map_ref, w_ref, r_ref, rows_ref):
     wt = w_ref[...].T
     lane = lax.broadcasted_iota(jnp.int32, (1, BLK), 1)
-    cells = jnp.zeros((1, BLK), jnp.int32)
-    for i in range(NB):
-        cells = jnp.where(lane % NB == i, map_ref[i], cells)
+    cells = cell_row(map_ref, lane)
     mine = lane // NB == lax.axis_index(GATHER) % 8
     cells = jnp.where(mine, cells, 0).astype(F32)
     rows = []
@@ -160,13 +160,16 @@
 
 
 def group_ghosts(t_ref):
-    return jnp.sum(t_ref[:, NB : 2 * NB, :], axis=0)
+    row = t_ref[0, 1:2]
+    for g in range(1, t_ref.shape[0]):
+        row = row + t_ref[g, 1:2]
+    return row
 
 
 def open_body(ready, emit, rows_ref, t_ref, msg_ref):
     ghosts = group_ghosts(t_ref)
     lane = lax.broadcasted_iota(jnp.int32, (1, BLK), 1)
-    ends = jnp.where(lane < BLK // 2, ghosts[:1], ghosts[NB - 1 :])
+    ends = jnp.where(lane < BLK // 2, ghosts[:, :1], ghosts[:, NB - 1 : NB])
     rows = jnp.concatenate([rows_ref[: NB + 1], ends], axis=0)
     broadcast(msg_ref, rows)
     emit(0)
@@ -198,16 +201,13 @@
 def target_body(ready, emit, send_ref, map_ref, diag_ref, out_ref):
     slots = 2 * out_ref.shape[0]
     place = lax.axis_index(SCATTER)
-    row = lax.broadcasted_iota(jnp.int32, (slots, BLK), 0)
-    to_next = jnp.full((slots, BLK), map_ref[send_ref[0, 1]], jnp.int32)
-    to_prev = jnp.full((slots, BLK), map_ref[send_ref[0, 0]], jnp.int32)
-    ghosts = jnp.where(row == (2 * place + 2) % slots, to_next, 0)
-    ghosts = jnp.where(row == (2 * place + slots - 1) % slots, to_prev, ghosts).astype(F32)
-    own = column_cells(map_ref)
+    lane = lax.broadcasted_iota(jnp.int32, (1, BLK), 1)
+    ghosts = jnp.where(lane == (2 * place + 2) % slots, map_ref[send_ref[0, 1]], 0)
+    ghosts = jnp.where(lane == (2 * place + slots - 1) % slots, map_ref[send_ref[0, 0]], ghosts)
+    cells = [cell_row(map_ref, lane), ghosts, jnp.zeros((6, BLK), jnp.int32)]
+    block = jnp.concatenate([jnp.concatenate(cells, axis=0).astype(F32), diag_ref[...]], axis=0)
     for a in range(out_ref.shape[0]):
-        out_ref[a, :NB] = own
-        out_ref[a, NB : 2 * NB] = ghosts
-        out_ref[a, 2 * NB :] = diag_ref[...]
+        out_ref[a] = block
     emit(0)
 
 
@@ -262,27 +262,34 @@
         use(r, t[r] * (inv[r : r + 1] * OMEGA))
 
 
-def sweep_body(ready, emit, t_ref, out_ref, cell_ref):
-    inv = 1.0 / (4.0 + t_ref[0, 2 * NB :, :])
-    out_ref[CROWS, :CROWS, :] = inv
+def sweep_body(ready, emit, t_ref, out_ref, inv_ref, cell_ref, rows_ref):
+    inv = 1.0 / (4.0 + t_ref[0, 8:, :])
+    inv_ref[...] = inv
+    emit(1)
     devs = t_ref.shape[0]
+    own = jnp.concatenate([t_ref[g, :1] for g in range(devs)], axis=0).T
     for g in range(devs):
-        cell_ref[g * NB : (g + 1) * NB] = t_ref[g, :NB]
+        cell_ref[g * NB : (g + 1) * NB] = jnp.broadcast_to(own[:NB, g : g + 1], (NB, BLK))
     slots = 2 * devs
+    ghosts = jnp.broadcast_to(group_ghosts(t_ref), (8, BLK)).T[:slots, :1]
     row = lax.broadcasted_iota(jnp.int32, (slots, BLK), 0)
     inner = (row > 0) & (row < slots - 1)
-    cell_ref[devs * NB :] = jnp.where(inner, group_ghosts(t_ref), -1.0)
+    cell_ref[devs * NB :] = jnp.where(inner, ghosts, -1.0)
 
     def chunk(c, _):
         here = pl.ds(pl.multiple_of(c * 8, 8), 8)
 
         def use(r, value):
-            out_ref[r, here, :] = value
+            rows_ref[r, here, :] = value
 
         solve_rows(cell_ref[here, :], inv, use)
         return 0
 
-    lax.fori_loop(0, cell_ref.shape[0] // 8, chunk, 0, unroll=3)
+    size = cell_ref.shape[0]
+    lax.fori_loop(0, size // 8, chunk, 0, unroll=3)
+    for r in range(CROWS):
+        here = slice(r * BLK, (r + 1) * BLK)
+        out_ref[:size, here], out_ref[size:, here] = split(rows_ref[r])
     emit(0)
 
 
@@ -295,10 +302,14 @@
 
 
 def coarse_body(
-    ready, emit, rows_hbm, g_ref, part_ref, wh_ref, wl_ref, rows_ref, sh_ref, sl_ref, oh_ref, sem
+    ready, emit, rows_hbm, inv_hbm, g_ref, part_ref, wh_ref, wl_ref, s_ref, inv_ref, oh_ref, sem
 ):
-    copy = pltpu.make_async_copy(rows_hbm, rows_ref, sem)
-    copy.start()
+    copies = [
+        pltpu.make_async_copy(inv_hbm, inv_ref, sem.at[0]),
+        pltpu.make_async_copy(rows_hbm, s_ref, sem.at[1]),
+    ]
+    for copy in copies:
+        copy.start()
     devs = g_ref.shape[0]
     sources = devs * NB
     cells = g_ref[:, NB : NB + 1, :].reshape(devs, BLK)
@@ -314,21 +325,19 @@
     after = g_ref[(place + 1) % devs][NB + 1 : NB + 2, BLK - 1 :]
     row = lax.broadcasted_iota(jnp.int32, (8, BLK), 0)
     outer = jnp.where(row == 0, before, jnp.where(row == 7, after, -1.0))
-    copy.wait()
-    size = rows_ref.shape[1]
-    base = size - NB
+    for copy in copies:
+        copy.wait()
+    size = s_ref.shape[0] // 2
 
     def use(r, value):
-        rows_ref[r, base : base + 8, :] += jnp.where(row == 0, value, 0.0)
-        rows_ref[r, size - 8 :, :] += jnp.where(row == 7, value, 0.0)
-
-    solve_rows(outer, rows_ref[CROWS, :CROWS, :], use)
-    for r in range(CROWS):
+        ends = jnp.concatenate([jnp.where(row == 0, value, 0.0), jnp.where(row == 7, value, 0.0)], axis=0)
         here = slice(r * BLK, (r + 1) * BLK)
-        high, low = split(rows_ref[r])
-        sh_ref[:, here] = high
-        sl_ref[:, here] = low
-    w = dot(sh_ref[...], oh_ref[...]) + dot(sl_ref[...], oh_ref[...])
+        for start, piece in zip((size - NB, 2 * size - NB), split(ends)):
+            s_ref[start : start + NB, here] += piece
+
+    solve_rows(outer, inv_ref[...], use)
+    w = dot(s_ref[...], oh_ref[...])
+    w = w[:size] + w[size:]
     wh, wl = split(w)
     wh_ref[...] = wh
     wl_ref[...] = wl
@@ -642,11 +651,11 @@
     inner = lax.ppermute(inner, RING, swaps[0])
     outer = lax.ppermute(outer, RING, swaps[1])
     rows = scattered * EXT
-    (coarse_rows,) = staged(
+    coarse_rows, coarse_inv = staged(
         sweep_body,
         [(targets, "vmem")],
-        [((CROWS + 1, rows, BLK), F32, "whole")],
-        scratch=[pltpu.VMEM((rows, BLK), F32)],
+        [((2 * rows, CROWS * BLK), BF16, "whole"), ((CROWS, BLK), F32, "whole")],
+        scratch=[pltpu.VMEM((rows, BLK), F32), pltpu.VMEM((CROWS, rows, BLK), F32)],
         flops=10**8,
         moved=big,
         limit=SMALL,
@@ -659,14 +668,13 @@
     cells_all = CROWS * BLK
     part, wh, wl = staged(
         coarse_body,
-        [(coarse_rows, "hbm"), (got, "vmem")],
+        [(coarse_rows, "hbm"), (coarse_inv, "hbm"), (got, "vmem")],
         [part_out, weights_out, weights_out],
         scratch=[
-            pltpu.VMEM((CROWS + 1, rows, BLK), F32),
-            pltpu.VMEM((rows, cells_all), BF16),
-            pltpu.VMEM((rows, cells_all), BF16),
+            pltpu.VMEM((2 * rows, cells_all), BF16),
+            pltpu.VMEM((CROWS, BLK), F32),
             pltpu.VMEM((cells_all, gathered * NB), BF16),
-            pltpu.SemaphoreType.DMA(()),
+            pltpu.SemaphoreType.DMA((2,)),
         ],
         flops=10**9,
         moved=big,

time: 131 us -> 131 us (level)
  transfers between devices with their start and end apart: 10 -> 10, of which waited for: 4 -> 4; matrix products, arithmetic and copies ran while one was open for 0% -> 0% of each run, Pallas kernels for 26% -> 27%
where the time goes in v5:
time: 131 us; the launch traced here: 129 us
  Pallas kernels  49.2 us (38%)
  starting transfers between devices  47.6 us (36%)
  waiting for transfers between devices  16.1 us (12%)
  blocking collectives  12.2 us (9%)
  local copies, waits for them, and re-layouts  3.2 us (2%)
    pallas_call x13, Pallas kernels, staged(): pl.pallas_call(kernel, out_shape=[jax.ShapeDtypeStruct(sh, dt) for sh, dt...  38.2 us
    all_to_all x2, starting transfers between devices, on_device(): got = lax.all_to_all(msg, GATHER, 0, 0, tiled=True)  15.8 us
    all_to_all x1, blocking collectives, exchange(): return lax.all_to_all(part, SCATTER, 0, 0, tiled=True)  12.2 us
    pallas_call x2, Pallas kernels, apply_operator(): pl.pallas_call(functools.partial(operator_kernel, first), out_shape=outs,...  11.1 us
    all_to_all x2, waiting for transfers between devices, on_device(): got = lax.all_to_all(msg, GATHER, 0, 0, tiled=True)  9.86 us
    all_to_all x1, starting transfers between devices, exchange(): return lax.all_to_all(part, SCATTER, 0, 0, tiled=True)  7.22 us
    all_to_all x1, starting transfers between devices, on_device(): got = lax.all_to_all(part, SCATTER, 0, 0, tiled=True)  6.7 us
    all_to_all x1, starting transfers between devices, on_device(): targets = lax.all_to_all(target, SCATTER, 0, 0, tiled=True)  6.54 us
  transfers between devices with their start and end apart: 10, of which 4 were waited for; matrix products, arithmetic and copies ran while one was open for 0% of the time, Pallas kernels for 27%

profile of v5, /device:TPU:1, one launch (start us, length us, event | category | flops | bytes accessed | tf_op | source)
XLA Modules:
  0.0 129.4 jit_solution(258080176436308076)
XLA Ops:
  0.6 1.4 %shard_map.103 = f32[8,24,128]{2,1,0:T(8,128)} custom-call(s32[1,2]{1,0:T(1,128)} %bitcast.2, s32[16]{0:T(128)} %refs_0_.1, f32[16,128]{1,0:T(8,128)} %refs_2_.4), custom_call_target="tpu_custom_call" | custom-call | bytes 262144 | tf_op jit(solution)/shard_map/pallas_call | solution.py:120
  2.1 6.5 %all-to-all-start = ((f32[8,24,128]{2,1,0:T(8,128)}), f32[8,24,128]{2,1,0:T(8,128)S(1)}, u32[]{:S(2)}, u32[]{:S(2)}) async-start(f32[8,24,128]{2,1,0:T(8,128)} %shard_map.103), calls=%async_computation | async-start | bytes 196608 | tf_op jit(solution)/shard_map/all_to_all | solution.py:631
  8.6 2.2 %shard_map.105.refs_0_.refs_2_ = f32[24,128]{1,0:T(8,128)} custom-call(s32[16]{0:T(128)} %refs_0_.1, f32[16,128]{1,0:T(8,128)} %refs_3_.5, f32[16,128,128]{2,1,0:T(8,128)} %refs_4_.5), custom_call_target="tpu_custom_call" | custom-call | flops 1000000 | bytes 2097152 | tf_op jit(solution)/shard_map/pallas_call | solution.py:120
  10.8 2.8 %all-to-all-done.refs_0_.refs_1_ = f32[8,24,128]{2,1,0:T(8,128)S(1)} async-done(((f32[8,24,128]{2,1,0:T(8,128)}), f32[8,24,128]{2,1,0:T(8,128)S(1)}, u32[]{:S(2)}, u32[]{:S(2)}) %all-to-all-start) | async-done | bytes 98336 | tf_op jit(solution)/shard_map/all_to_all | solution.py:631
  13.6 0.7 copy-done
  14.3 0.9 shard_map.106
  15.2 10.5 %all-to-all-start.1 = ((f32[32,18,128]{2,1,0:T(8,128)}), f32[32,18,128]{2,1,0:T(8,128)S(1)}, u32[]{:S(2)}, u32[]{:S(2)}) async-start(f32[32,18,128]{2,1,0:T(8,128)} %shard_map.106), calls=%async_computation.1 | async-start | bytes 786432 | tf_op jit(solution)/shard_map/all_to_all | solution.py:642
  25.7 3.5 %shard_map.107 = (f32[16,128,128]{2,1,0:T(8,128)}, f32[136,128]{1,0:T(8,128)}, f32[136,128]{1,0:T(8,128)}, f32[8,128]{1,0:T(8,128)}) custom-call(s32[1,2]{1,0:T(1,128)} %bitcast.3, f32[16,128]{1,0:T(8,128)} %refs_3_.5, f32[16,128,128]{2,1,0:T(8,128)} %refs_4_.5, f32[16,128,128]{2,1,0:T(8,128)} %refs_4_.4), custom_call_target="tpu_custom_call" | custom-call | flops 200000000 | bytes 2097152 | tf_op jit(solution)/shard_map/pallas_call | solution.py:120
  29.2 0.6 collective-permute-start
  29.9 1.5 %collective-permute-start.1 = (f32[136,128]{1,0:T(8,128)}, f32[136,128]{1,0:T(8,128)S(1)}, u32[]{:S(2)}, u32[]{:S(2)}) collective-permute-start(f32[136,128]{1,0:T(8,128)} %get-tuple-element.38), channel_id=1, source_target_pairs={{1,2},{3,4},{5,6},{7,8},{9,10},{11,12},{13,14},{15,16},{17,18},{19... | collective-permute-start | bytes 208904 | tf_op jit(solution)/shard_map/ppermute | solution.py:652
  31.3 4.0 %shard_map.104 = (bf16[288,2048]{1,0:T(8,128)(2,1)S(1)}, f32[16,128]{1,0:T(8,128)S(1)}) custom-call(f32[8,24,128]{2,1,0:T(8,128)S(1)} %all-to-all-done.refs_0_.refs_1_), custom_call_target="tpu_custom_call" | custom-call | flops 100000000 | bytes 2097152 | tf_op jit(solution)/shard_map/pallas_call | solution.py:120
  35.4 2.0 %all-to-all-done.1.refs_2_ = f32[32,18,128]{2,1,0:T(8,128)S(1)} async-done(((f32[32,18,128]{2,1,0:T(8,128)}), f32[32,18,128]{2,1,0:T(8,128)S(1)}, u32[]{:S(2)}, u32[]{:S(2)}) %all-to-all-start.1) | async-done | bytes 294944 | tf_op jit(solution)/shard_map/all_to_all | solution.py:642
  37.4 3.3 %shard_map.108 = (f32[8,24,128]{2,1,0:T(8,128)}, bf16[144,512]{1,0:T(8,128)(2,1)S(1)}, bf16[144,512]{1,0:T(8,128)(2,1)S(1)}) custom-call(bf16[288,2048]{1,0:T(8,128)(2,1)S(1)} %get-tuple-element.28.refs_0_, f32[16,128]{1,0:T(8,128)S(1)} %get-tuple-element.29.refs_1_, f32[32,18,128]{2,1,0:T(8,128)S(1)} %all-to-all-done.1.refs_2_), custom_call_target="tpu_custom_call" | custom-call | flops 1000000000 | bytes 2097152 | tf_op jit(solution)/shard_map/pallas_call | solution.py:120
  40.7 6.7 %all-to-all-start.2 = ((f32[8,24,128]{2,1,0:T(8,128)}), f32[8,24,128]{2,1,0:T(8,128)S(1)}, u32[]{:S(2)}, u32[]{:S(2)}) async-start(f32[8,24,128]{2,1,0:T(8,128)} %get-tuple-element.34), calls=%async_computation.2 | async-start | bytes 196608 | tf_op jit(solution)/shard_map/all_to_all | solution.py:683
  48.0 6.1 %shard_map.109 = (f32[16,128,128]{2,1,0:T(8,128)}, bf16[16,128,128]{2,1,0:T(8,128)(2,1)}) custom-call(s32[6,16]{1,0:T(8,128)} %bitcast.5, f32[16,6,128,128]{3,2,1,0:T(8,128)} %s_hbm.3, f32[16,128,128]{2,1,0:T(8,128)} %get-tuple-element.36.f_hbm.refs_4_.refs_5_.refs_6_, f32[136,128]{1,0:T(8,128)} %copy-done.3, f32[136,128]{1,0:T(8,128)} %copy-done.4, ...), custom_call_target="tpu_custom_call" | custom-call | flops 6000000000 | bytes 8388608 | tf_op jit(solution)/shard_map/pallas_call | solution.py:590
  54.8 2.9 %shard_map.110 = (f32[32,18,128]{2,1,0:T(8,128)}, f32[24,128]{1,0:T(8,128)}) custom-call(f32[8,24,128]{2,1,0:T(8,128)} %copy-done.1, f32[16,128]{1,0:T(8,128)} %refs_3_.5, f32[24,128]{1,0:T(8,128)} %shard_map.105.refs_0_.refs_2_, f32[8,128]{1,0:T(8,128)} %get-tuple-element.35.refs_3_, f32[16,128,128]{2,1,0:T(8,128)} %get-tuple-element.36.f_hbm.refs_4_.refs_5_.refs_6_, ...), custom_call_target="tpu_custom_call" | custom-call | flops 100000000 | bytes 2097152 | tf_op jit(solution)/shard_map/pallas_call | solution.py:120
  57.7 5.2 %all-to-all-start.3 = ((f32[32,18,128]{2,1,0:T(8,128)}), f32[32,18,128]{2,1,0:T(8,128)S(1)}, u32[]{:S(2)}, u32[]{:S(2)}) async-start(f32[32,18,128]{2,1,0:T(8,128)} %get-tuple-element.41), calls=%async_computation.3 | async-start | bytes 786432 | tf_op jit(solution)/shard_map/all_to_all | solution.py:716
  63.0 4.8 %shard_map.112 = (f32[16,128,128]{2,1,0:T(8,128)}, f32[16,128,128]{2,1,0:T(8,128)}, f32[128,128]{1,0:T(8,128)}, f32[128,128]{1,0:T(8,128)}) custom-call(s32[1,2]{1,0:T(1,128)} %bitcast.4, f32[24,128]{1,0:T(8,128)} %get-tuple-element.42.refs_1_, f32[16,128,128]{2,1,0:T(8,128)} %get-tuple-element.39.refs_5_.refs_2_, ...), custom_call_target="tpu_custom_call" | custom-call | flops 200000000 | bytes 2097152 | tf_op jit(solution)/shard_map/pallas_call | solution.py:120
  67.8 1.5 %collective-permute-start.2 = (f32[128,128]{1,0:T(8,128)}, f32[128,128]{1,0:T(8,128)S(1)}, u32[]{:S(2)}, u32[]{:S(2)}) collective-permute-start(f32[128,128]{1,0:T(8,128)} %get-tuple-element.45), channel_id=1, source_target_pairs={{0,1},{2,3},{4,5},{6,7},{8,9},{10,11},{12,13},{14,15},{16,17},{18,... | collective-permute-start | bytes 196616 | tf_op jit(solution)/shard_map/ppermute | solution.py:701
  69.2 2.6 %collective-permute-start.3 = (f32[128,128]{1,0:T(8,128)}, f32[128,128]{1,0:T(8,128)S(1)}, u32[]{:S(2)}, u32[]{:S(2)}) collective-permute-start(f32[128,128]{1,0:T(8,128)} %get-tuple-element.46), channel_id=1, source_target_pairs={{1,2},{3,4},{5,6},{7,8},{9,10},{11,12},{13,14},{15,16},{17,18},{19... | collective-permute-start | bytes 196616 | tf_op jit(solution)/shard_map/ppermute | solution.py:702
  71.8 3.4 %all-to-all-done.3.refs_2_ = f32[32,18,128]{2,1,0:T(8,128)S(1)} async-done(((f32[32,18,128]{2,1,0:T(8,128)}), f32[32,18,128]{2,1,0:T(8,128)S(1)}, u32[]{:S(2)}, u32[]{:S(2)}) %all-to-all-start.3) | async-done | bytes 294944 | tf_op jit(solution)/shard_map/all_to_all | solution.py:716
  75.2 1.3 %shard_map.111 = f32[8,24,128]{2,1,0:T(8,128)} custom-call(bf16[144,512]{1,0:T(8,128)(2,1)S(1)} %get-tuple-element.32.refs_0_, bf16[144,512]{1,0:T(8,128)(2,1)S(1)} %get-tuple-element.33.refs_1_, f32[32,18,128]{2,1,0:T(8,128)S(1)} %all-to-all-done.3.refs_2_), custom_call_target="tpu_custom_call" | custom-call | flops 100000000 | bytes 2097152 | tf_op jit(solution)/shard_map/pallas_call | solution.py:120
  76.6 7.2 %all-to-all-start.4 = ((f32[8,24,128]{2,1,0:T(8,128)}), f32[8,24,128]{2,1,0:T(8,128)S(1)}, u32[]{:S(2)}, u32[]{:S(2)}) async-start(f32[8,24,128]{2,1,0:T(8,128)} %shard_map.111), calls=%async_computation.4 | async-start | bytes 196608 | tf_op jit(solution)/shard_map/all_to_all | solution.py:714
  84.4 4.9 %shard_map.113.refs_7_.refs_2_ = f32[16,128,128]{2,1,0:T(8,128)} custom-call(s32[6,16]{1,0:T(8,128)} %bitcast.6, f32[16,6,128,128]{3,2,1,0:T(8,128)} %s_hbm.3, f32[16,128,128]{2,1,0:T(8,128)} %get-tuple-element.44.f_hbm.refs_6_.refs_7_, f32[128,128]{1,0:T(8,128)} %copy-done.5, f32[128,128]{1,0:T(8,128)} %copy-done.6), custom_call_target="tpu_custom_call" | custom-call | flops 6000000000 | bytes 8388608 | tf_op jit(solution)/shard_map/pallas_call | solution.py:590
  89.4 0.6 copy-done.2
  90.0 4.1 %shard_map.114 = (f32[32,19,128]{2,1,0:T(8,128)}, f32[24,128]{1,0:T(8,128)}) custom-call(f32[8,24,128]{2,1,0:T(8,128)} %copy-done.2, f32[24,128]{1,0:T(8,128)} %get-tuple-element.42.refs_1_, f32[16,128]{1,0:T(8,128)} %refs_3_.5, f32[16,128,128]{2,1,0:T(8,128)} %refs_4_.5, f32[16,128,128]{2,1,0:T(8,128)} %get-tuple-element.43.refs_4_.refs_1_.refs_5_, ...), custom_call_target="tpu_custom_call" | custom-call | flops 100000000 | bytes 2097152 | tf_op jit(solution)/shard_map/pallas_call | solution.py:120
  94.1 5.3 %all-to-all-start.5 = ((f32[32,19,128]{2,1,0:T(8,128)}), f32[32,19,128]{2,1,0:T(8,128)S(1)}, u32[]{:S(2)}, u32[]{:S(2)}) async-start(f32[32,19,128]{2,1,0:T(8,128)} %get-tuple-element.47), calls=%async_computation.5 | async-start | bytes 786432 | tf_op jit(solution)/shard_map/all_to_all | solution.py:734
  99.4 4.4 %shard_map.115 = (f32[16,128,128]{2,1,0:T(8,128)}, f32[16,128,128]{2,1,0:T(8,128)}) custom-call(f32[24,128]{1,0:T(8,128)} %get-tuple-element.48.refs_0_.refs_2_, f32[16,128,128]{2,1,0:T(8,128)} %get-tuple-element.43.refs_4_.refs_1_.refs_5_, f32[16,128,128]{2,1,0:T(8,128)} %shard_map.113.refs_7_.refs_2_, ...), custom_call_target="tpu_custom_call" | custom-call | flops 200000000 | bytes 2097152 | tf_op jit(solution)/shard_map/pallas_call | solution.py:120
  103.8 7.8 %all-to-all-done.5.refs_2_ = f32[32,19,128]{2,1,0:T(8,128)S(1)} async-done(((f32[32,19,128]{2,1,0:T(8,128)}), f32[32,19,128]{2,1,0:T(8,128)S(1)}, u32[]{:S(2)}, u32[]{:S(2)}) %all-to-all-start.5) | async-done | bytes 311328 | tf_op jit(solution)/shard_map/all_to_all | solution.py:734
  111.6 0.8 shard_map.116
  112.5 12.2 %all_to_all.35.refs_0_ = f32[8,24,128]{2,1,0:T(8,128)} all-to-all(f32[8,24,128]{2,1,0:T(8,128)S(1)} %shard_map.116), channel_id=1, replica_groups=mesh['y'=4,'z'=8,'core'=2,'crs'=4] {'core','crs'}, dimensions={0} | all-to-all | bytes 196608 | tf_op jit(solution)/shard_map/all_to_all | solution.py:714
  124.7 4.6 %shard_map.117 = (f32[16,128,128]{2,1,0:T(8,128)}, f32[16,128,128]{2,1,0:T(8,128)}, f32[16,128,128]{2,1,0:T(8,128)}) custom-call(f32[8,24,128]{2,1,0:T(8,128)} %all_to_all.35.refs_0_, f32[24,128]{1,0:T(8,128)} %get-tuple-element.42.refs_1_, f32[24,128]{1,0:T(8,128)} %get-tuple-element.48.refs_0_.refs_2_, f32[16,128]{1,0:T(8,128)} %refs_3_.5, ...), custom_call_target="tpu_custom_call" | custom-call | flops 100000000 | bytes 2097152 | tf_op jit(solution)/shard_map/pallas_call | solution.py:120
  (18 shorter events, 1.9 us)
Async XLA Ops:
  2.1 11.5 %all-to-all-start = ((f32[8,24,128]{2,1,0:T(8,128)}), f32[8,24,128]{2,1,0:T(8,128)S(1)}, u32[]{:S(2)}, u32[]{:S(2)}) async-start(f32[8,24,128]{2,1,0:T(8,128)} %shard_map.103), calls=%async_computation | async-start | bytes 196608 | tf_op jit(solution)/shard_map/all_to_all | solution.py:631
  13.6 0.7 copy-start
  15.2 22.3 %all-to-all-start.1 = ((f32[32,18,128]{2,1,0:T(8,128)}), f32[32,18,128]{2,1,0:T(8,128)S(1)}, u32[]{:S(2)}, u32[]{:S(2)}) async-start(f32[32,18,128]{2,1,0:T(8,128)} %shard_map.106), calls=%async_computation.1 | async-start | bytes 786432 | tf_op jit(solution)/shard_map/all_to_all | solution.py:642
  29.2 6.2 %collective-permute-start = (f32[136,128]{1,0:T(8,128)}, f32[136,128]{1,0:T(8,128)S(1)}, u32[]{:S(2)}, u32[]{:S(2)}) collective-permute-start(f32[136,128]{1,0:T(8,128)} %get-tuple-element.30), channel_id=1, source_target_pairs={{0,1},{2,3},{4,5},{6,7},{8,9},{10,11},{12,13},{14,15},{16,17},{18,... | collective-permute-start | bytes 208904 | tf_op jit(solution)/shard_map/ppermute | solution.py:651
  29.9 17.5 %collective-permute-start.1 = (f32[136,128]{1,0:T(8,128)}, f32[136,128]{1,0:T(8,128)S(1)}, u32[]{:S(2)}, u32[]{:S(2)}) collective-permute-start(f32[136,128]{1,0:T(8,128)} %get-tuple-element.38), channel_id=1, source_target_pairs={{1,2},{3,4},{5,6},{7,8},{9,10},{11,12},{13,14},{15,16},{17,18},{19... | collective-permute-start | bytes 208904 | tf_op jit(solution)/shard_map/ppermute | solution.py:652
  35.4 12.0 %copy-start.3 = (f32[136,128]{1,0:T(8,128)}, f32[136,128]{1,0:T(8,128)S(1)}, u32[]{:S(2)}) copy-start(f32[136,128]{1,0:T(8,128)S(1)} %collective-permute-done.inner_hbm) | copy-start | bytes 208900
  40.7 13.5 %all-to-all-start.2 = ((f32[8,24,128]{2,1,0:T(8,128)}), f32[8,24,128]{2,1,0:T(8,128)S(1)}, u32[]{:S(2)}, u32[]{:S(2)}) async-start(f32[8,24,128]{2,1,0:T(8,128)} %get-tuple-element.34), calls=%async_computation.2 | async-start | bytes 196608 | tf_op jit(solution)/shard_map/all_to_all | solution.py:683
  47.4 0.6 copy-start.4
  54.2 0.6 copy-start.1
  57.7 17.5 %all-to-all-start.3 = ((f32[32,18,128]{2,1,0:T(8,128)}), f32[32,18,128]{2,1,0:T(8,128)S(1)}, u32[]{:S(2)}, u32[]{:S(2)}) async-start(f32[32,18,128]{2,1,0:T(8,128)} %get-tuple-element.41), calls=%async_computation.3 | async-start | bytes 786432 | tf_op jit(solution)/shard_map/all_to_all | solution.py:716
  67.8 16.0 %collective-permute-start.2 = (f32[128,128]{1,0:T(8,128)}, f32[128,128]{1,0:T(8,128)S(1)}, u32[]{:S(2)}, u32[]{:S(2)}) collective-permute-start(f32[128,128]{1,0:T(8,128)} %get-tuple-element.45), channel_id=1, source_target_pairs={{0,1},{2,3},{4,5},{6,7},{8,9},{10,11},{12,13},{14,15},{16,17},{18,... | collective-permute-start | bytes 196616 | tf_op jit(solution)/shard_map/ppermute | solution.py:701
  69.2 14.6 %collective-permute-start.3 = (f32[128,128]{1,0:T(8,128)}, f32[128,128]{1,0:T(8,128)S(1)}, u32[]{:S(2)}, u32[]{:S(2)}) collective-permute-start(f32[128,128]{1,0:T(8,128)} %get-tuple-element.46), channel_id=1, source_target_pairs={{1,2},{3,4},{5,6},{7,8},{9,10},{11,12},{13,14},{15,16},{17,18},{19... | collective-permute-start | bytes 196616 | tf_op jit(solution)/shard_map/ppermute | solution.py:702
  76.6 12.8 %all-to-all-start.4 = ((f32[8,24,128]{2,1,0:T(8,128)}), f32[8,24,128]{2,1,0:T(8,128)S(1)}, u32[]{:S(2)}, u32[]{:S(2)}) async-start(f32[8,24,128]{2,1,0:T(8,128)} %shard_map.111), calls=%async_computation.4 | async-start | bytes 196608 | tf_op jit(solution)/shard_map/all_to_all | solution.py:714
  83.8 0.6 copy-start.5
  83.8 0.6 copy-start.6
  89.4 0.6 copy-start.2
  94.1 17.5 %all-to-all-start.5 = ((f32[32,19,128]{2,1,0:T(8,128)}), f32[32,19,128]{2,1,0:T(8,128)S(1)}, u32[]{:S(2)}, u32[]{:S(2)}) async-start(f32[32,19,128]{2,1,0:T(8,128)} %get-tuple-element.47), calls=%async_computation.5 | async-start | bytes 786432 | tf_op jit(solution)/shard_map/all_to_all | solution.py:734

commit v6 on v5

--- a/solution.py
+++ b/solution.py
@@ -14,7 +14,7 @@
 KB = 6
 EXT = 18
 DOTS = EXT
-ROWS = 24
+ROWS = 22
 CROWS = 16
 RING = ("y", "z", "core", "crs")
 GATHER = ("y", "z")

time: 131 us -> 130 us (level)
  no operation moved by 1% of the time
where the time goes in v6:
time: 130 us; the launch traced here: 129 us
  Pallas kernels  49.1 us (38%)
  starting transfers between devices  47.6 us (37%)
  waiting for transfers between devices  16.1 us (12%)
  blocking collectives  12.2 us (9%)
  local copies, waits for them, and re-layouts  3.2 us (2%)
    pallas_call x13, Pallas kernels, staged(): pl.pallas_call(kernel, out_shape=[jax.ShapeDtypeStruct(sh, dt) for sh, dt...  38.1 us
    all_to_all x2, starting transfers between devices, on_device(): got = lax.all_to_all(msg, GATHER, 0, 0, tiled=True)  15.8 us
    all_to_all x1, blocking collectives, exchange(): return lax.all_to_all(part, SCATTER, 0, 0, tiled=True)  12.2 us
    pallas_call x2, Pallas kernels, apply_operator(): pl.pallas_call(functools.partial(operator_kernel, first), out_shape=outs,...  11.1 us
    all_to_all x2, waiting for transfers between devices, on_device(): got = lax.all_to_all(msg, GATHER, 0, 0, tiled=True)  9.86 us
    all_to_all x1, starting transfers between devices, exchange(): return lax.all_to_all(part, SCATTER, 0, 0, tiled=True)  7.22 us
    all_to_all x1, starting transfers between devices, on_device(): got = lax.all_to_all(part, SCATTER, 0, 0, tiled=True)  6.7 us
    all_to_all x1, starting transfers between devices, on_device(): targets = lax.all_to_all(target, SCATTER, 0, 0, tiled=True)  6.54 us
  transfers between devices with their start and end apart: 10, of which 4 were waited for; matrix products, arithmetic and copies ran while one was open for 0% of the time, Pallas kernels for 27%

profile of v6, /device:TPU:1, one launch (start us, length us, event | category | flops | bytes accessed | tf_op | source)
XLA Modules:
  0.0 129.3 jit_solution(5215597348216633370)
XLA Ops:
  0.6 1.4 %shard_map.103 = f32[8,24,128]{2,1,0:T(8,128)} custom-call(s32[1,2]{1,0:T(1,128)} %bitcast.2, s32[16]{0:T(128)} %refs_0_.1, f32[16,128]{1,0:T(8,128)} %refs_2_.4), custom_call_target="tpu_custom_call" | custom-call | bytes 262144 | tf_op jit(solution)/shard_map/pallas_call | solution.py:120
  2.1 6.5 %all-to-all-start = ((f32[8,24,128]{2,1,0:T(8,128)}), f32[8,24,128]{2,1,0:T(8,128)S(1)}, u32[]{:S(2)}, u32[]{:S(2)}) async-start(f32[8,24,128]{2,1,0:T(8,128)} %shard_map.103), calls=%async_computation | async-start | bytes 196608 | tf_op jit(solution)/shard_map/all_to_all | solution.py:631
  8.6 2.2 %shard_map.105.refs_0_.refs_2_ = f32[22,128]{1,0:T(8,128)} custom-call(s32[16]{0:T(128)} %refs_0_.1, f32[16,128]{1,0:T(8,128)} %refs_3_.5, f32[16,128,128]{2,1,0:T(8,128)} %refs_4_.5), custom_call_target="tpu_custom_call" | custom-call | flops 1000000 | bytes 2097152 | tf_op jit(solution)/shard_map/pallas_call | solution.py:120
  10.8 2.8 %all-to-all-done.refs_0_.refs_1_ = f32[8,24,128]{2,1,0:T(8,128)S(1)} async-done(((f32[8,24,128]{2,1,0:T(8,128)}), f32[8,24,128]{2,1,0:T(8,128)S(1)}, u32[]{:S(2)}, u32[]{:S(2)}) %all-to-all-start) | async-done | bytes 98336 | tf_op jit(solution)/shard_map/all_to_all | solution.py:631
  13.6 0.7 copy-done
  14.3 0.9 shard_map.106
  15.2 10.5 %all-to-all-start.1 = ((f32[32,18,128]{2,1,0:T(8,128)}), f32[32,18,128]{2,1,0:T(8,128)S(1)}, u32[]{:S(2)}, u32[]{:S(2)}) async-start(f32[32,18,128]{2,1,0:T(8,128)} %shard_map.106), calls=%async_computation.1 | async-start | bytes 786432 | tf_op jit(solution)/shard_map/all_to_all | solution.py:642
  25.7 3.5 %shard_map.107 = (f32[16,128,128]{2,1,0:T(8,128)}, f32[136,128]{1,0:T(8,128)}, f32[136,128]{1,0:T(8,128)}, f32[8,128]{1,0:T(8,128)}) custom-call(s32[1,2]{1,0:T(1,128)} %bitcast.3, f32[16,128]{1,0:T(8,128)} %refs_3_.5, f32[16,128,128]{2,1,0:T(8,128)} %refs_4_.5, f32[16,128,128]{2,1,0:T(8,128)} %refs_4_.4), custom_call_target="tpu_custom_call" | custom-call | flops 200000000 | bytes 2097152 | tf_op jit(solution)/shard_map/pallas_call | solution.py:120
  29.2 0.6 collective-permute-start
  29.9 1.5 %collective-permute-start.1 = (f32[136,128]{1,0:T(8,128)}, f32[136,128]{1,0:T(8,128)S(1)}, u32[]{:S(2)}, u32[]{:S(2)}) collective-permute-start(f32[136,128]{1,0:T(8,128)} %get-tuple-element.38), channel_id=1, source_target_pairs={{1,2},{3,4},{5,6},{7,8},{9,10},{11,12},{13,14},{15,16},{17,18},{19... | collective-permute-start | bytes 208904 | tf_op jit(solution)/shard_map/ppermute | solution.py:652
  31.3 4.0 %shard_map.104 = (bf16[288,2048]{1,0:T(8,128)(2,1)S(1)}, f32[16,128]{1,0:T(8,128)S(1)}) custom-call(f32[8,24,128]{2,1,0:T(8,128)S(1)} %all-to-all-done.refs_0_.refs_1_), custom_call_target="tpu_custom_call" | custom-call | flops 100000000 | bytes 2097152 | tf_op jit(solution)/shard_map/pallas_call | solution.py:120
  35.4 2.0 %all-to-all-done.1.refs_2_ = f32[32,18,128]{2,1,0:T(8,128)S(1)} async-done(((f32[32,18,128]{2,1,0:T(8,128)}), f32[32,18,128]{2,1,0:T(8,128)S(1)}, u32[]{:S(2)}, u32[]{:S(2)}) %all-to-all-start.1) | async-done | bytes 294944 | tf_op jit(solution)/shard_map/all_to_all | solution.py:642
  37.4 3.3 %shard_map.108 = (f32[8,22,128]{2,1,0:T(8,128)}, bf16[144,512]{1,0:T(8,128)(2,1)S(1)}, bf16[144,512]{1,0:T(8,128)(2,1)S(1)}) custom-call(bf16[288,2048]{1,0:T(8,128)(2,1)S(1)} %get-tuple-element.28.refs_0_, f32[16,128]{1,0:T(8,128)S(1)} %get-tuple-element.29.refs_1_, f32[32,18,128]{2,1,0:T(8,128)S(1)} %all-to-all-done.1.refs_2_), custom_call_target="tpu_custom_call" | custom-call | flops 1000000000 | bytes 2097152 | tf_op jit(solution)/shard_map/pallas_call | solution.py:120
  40.7 6.7 %all-to-all-start.2 = ((f32[8,22,128]{2,1,0:T(8,128)}), f32[8,22,128]{2,1,0:T(8,128)S(1)}, u32[]{:S(2)}, u32[]{:S(2)}) async-start(f32[8,22,128]{2,1,0:T(8,128)} %get-tuple-element.34), calls=%async_computation.2 | async-start | bytes 196608 | tf_op jit(solution)/shard_map/all_to_all | solution.py:683
  48.0 6.1 %shard_map.109 = (f32[16,128,128]{2,1,0:T(8,128)}, bf16[16,128,128]{2,1,0:T(8,128)(2,1)}) custom-call(s32[6,16]{1,0:T(8,128)} %bitcast.5, f32[16,6,128,128]{3,2,1,0:T(8,128)} %s_hbm.3, f32[16,128,128]{2,1,0:T(8,128)} %get-tuple-element.36.f_hbm.refs_4_.refs_5_.refs_6_, f32[136,128]{1,0:T(8,128)} %copy-done.3, f32[136,128]{1,0:T(8,128)} %copy-done.4, ...), custom_call_target="tpu_custom_call" | custom-call | flops 6000000000 | bytes 8388608 | tf_op jit(solution)/shard_map/pallas_call | solution.py:590
  54.8 2.9 %shard_map.110 = (f32[32,18,128]{2,1,0:T(8,128)}, f32[22,128]{1,0:T(8,128)}) custom-call(f32[8,22,128]{2,1,0:T(8,128)} %copy-done.1, f32[16,128]{1,0:T(8,128)} %refs_3_.5, f32[22,128]{1,0:T(8,128)} %shard_map.105.refs_0_.refs_2_, f32[8,128]{1,0:T(8,128)} %get-tuple-element.35.refs_3_, f32[16,128,128]{2,1,0:T(8,128)} %get-tuple-element.36.f_hbm.refs_4_.refs_5_.refs_6_, ...), custom_call_target="tpu_custom_call" | custom-call | flops 100000000 | bytes 2097152 | tf_op jit(solution)/shard_map/pallas_call | solution.py:120
  57.7 5.2 %all-to-all-start.3 = ((f32[32,18,128]{2,1,0:T(8,128)}), f32[32,18,128]{2,1,0:T(8,128)S(1)}, u32[]{:S(2)}, u32[]{:S(2)}) async-start(f32[32,18,128]{2,1,0:T(8,128)} %get-tuple-element.41), calls=%async_computation.3 | async-start | bytes 786432 | tf_op jit(solution)/shard_map/all_to_all | solution.py:716
  63.0 4.8 %shard_map.112 = (f32[16,128,128]{2,1,0:T(8,128)}, f32[16,128,128]{2,1,0:T(8,128)}, f32[128,128]{1,0:T(8,128)}, f32[128,128]{1,0:T(8,128)}) custom-call(s32[1,2]{1,0:T(1,128)} %bitcast.4, f32[22,128]{1,0:T(8,128)} %get-tuple-element.42.refs_1_, f32[16,128,128]{2,1,0:T(8,128)} %get-tuple-element.39.refs_5_.refs_2_, ...), custom_call_target="tpu_custom_call" | custom-call | flops 200000000 | bytes 2097152 | tf_op jit(solution)/shard_map/pallas_call | solution.py:120
  67.8 1.4 %collective-permute-start.2 = (f32[128,128]{1,0:T(8,128)}, f32[128,128]{1,0:T(8,128)S(1)}, u32[]{:S(2)}, u32[]{:S(2)}) collective-permute-start(f32[128,128]{1,0:T(8,128)} %get-tuple-element.45), channel_id=1, source_target_pairs={{0,1},{2,3},{4,5},{6,7},{8,9},{10,11},{12,13},{14,15},{16,17},{18,... | collective-permute-start | bytes 196616 | tf_op jit(solution)/shard_map/ppermute | solution.py:701
  69.2 2.6 %collective-permute-start.3 = (f32[128,128]{1,0:T(8,128)}, f32[128,128]{1,0:T(8,128)S(1)}, u32[]{:S(2)}, u32[]{:S(2)}) collective-permute-start(f32[128,128]{1,0:T(8,128)} %get-tuple-element.46), channel_id=1, source_target_pairs={{1,2},{3,4},{5,6},{7,8},{9,10},{11,12},{13,14},{15,16},{17,18},{19... | collective-permute-start | bytes 196616 | tf_op jit(solution)/shard_map/ppermute | solution.py:702
  71.8 3.4 %all-to-all-done.3.refs_2_ = f32[32,18,128]{2,1,0:T(8,128)S(1)} async-done(((f32[32,18,128]{2,1,0:T(8,128)}), f32[32,18,128]{2,1,0:T(8,128)S(1)}, u32[]{:S(2)}, u32[]{:S(2)}) %all-to-all-start.3) | async-done | bytes 294944 | tf_op jit(solution)/shard_map/all_to_all | solution.py:716
  75.2 1.3 %shard_map.111 = f32[8,22,128]{2,1,0:T(8,128)} custom-call(bf16[144,512]{1,0:T(8,128)(2,1)S(1)} %get-tuple-element.32.refs_0_, bf16[144,512]{1,0:T(8,128)(2,1)S(1)} %get-tuple-element.33.refs_1_, f32[32,18,128]{2,1,0:T(8,128)S(1)} %all-to-all-done.3.refs_2_), custom_call_target="tpu_custom_call" | custom-call | flops 100000000 | bytes 2097152 | tf_op jit(solution)/shard_map/pallas_call | solution.py:120
  76.6 7.2 %all-to-all-start.4 = ((f32[8,22,128]{2,1,0:T(8,128)}), f32[8,22,128]{2,1,0:T(8,128)S(1)}, u32[]{:S(2)}, u32[]{:S(2)}) async-start(f32[8,22,128]{2,1,0:T(8,128)} %shard_map.111), calls=%async_computation.4 | async-start | bytes 196608 | tf_op jit(solution)/shard_map/all_to_all | solution.py:714
  84.4 4.9 %shard_map.113.refs_7_.refs_2_ = f32[16,128,128]{2,1,0:T(8,128)} custom-call(s32[6,16]{1,0:T(8,128)} %bitcast.6, f32[16,6,128,128]{3,2,1,0:T(8,128)} %s_hbm.3, f32[16,128,128]{2,1,0:T(8,128)} %get-tuple-element.44.f_hbm.refs_6_.refs_7_, f32[128,128]{1,0:T(8,128)} %copy-done.5, f32[128,128]{1,0:T(8,128)} %copy-done.6), custom_call_target="tpu_custom_call" | custom-call | flops 6000000000 | bytes 8388608 | tf_op jit(solution)/shard_map/pallas_call | solution.py:590
  89.4 0.6 copy-done.2
  90.0 4.1 %shard_map.114 = (f32[32,19,128]{2,1,0:T(8,128)}, f32[22,128]{1,0:T(8,128)}) custom-call(f32[8,22,128]{2,1,0:T(8,128)} %copy-done.2, f32[22,128]{1,0:T(8,128)} %get-tuple-element.42.refs_1_, f32[16,128]{1,0:T(8,128)} %refs_3_.5, f32[16,128,128]{2,1,0:T(8,128)} %refs_4_.5, f32[16,128,128]{2,1,0:T(8,128)} %get-tuple-element.43.refs_4_.refs_1_.refs_5_, ...), custom_call_target="tpu_custom_call" | custom-call | flops 100000000 | bytes 2097152 | tf_op jit(solution)/shard_map/pallas_call | solution.py:120
  94.1 5.3 %all-to-all-start.5 = ((f32[32,19,128]{2,1,0:T(8,128)}), f32[32,19,128]{2,1,0:T(8,128)S(1)}, u32[]{:S(2)}, u32[]{:S(2)}) async-start(f32[32,19,128]{2,1,0:T(8,128)} %get-tuple-element.47), calls=%async_computation.5 | async-start | bytes 786432 | tf_op jit(solution)/shard_map/all_to_all | solution.py:734
  99.4 4.4 %shard_map.115 = (f32[16,128,128]{2,1,0:T(8,128)}, f32[16,128,128]{2,1,0:T(8,128)}) custom-call(f32[22,128]{1,0:T(8,128)} %get-tuple-element.48.refs_0_.refs_2_, f32[16,128,128]{2,1,0:T(8,128)} %get-tuple-element.43.refs_4_.refs_1_.refs_5_, f32[16,128,128]{2,1,0:T(8,128)} %shard_map.113.refs_7_.refs_2_, ...), custom_call_target="tpu_custom_call" | custom-call | flops 200000000 | bytes 2097152 | tf_op jit(solution)/shard_map/pallas_call | solution.py:120
  103.8 7.8 %all-to-all-done.5.refs_2_ = f32[32,19,128]{2,1,0:T(8,128)S(1)} async-done(((f32[32,19,128]{2,1,0:T(8,128)}), f32[32,19,128]{2,1,0:T(8,128)S(1)}, u32[]{:S(2)}, u32[]{:S(2)}) %all-to-all-start.5) | async-done | bytes 311328 | tf_op jit(solution)/shard_map/all_to_all | solution.py:734
  111.6 0.7 shard_map.116
  112.3 12.2 %all_to_all.35.refs_0_ = f32[8,22,128]{2,1,0:T(8,128)} all-to-all(f32[8,22,128]{2,1,0:T(8,128)S(1)} %shard_map.116), channel_id=1, replica_groups=mesh['y'=4,'z'=8,'core'=2,'crs'=4] {'core','crs'}, dimensions={0} | all-to-all | bytes 180224 | tf_op jit(solution)/shard_map/all_to_all | solution.py:714
  124.6 4.6 %shard_map.117 = (f32[16,128,128]{2,1,0:T(8,128)}, f32[16,128,128]{2,1,0:T(8,128)}, f32[16,128,128]{2,1,0:T(8,128)}) custom-call(f32[8,22,128]{2,1,0:T(8,128)} %all_to_all.35.refs_0_, f32[22,128]{1,0:T(8,128)} %get-tuple-element.42.refs_1_, f32[22,128]{1,0:T(8,128)} %get-tuple-element.48.refs_0_.refs_2_, f32[16,128]{1,0:T(8,128)} %refs_3_.5, ...), custom_call_target="tpu_custom_call" | custom-call | flops 100000000 | bytes 2097152 | tf_op jit(solution)/shard_map/pallas_call | solution.py:120
  (18 shorter events, 1.9 us)
Async XLA Ops:
  2.1 11.5 %all-to-all-start = ((f32[8,24,128]{2,1,0:T(8,128)}), f32[8,24,128]{2,1,0:T(8,128)S(1)}, u32[]{:S(2)}, u32[]{:S(2)}) async-start(f32[8,24,128]{2,1,0:T(8,128)} %shard_map.103), calls=%async_computation | async-start | bytes 196608 | tf_op jit(solution)/shard_map/all_to_all | solution.py:631
  13.6 0.7 copy-start
  15.2 22.3 %all-to-all-start.1 = ((f32[32,18,128]{2,1,0:T(8,128)}), f32[32,18,128]{2,1,0:T(8,128)S(1)}, u32[]{:S(2)}, u32[]{:S(2)}) async-start(f32[32,18,128]{2,1,0:T(8,128)} %shard_map.106), calls=%async_computation.1 | async-start | bytes 786432 | tf_op jit(solution)/shard_map/all_to_all | solution.py:642
  29.2 6.2 %collective-permute-start = (f32[136,128]{1,0:T(8,128)}, f32[136,128]{1,0:T(8,128)S(1)}, u32[]{:S(2)}, u32[]{:S(2)}) collective-permute-start(f32[136,128]{1,0:T(8,128)} %get-tuple-element.30), channel_id=1, source_target_pairs={{0,1},{2,3},{4,5},{6,7},{8,9},{10,11},{12,13},{14,15},{16,17},{18,... | collective-permute-start | bytes 208904 | tf_op jit(solution)/shard_map/ppermute | solution.py:651
  29.9 17.5 %collective-permute-start.1 = (f32[136,128]{1,0:T(8,128)}, f32[136,128]{1,0:T(8,128)S(1)}, u32[]{:S(2)}, u32[]{:S(2)}) collective-permute-start(f32[136,128]{1,0:T(8,128)} %get-tuple-element.38), channel_id=1, source_target_pairs={{1,2},{3,4},{5,6},{7,8},{9,10},{11,12},{13,14},{15,16},{17,18},{19... | collective-permute-start | bytes 208904 | tf_op jit(solution)/shard_map/ppermute | solution.py:652
  35.4 12.0 %copy-start.3 = (f32[136,128]{1,0:T(8,128)}, f32[136,128]{1,0:T(8,128)S(1)}, u32[]{:S(2)}) copy-start(f32[136,128]{1,0:T(8,128)S(1)} %collective-permute-done.inner_hbm) | copy-start | bytes 208900
  40.7 13.5 %all-to-all-start.2 = ((f32[8,22,128]{2,1,0:T(8,128)}), f32[8,22,128]{2,1,0:T(8,128)S(1)}, u32[]{:S(2)}, u32[]{:S(2)}) async-start(f32[8,22,128]{2,1,0:T(8,128)} %get-tuple-element.34), calls=%async_computation.2 | async-start | bytes 196608 | tf_op jit(solution)/shard_map/all_to_all | solution.py:683
  47.4 0.6 copy-start.4
  54.2 0.6 copy-start.1
  57.7 17.5 %all-to-all-start.3 = ((f32[32,18,128]{2,1,0:T(8,128)}), f32[32,18,128]{2,1,0:T(8,128)S(1)}, u32[]{:S(2)}, u32[]{:S(2)}) async-start(f32[32,18,128]{2,1,0:T(8,128)} %get-tuple-element.41), calls=%async_computation.3 | async-start | bytes 786432 | tf_op jit(solution)/shard_map/all_to_all | solution.py:716
  67.8 16.0 %collective-permute-start.2 = (f32[128,128]{1,0:T(8,128)}, f32[128,128]{1,0:T(8,128)S(1)}, u32[]{:S(2)}, u32[]{:S(2)}) collective-permute-start(f32[128,128]{1,0:T(8,128)} %get-tuple-element.45), channel_id=1, source_target_pairs={{0,1},{2,3},{4,5},{6,7},{8,9},{10,11},{12,13},{14,15},{16,17},{18,... | collective-permute-start | bytes 196616 | tf_op jit(solution)/shard_map/ppermute | solution.py:701
  69.2 14.6 %collective-permute-start.3 = (f32[128,128]{1,0:T(8,128)}, f32[128,128]{1,0:T(8,128)S(1)}, u32[]{:S(2)}, u32[]{:S(2)}) collective-permute-start(f32[128,128]{1,0:T(8,128)} %get-tuple-element.46), channel_id=1, source_target_pairs={{1,2},{3,4},{5,6},{7,8},{9,10},{11,12},{13,14},{15,16},{17,18},{19... | collective-permute-start | bytes 196616 | tf_op jit(solution)/shard_map/ppermute | solution.py:702
  76.6 12.8 %all-to-all-start.4 = ((f32[8,22,128]{2,1,0:T(8,128)}), f32[8,22,128]{2,1,0:T(8,128)S(1)}, u32[]{:S(2)}, u32[]{:S(2)}) async-start(f32[8,22,128]{2,1,0:T(8,128)} %shard_map.111), calls=%async_computation.4 | async-start | bytes 196608 | tf_op jit(solution)/shard_map/all_to_all | solution.py:714
  83.8 0.6 copy-start.5
  83.8 0.6 copy-start.6
  89.4 0.6 copy-start.2
  94.1 17.5 %all-to-all-start.5 = ((f32[32,19,128]{2,1,0:T(8,128)}), f32[32,19,128]{2,1,0:T(8,128)S(1)}, u32[]{:S(2)}, u32[]{:S(2)}) async-start(f32[32,19,128]{2,1,0:T(8,128)} %get-tuple-element.47), calls=%async_computation.5 | async-start | bytes 786432 | tf_op jit(solution)/shard_map/all_to_all | solution.py:734
